TPU v7x, 128 devices: a whole 4x4x4 slice. The times are simulated.
128 devices in a mesh: dp: 64 (over y_hi, x, z, core), fsdp: 2 (over y_lo).
Axes of the slice: x: 4, y: 4 (y_hi: 2, y_lo: 2; y = y_hi * 2 + y_lo), z: 4, core: 2. Of those that a mesh axis runs over, the one named last changes fastest.
Arguments:
- tokens: bfloat16 [128, 192, 1024], P(('dp', 'fsdp')), may hold values from -6 to 6
- memory: float32 [128, 192, 1024], P(('dp', 'fsdp')), may hold values from -6 to 6
- compressed: float32 [128, 192, 1024], P(('dp', 'fsdp')), may hold values from -6 to 6
- cotangent: bfloat16 [128, 192, 1024], P(('dp', 'fsdp')), may hold values from -6 to 6
- ln1_g: bfloat16 [1024], P('fsdp'), may hold values from 0.5 to 1.5
- ln1_b: bfloat16 [1024], P('fsdp'), may hold values from -1.75 to 1.75
- w_q: bfloat16 [1024, 1024], P('fsdp'), may hold values from -0.1875 to 0.1875
- w_kv: bfloat16 [1024, 2048], P('fsdp'), may hold values from -0.1875 to 0.1875
- w_r: bfloat16 [1024, 1024], P('fsdp'), may hold values from -0.1875 to 0.1875
- bias_u: bfloat16 [1024], P('fsdp'), may hold values from -3 to 3
- bias_v: bfloat16 [1024], P('fsdp'), may hold values from -3 to 3
- w_o: bfloat16 [1024, 1024], P('fsdp'), may hold values from -0.75 to 0.75
- ln2_g: bfloat16 [1024], P('fsdp'), may hold values from 0.5 to 1.5
- ln2_b: bfloat16 [1024], P('fsdp'), may hold values from -1.75 to 1.75
- w_in: bfloat16 [1024, 4096], P('fsdp'), may hold values from -0.1875 to 0.1875
- b_in: bfloat16 [4096], P('fsdp'), may hold values from -1.75 to 1.75
- w_out: bfloat16 [4096, 1024], P('fsdp'), may hold values from -0.09375 to 0.09375
- b_out: bfloat16 [1024], P('fsdp'), may hold values from -1.75 to 1.75
- conv_w: bfloat16 [3072, 1024], P('fsdp'), may hold values from -0.109375 to 0.109375
- conv_b: bfloat16 [1024], P('fsdp'), may hold values from -1.75 to 1.75
Outputs:
- mixed_out: bfloat16 [128, 192, 1024], P(('dp', 'fsdp'))
- compressed_next: float32 [128, 192, 1024], P(('dp', 'fsdp'))
- recon_loss: float32 [128], P(('dp', 'fsdp'))
- grad_tokens: float32 [128, 192, 1024], P(('dp', 'fsdp'))
- grad_ln1_g: float32 [1024], P('fsdp')
- grad_ln1_b: float32 [1024], P('fsdp')
- grad_w_q: float32 [1024, 1024], P('fsdp')
- grad_w_kv: float32 [1024, 2048], P('fsdp')
- grad_w_r: float32 [1024, 1024], P('fsdp')
- grad_bias_u: float32 [1024], P('fsdp')
- grad_bias_v: float32 [1024], P('fsdp')
- grad_w_o: float32 [1024, 1024], P('fsdp')
- grad_ln2_g: float32 [1024], P('fsdp')
- grad_ln2_b: float32 [1024], P('fsdp')
- grad_w_in: float32 [1024, 4096], P('fsdp')
- grad_b_in: float32 [4096], P('fsdp')
- grad_w_out: float32 [4096, 1024], P('fsdp')
- grad_b_out: float32 [1024], P('fsdp')
- grad_conv_w: float32 [3072, 1024], P('fsdp')
- grad_conv_b: float32 [1024], P('fsdp')
All inputs are finite; a program needn't handle non-finite values.
Results may differ from a plain program's by a relative error of at most 0.015.
Values may be sent and summed in bfloat16 or wider, within the bound.
No kernel may reach another device: no remote copies, remote signals or barrier semaphores. Data moves between devices by JAX's collectives and lax.ppermute only.
A program may use at most 384 MiB of HBM per device.

v0:
```python
import jax
import jax.numpy as jnp
from jax import lax
from jax.sharding import PartitionSpec as P

H = 8


def layer_norm(values, scaling, offset):
    center = values - jnp.mean(values, axis=-1, keepdims=True)
    spread = jnp.mean(center * center, axis=-1, keepdims=True)
    return center * lax.rsqrt(spread + 1e-05) * scaling + offset


def sinusoid(key_count, model_dim):
    distance = (key_count - 1 - jnp.arange(key_count)).astype(jnp.float32)
    inverse = 1.0 / 10000.0 ** (jnp.arange(0, model_dim, 2).astype(jnp.float32) / model_dim)
    angles = distance[:, None] * inverse[None, :]
    return jnp.concatenate([jnp.sin(angles), jnp.cos(angles)], axis=-1)


def rel_shift(scores):
    padded = jnp.pad(scores, ((0, 0), (0, 0), (1, 0)))
    padded = padded.reshape(scores.shape[0], scores.shape[2] + 1, scores.shape[1])
    return padded[:, 1:, :].reshape(scores.shape)


def softmax_rows(scores):
    largest = jnp.max(scores, axis=-1, keepdims=True)
    exponent = jnp.exp(scores - largest)
    return exponent / jnp.sum(exponent, axis=-1, keepdims=True)


def split_heads(rows):
    model_dim = rows.shape[1] // 2
    head_size = model_dim // H
    keys_h = rows[:, :model_dim].reshape(rows.shape[0], H, head_size)
    values_h = rows[:, model_dim:].reshape(rows.shape[0], H, head_size)
    return (keys_h, values_h)


def content_attend(asking, rows):
    keys_h, values_h = split_heads(rows)
    scores = jnp.einsum("ihd,jhd->hij", asking, keys_h, preferred_element_type=jnp.float32)
    attn_probs = softmax_rows(scores)
    mixture = jnp.einsum(
        "hij,jhd->ihd",
        attn_probs.astype(jnp.bfloat16),
        values_h,
        preferred_element_type=jnp.float32,
    )
    return (mixture.reshape(asking.shape[0], rows.shape[1] // 2), attn_probs)


def stream_state(weights, tokens, memory, compressed):
    (
        ln1_g,
        ln1_b,
        w_q,
        w_kv,
        w_r,
        bias_u,
        bias_v,
        w_o,
        ln2_g,
        ln2_b,
        w_in,
        b_in,
        w_out,
        b_out,
        conv_w,
        conv_b,
    ) = weights
    seg_len = tokens.shape[0]
    model_dim = w_q.shape[0]
    head_size = model_dim // H
    key_count = compressed.shape[0] + memory.shape[0] + seg_len
    first_query = key_count - seg_len
    factor = head_size ** (-0.5)
    joined = jnp.concatenate([compressed, memory, tokens.astype(jnp.float32)], axis=0)
    normed = layer_norm(joined, ln1_g.astype(jnp.float32), ln1_b.astype(jnp.float32)).astype(
        jnp.bfloat16
    )
    queries = jnp.dot(normed[first_query:], w_q, preferred_element_type=jnp.float32)
    key_value = jnp.dot(normed, w_kv, preferred_element_type=jnp.float32).astype(jnp.bfloat16)
    sinus_table = sinusoid(key_count, model_dim).astype(jnp.bfloat16)
    relative = jnp.dot(sinus_table, w_r, preferred_element_type=jnp.float32).astype(jnp.bfloat16)
    content = (
        ((queries + bias_u.astype(jnp.float32)) * factor)
        .astype(jnp.bfloat16)
        .reshape(seg_len, H, head_size)
    )
    located = (
        ((queries + bias_v.astype(jnp.float32)) * factor)
        .astype(jnp.bfloat16)
        .reshape(seg_len, H, head_size)
    )
    keys_h, values_h = split_heads(key_value)
    relative_h = relative.reshape(key_count, H, head_size)
    raw_scores = jnp.einsum("ihd,jhd->hij", located, relative_h, preferred_element_type=jnp.float32)
    scores = jnp.einsum(
        "ihd,jhd->hij", content, keys_h, preferred_element_type=jnp.float32
    ) + rel_shift(raw_scores)
    row_ids = jnp.arange(seg_len)[:, None]
    col_ids = jnp.arange(key_count)[None, :]
    allowed = col_ids <= row_ids + first_query
    attn_probs = softmax_rows(jnp.where(allowed[None], scores, -1e30))
    probs_low = attn_probs.astype(jnp.bfloat16)
    mixture = jnp.einsum("hij,jhd->ihd", probs_low, values_h, preferred_element_type=jnp.float32)
    attended = mixture.reshape(seg_len, model_dim).astype(jnp.bfloat16)
    residual = tokens.astype(jnp.float32) + jnp.dot(
        attended, w_o, preferred_element_type=jnp.float32
    )
    normed2 = layer_norm(residual, ln2_g.astype(jnp.float32), ln2_b.astype(jnp.float32)).astype(
        jnp.bfloat16
    )
    pre_act = jnp.dot(normed2, w_in, preferred_element_type=jnp.float32) + b_in.astype(jnp.float32)
    hidden = jax.nn.gelu(pre_act).astype(jnp.bfloat16)
    result = (
        residual
        + jnp.dot(hidden, w_out, preferred_element_type=jnp.float32)
        + b_out.astype(jnp.float32)
    )
    oldest = memory.reshape(seg_len // 3, 3 * model_dim).astype(jnp.bfloat16)
    compact = jnp.dot(oldest, conv_w, preferred_element_type=jnp.float32) + conv_b.astype(
        jnp.float32
    )
    comp_normed = layer_norm(compact, ln1_g.astype(jnp.float32), ln1_b.astype(jnp.float32)).astype(
        jnp.bfloat16
    )
    comp_pair = jnp.dot(comp_normed, w_kv, preferred_element_type=jnp.float32).astype(jnp.bfloat16)
    asking = (queries * factor).astype(jnp.bfloat16).reshape(seg_len, H, head_size)
    start_old = compressed.shape[0]
    target = content_attend(asking, key_value[start_old : start_old + seg_len])[0]
    guess, guess_probs = content_attend(asking, comp_pair)
    mismatch = target - guess
    recon_loss = jnp.mean(mismatch * mismatch)
    return {
        "joined": joined,
        "normed": normed,
        "key_value": key_value,
        "sinus_table": sinus_table,
        "relative": relative,
        "content": content,
        "located": located,
        "raw_scores": raw_scores,
        "attn_probs": attn_probs,
        "probs_low": probs_low,
        "attended": attended,
        "residual": residual,
        "normed2": normed2,
        "pre_act": pre_act,
        "hidden": hidden,
        "result": result,
        "oldest": oldest,
        "compact": compact,
        "comp_pair": comp_pair,
        "asking": asking,
        "guess_probs": guess_probs,
        "mismatch": mismatch,
        "recon_loss": recon_loss,
    }


def stream_grads(weights, tokens, memory, compressed, cotangent):
    (
        ln1_g,
        ln1_b,
        w_q,
        w_kv,
        w_r,
        bias_u,
        bias_v,
        w_o,
        ln2_g,
        ln2_b,
        w_in,
        b_in,
        w_out,
        b_out,
        conv_w,
        conv_b,
    ) = weights
    state = stream_state(weights, tokens, memory, compressed)
    seg_len = tokens.shape[0]
    model_dim = w_q.shape[0]
    head_size = model_dim // H
    key_count = state["joined"].shape[0]
    first_query = key_count - seg_len
    factor = head_size ** (-0.5)
    gain_one = ln1_g.astype(jnp.float32)
    bias_one = ln1_b.astype(jnp.float32)
    cot_wide = cotangent.astype(jnp.float32)
    d_b_out = jnp.sum(cot_wide, axis=0)
    d_w_out = jnp.einsum(
        "tf,td->fd", state["hidden"], cotangent, preferred_element_type=jnp.float32
    )
    d_hidden = jnp.einsum("td,fd->tf", cotangent, w_out, preferred_element_type=jnp.float32)
    unused_slot, gelu_back = jax.vjp(jax.nn.gelu, state["pre_act"])
    d_pre = gelu_back(d_hidden)[0].astype(jnp.bfloat16)
    d_b_in = jnp.sum(d_pre.astype(jnp.float32), axis=0)
    d_w_in = jnp.einsum("td,tf->df", state["normed2"], d_pre, preferred_element_type=jnp.float32)
    d_normed2 = jnp.einsum("tf,df->td", d_pre, w_in, preferred_element_type=jnp.float32)
    unused_slot, norm_back2 = jax.vjp(
        layer_norm, state["residual"], ln2_g.astype(jnp.float32), ln2_b.astype(jnp.float32)
    )
    d_mid_norm, d_ln2_g, d_ln2_b = norm_back2(d_normed2)
    d_residual = cot_wide + d_mid_norm
    d_branch = d_residual.astype(jnp.bfloat16)
    d_w_o = jnp.einsum("ti,td->id", state["attended"], d_branch, preferred_element_type=jnp.float32)
    d_attended = jnp.einsum("td,id->ti", d_branch, w_o, preferred_element_type=jnp.float32)
    d_attended = d_attended.astype(jnp.bfloat16).reshape(seg_len, H, head_size)
    keys_h, values_h = split_heads(state["key_value"])
    attn_probs = state["attn_probs"]
    d_probs = jnp.einsum("ihd,jhd->hij", d_attended, values_h, preferred_element_type=jnp.float32)
    d_values = jnp.einsum(
        "hij,ihd->jhd", state["probs_low"], d_attended, preferred_element_type=jnp.float32
    )
    d_scores = (
        attn_probs * (d_probs - jnp.sum(attn_probs * d_probs, axis=-1, keepdims=True))
    ).astype(jnp.bfloat16)
    d_content = jnp.einsum("hij,jhd->ihd", d_scores, keys_h, preferred_element_type=jnp.float32)
    d_keys = jnp.einsum(
        "hij,ihd->jhd", d_scores, state["content"], preferred_element_type=jnp.float32
    )
    unused_slot, shift_back = jax.vjp(rel_shift, state["raw_scores"])
    d_raw = shift_back(d_scores.astype(jnp.float32))[0].astype(jnp.bfloat16)
    relative_h = state["relative"].reshape(key_count, H, head_size)
    d_located = jnp.einsum("hij,jhd->ihd", d_raw, relative_h, preferred_element_type=jnp.float32)
    d_relative = jnp.einsum(
        "hij,ihd->jhd", d_raw, state["located"], preferred_element_type=jnp.float32
    )
    d_relative = d_relative.reshape(key_count, model_dim).astype(jnp.bfloat16)
    d_w_r = jnp.einsum(
        "kc,kd->cd", state["sinus_table"], d_relative, preferred_element_type=jnp.float32
    )
    d_content = d_content.reshape(seg_len, model_dim) * factor
    d_located = d_located.reshape(seg_len, model_dim) * factor
    d_bias_u = jnp.sum(d_content, axis=0)
    d_bias_v = jnp.sum(d_located, axis=0)
    d_queries = (d_content + d_located).astype(jnp.bfloat16)
    normed = state["normed"]
    d_w_q = jnp.einsum(
        "ti,td->id", normed[first_query:], d_queries, preferred_element_type=jnp.float32
    )
    d_pair = jnp.concatenate(
        [d_keys.reshape(key_count, model_dim), d_values.reshape(key_count, model_dim)], axis=1
    ).astype(jnp.bfloat16)
    d_w_kv = jnp.einsum("ki,kd->id", normed, d_pair, preferred_element_type=jnp.float32)
    d_normed = jnp.einsum("kd,id->ki", d_pair, w_kv, preferred_element_type=jnp.float32)
    d_normed_q = jnp.einsum("td,id->ti", d_queries, w_q, preferred_element_type=jnp.float32)
    d_normed = jnp.concatenate(
        [d_normed[:first_query], d_normed[first_query:] + d_normed_q], axis=0
    )
    unused_slot, norm_back1 = jax.vjp(layer_norm, state["joined"], gain_one, bias_one)
    d_joined, d_ln1_g, d_ln1_b = norm_back1(d_normed)
    d_tokens = d_residual + d_joined[first_query:]
    compact_len = seg_len // 3
    d_guess = (
        (-2.0 / (seg_len * model_dim) * state["mismatch"])
        .astype(jnp.bfloat16)
        .reshape(seg_len, H, head_size)
    )
    comp_keys, comp_values = split_heads(state["comp_pair"])
    guess_probs = state["guess_probs"]
    d_gprobs = jnp.einsum("ihd,jhd->hij", d_guess, comp_values, preferred_element_type=jnp.float32)
    d_comp_values = jnp.einsum(
        "hij,ihd->jhd",
        guess_probs.astype(jnp.bfloat16),
        d_guess,
        preferred_element_type=jnp.float32,
    )
    d_gscores = (
        guess_probs * (d_gprobs - jnp.sum(guess_probs * d_gprobs, axis=-1, keepdims=True))
    ).astype(jnp.bfloat16)
    d_comp_keys = jnp.einsum(
        "hij,ihd->jhd", d_gscores, state["asking"], preferred_element_type=jnp.float32
    )
    d_comp_pair = jnp.concatenate(
        [
            d_comp_keys.reshape(compact_len, model_dim),
            d_comp_values.reshape(compact_len, model_dim),
        ],
        axis=1,
    ).astype(jnp.bfloat16)
    d_comp_normed = jnp.einsum("kd,id->ki", d_comp_pair, w_kv, preferred_element_type=jnp.float32)
    unused_slot, norm_back3 = jax.vjp(
        lambda values: layer_norm(values, gain_one, bias_one), state["compact"]
    )
    d_compact = norm_back3(d_comp_normed)[0].astype(jnp.bfloat16)
    d_conv_w = jnp.einsum(
        "ki,kd->id", state["oldest"], d_compact, preferred_element_type=jnp.float32
    )
    d_conv_b = jnp.sum(d_compact.astype(jnp.float32), axis=0)
    return (
        d_tokens,
        (
            d_ln1_g,
            d_ln1_b,
            d_w_q,
            d_w_kv,
            d_w_r,
            d_bias_u,
            d_bias_v,
            d_w_o,
            d_ln2_g,
            d_ln2_b,
            d_w_in,
            d_b_in,
            d_w_out,
            d_b_out,
            d_conv_w,
            d_conv_b,
        ),
    )


def per_device(
    tokens,
    memory,
    compressed,
    cotangent,
    ln1_g,
    ln1_b,
    w_q,
    w_kv,
    w_r,
    bias_u,
    bias_v,
    w_o,
    ln2_g,
    ln2_b,
    w_in,
    b_in,
    w_out,
    b_out,
    conv_w,
    conv_b,
):
    gathered = (
        lax.all_gather(ln1_g, "fsdp", axis=0, tiled=True),
        lax.all_gather(ln1_b, "fsdp", axis=0, tiled=True),
        lax.all_gather(w_q, "fsdp", axis=0, tiled=True),
        lax.all_gather(w_kv, "fsdp", axis=0, tiled=True),
        lax.all_gather(w_r, "fsdp", axis=0, tiled=True),
        lax.all_gather(bias_u, "fsdp", axis=0, tiled=True),
        lax.all_gather(bias_v, "fsdp", axis=0, tiled=True),
        lax.all_gather(w_o, "fsdp", axis=0, tiled=True),
        lax.all_gather(ln2_g, "fsdp", axis=0, tiled=True),
        lax.all_gather(ln2_b, "fsdp", axis=0, tiled=True),
        lax.all_gather(w_in, "fsdp", axis=0, tiled=True),
        lax.all_gather(b_in, "fsdp", axis=0, tiled=True),
        lax.all_gather(w_out, "fsdp", axis=0, tiled=True),
        lax.all_gather(b_out, "fsdp", axis=0, tiled=True),
        lax.all_gather(conv_w, "fsdp", axis=0, tiled=True),
        lax.all_gather(conv_b, "fsdp", axis=0, tiled=True),
    )
    states = jax.vmap(stream_state, in_axes=(None, 0, 0, 0))(gathered, tokens, memory, compressed)
    mixed_out = states["result"].astype(jnp.bfloat16)
    compact_len = tokens.shape[1] // 3
    compressed_next = jnp.concatenate([compressed[:, compact_len:], states["compact"]], axis=1)
    recon_loss = states["recon_loss"]
    regathered = (
        lax.all_gather(ln1_g, "fsdp", axis=0, tiled=True),
        lax.all_gather(ln1_b, "fsdp", axis=0, tiled=True),
        lax.all_gather(w_q, "fsdp", axis=0, tiled=True),
        lax.all_gather(w_kv, "fsdp", axis=0, tiled=True),
        lax.all_gather(w_r, "fsdp", axis=0, tiled=True),
        lax.all_gather(bias_u, "fsdp", axis=0, tiled=True),
        lax.all_gather(bias_v, "fsdp", axis=0, tiled=True),
        lax.all_gather(w_o, "fsdp", axis=0, tiled=True),
        lax.all_gather(ln2_g, "fsdp", axis=0, tiled=True),
        lax.all_gather(ln2_b, "fsdp", axis=0, tiled=True),
        lax.all_gather(w_in, "fsdp", axis=0, tiled=True),
        lax.all_gather(b_in, "fsdp", axis=0, tiled=True),
        lax.all_gather(w_out, "fsdp", axis=0, tiled=True),
        lax.all_gather(b_out, "fsdp", axis=0, tiled=True),
        lax.all_gather(conv_w, "fsdp", axis=0, tiled=True),
        lax.all_gather(conv_b, "fsdp", axis=0, tiled=True),
    )
    grad_tokens, per_stream = jax.vmap(stream_grads, in_axes=(None, 0, 0, 0, 0))(
        regathered, tokens, memory, compressed, cotangent
    )
    (
        sum_ln1_g,
        sum_ln1_b,
        sum_w_q,
        sum_w_kv,
        sum_w_r,
        sum_bias_u,
        sum_bias_v,
        sum_w_o,
        sum_ln2_g,
        sum_ln2_b,
        sum_w_in,
        sum_b_in,
        sum_w_out,
        sum_b_out,
        sum_conv_w,
        sum_conv_b,
    ) = [jnp.sum(gradient, axis=0) for gradient in per_stream]
    summed = lax.psum(
        (
            sum_ln1_g,
            sum_ln1_b,
            sum_w_q,
            sum_w_kv,
            sum_w_r,
            sum_bias_u,
            sum_bias_v,
            sum_w_o,
            sum_ln2_g,
            sum_ln2_b,
            sum_w_in,
            sum_b_in,
            sum_w_out,
            sum_b_out,
            sum_conv_w,
            sum_conv_b,
        ),
        ("dp", "fsdp"),
    )
    pair_size = lax.axis_size("fsdp")
    pair_index = lax.axis_index("fsdp")
    totals = tuple(
        (
            lax.dynamic_slice_in_dim(
                gradient,
                pair_index * (gradient.shape[0] // pair_size),
                gradient.shape[0] // pair_size,
                0,
            )
            for gradient in summed
        )
    )
    return (
        mixed_out,
        compressed_next,
        recon_loss,
        grad_tokens,
        totals[0],
        totals[1],
        totals[2],
        totals[3],
        totals[4],
        totals[5],
        totals[6],
        totals[7],
        totals[8],
        totals[9],
        totals[10],
        totals[11],
        totals[12],
        totals[13],
        totals[14],
        totals[15],
    )


def solution(mesh):
    placed = (
        P(("dp", "fsdp"), None, None),
        P(("dp", "fsdp"), None, None),
        P(("dp", "fsdp"), None, None),
        P(("dp", "fsdp"), None, None),
        P("fsdp"),
        P("fsdp"),
        P("fsdp", None),
        P("fsdp", None),
        P("fsdp", None),
        P("fsdp"),
        P("fsdp"),
        P("fsdp", None),
        P("fsdp"),
        P("fsdp"),
        P("fsdp", None),
        P("fsdp"),
        P("fsdp", None),
        P("fsdp"),
        P("fsdp", None),
        P("fsdp"),
    )
    return jax.shard_map(
        per_device,
        mesh=mesh,
        in_specs=placed,
        out_specs=(
            P(("dp", "fsdp"), None, None),
            P(("dp", "fsdp"), None, None),
            P(("dp", "fsdp")),
            P(("dp", "fsdp"), None, None),
            P("fsdp"),
            P("fsdp"),
            P("fsdp", None),
            P("fsdp", None),
            P("fsdp", None),
            P("fsdp"),
            P("fsdp"),
            P("fsdp", None),
            P("fsdp"),
            P("fsdp"),
            P("fsdp", None),
            P("fsdp"),
            P("fsdp", None),
            P("fsdp"),
            P("fsdp", None),
            P("fsdp"),
        ),
        check_vma=False,
    )
```

profile of v0, /device:TPU:1, one launch (start us, length us, event | category | flops | bytes accessed | tf_op | source)
XLA Modules:
  0.0 1095.2 jit_solution(11989352400563501817)
XLA Ops:
  49.1 5.7 fusion.37
  54.8 4.4 fusion.21
  59.1 28.0 %all-gather.18.cloned.1.call-done = bf16[1024,1024]{1,0:T(8,128)(2,1)} async-done(((bf16[512,1024]{1,0:T(8,128)(2,1)}), bf16[1024,1024]{1,0:T(8,128)(2,1)}) %all-gather.18.cloned.1.call-update) | async-done | bytes 2097168 | tf_op jit(solution)/shard_map/all_gather | solution.py:343
  95.0 7.7 transpose.112
  102.7 5.5 slice.68
  108.2 6.0 reshape.1430
  114.2 34.9 %all-gather.16.cloned.1.call-done = bf16[1024,2048]{1,0:T(8,128)(2,1)} async-done(((bf16[512,2048]{1,0:T(8,128)(2,1)}), bf16[1024,2048]{1,0:T(8,128)(2,1)}) %all-gather.16.cloned.1.call-update) | async-done | bytes 4194320 | tf_op jit(solution)/shard_map/all_gather | solution.py:344
  149.1 6.2 fusion.10
  164.2 6.9 fusion.36
  172.4 14.8 %all-gather.22.cloned.1.call-done = bf16[1024,1024]{1,0:T(8,128)(2,1)} async-done(((bf16[512,1024]{1,0:T(8,128)(2,1)}), bf16[1024,1024]{1,0:T(8,128)(2,1)}) %all-gather.22.cloned.1.call-update) | async-done | bytes 2097168 | tf_op jit(solution)/shard_map/all_gather | solution.py:348
  197.7 74.9 %all-gather.28.cloned.1.call-done = bf16[3072,1024]{1,0:T(8,128)(2,1)} async-done(((bf16[1536,1024]{1,0:T(8,128)(2,1)}), bf16[3072,1024]{1,0:T(8,128)(2,1)}) %all-gather.28.cloned.1.call-update) | async-done | bytes 6291472 | tf_op jit(solution)/shard_map/all_gather | solution.py:355
  272.6 4.4 fusion.161
  290.0 7.7 convolution_bitcast_fusion
  297.6 84.1 %all-gather.24.cloned.1.call-done = bf16[1024,4096]{1,0:T(8,128)(2,1)} async-done(((bf16[512,4096]{1,0:T(8,128)(2,1)}), bf16[1024,4096]{1,0:T(8,128)(2,1)}) %all-gather.24.cloned.1.call-update) | async-done | bytes 8388624 | tf_op jit(solution)/shard_map/all_gather | solution.py:351
  381.7 6.9 convolution_add_fusion
  388.6 102.3 %all-gather.26.cloned.1.call-done = bf16[4096,1024]{1,0:T(8,128)(2,1)} async-done(((bf16[2048,1024]{1,0:T(8,128)(2,1)}), bf16[4096,1024]{1,0:T(8,128)(2,1)}) %all-gather.26.cloned.1.call-update) | async-done | bytes 8388624 | tf_op jit(solution)/shard_map/all_gather | solution.py:353
  490.9 8.8 convert_reduce_fusion
  506.7 8.3 fusion.23
  523.5 5.0 reshape.1440
  528.5 4.0 fusion.72
  532.6 8.2 fusion.86
  540.7 8.2 fusion.142
  554.6 7.3 reshape.1441
  579.2 6.0 fusion.146
  594.1 6.4 convolution_bitcast_fusion.2
  607.3 67.5 %all-reduce.2 = (f32[1024]{0:T(1024)S(1)}, f32[1024]{0:T(1024)S(1)}, f32[1024]{0:T(1024)S(1)}, f32[1024]{0:T(1024)S(1)}, f32[1024]{0:T(1024)S(1)}, /*index=5*/f3...) all-reduce(f32[1024]{0:T(1024)S(1)} %get-tuple-element.80, ...), channel_id=1, replica_groups=mesh['dp'=64,'fsdp'=2] {'dp','fsdp'}, use_global_device_ids=true, to_apply=%region_19.20 | all-reduce | flops 12288 | bytes 98304 | tf_op jit(solution)/shard_map/psum | solution.py:402
  680.6 7.7 fusion.33
  688.3 360.1 %all-reduce.6.cloned.1.call-done = (f32[1024,1024]{1,0:T(8,128)}, f32[1024,2048]{1,0:T(8,128)}, f32[1024,1024]{1,0:T(8,128)}, f32[1024,1024]{1,0:T(8,128)}, f32[...) async-done(((f32[1024,1024]{1,0:T(8,128)}, f32[1024,2048]{1,0:T(8,128)}, f32[1024,1024]{1,0:T(8,128)}, f32[1024,1024]{1,0:T(8,128)}, ...) | async-done | bytes 67108880 | tf_op jit(solution)/shard_map/psum | solution.py:402
  1056.5 5.4 constant_dynamic-slice_fusion.5
  1065.8 5.9 constant_dynamic-slice_fusion
  1071.8 6.6 copy.119
  1078.3 8.4 constant_dynamic-slice_fusion.1
  (307 shorter events, 153.8 us)
Async XLA Ops:
  7.2 47.6 %all-gather.20.cloned.1.call-start = ((), (), s32[]{:S(2)}) async-start(), calls=%async_computation.2 | async-start | bytes 3145728 | tf_op jit(solution)/shard_map/all_gather | solution.py:345
  7.9 79.2 %all-gather.18.cloned.1.call-start = ((), (), s32[]{:S(2)}) async-start(), calls=%async_computation.1 | async-start | bytes 3145728 | tf_op jit(solution)/shard_map/all_gather | solution.py:343
  8.7 140.4 %all-gather.16.cloned.1.call-start = ((), (), s32[]{:S(2)}) async-start(), calls=%async_computation | async-start | bytes 6291456 | tf_op jit(solution)/shard_map/all_gather | solution.py:344
  9.4 177.8 %all-gather.22.cloned.1.call-start = ((), (), s32[]{:S(2)}) async-start(), calls=%async_computation.3 | async-start | bytes 3145728 | tf_op jit(solution)/shard_map/all_gather | solution.py:348
  10.0 262.6 %all-gather.28.cloned.1.call-start = ((), (), s32[]{:S(2)}) async-start(), calls=%async_computation.6 | async-start | bytes 9437184 | tf_op jit(solution)/shard_map/all_gather | solution.py:355
  10.6 371.1 %all-gather.24.cloned.1.call-start = ((), (), s32[]{:S(2)}) async-start(), calls=%async_computation.4 | async-start | bytes 12582912 | tf_op jit(solution)/shard_map/all_gather | solution.py:351
  11.2 5.9 copy-start.72
  11.2 9.7 copy-start.73
  11.2 13.5 %copy-start.74 = (bf16[512]{0:T(512)(128)(2,1)S(1)}, bf16[512]{0:T(512)(128)(2,1)}, u32[]{:S(2)}) copy-start(bf16[512]{0:T(512)(128)(2,1)} %param.30) | copy-start | bytes 3076
  11.2 17.6 %copy-start.75 = (bf16[512]{0:T(512)(128)(2,1)S(1)}, bf16[512]{0:T(512)(128)(2,1)}, u32[]{:S(2)}) copy-start(bf16[512]{0:T(512)(128)(2,1)} %param.32) | copy-start | bytes 3076
  11.2 21.1 %copy-start.76 = (bf16[512]{0:T(512)(128)(2,1)S(1)}, bf16[512]{0:T(512)(128)(2,1)}, u32[]{:S(2)}) copy-start(bf16[512]{0:T(512)(128)(2,1)} %param.33) | copy-start | bytes 3076
  11.2 24.6 %copy-start.77 = (bf16[512]{0:T(512)(128)(2,1)S(1)}, bf16[512]{0:T(512)(128)(2,1)}, u32[]{:S(2)}) copy-start(bf16[512]{0:T(512)(128)(2,1)} %param.39) | copy-start | bytes 3076
  11.2 28.8 %copy-start.68 = (bf16[2048]{0:T(1024)(128)(2,1)S(1)}, bf16[2048]{0:T(1024)(128)(2,1)}, u32[]{:S(2)}) copy-start(bf16[2048]{0:T(1024)(128)(2,1)} %param.35) | copy-start | bytes 12292
  11.2 33.7 %copy-start = (f32[1,192,1024]{2,1,0:T(8,128)S(1)}, f32[1,192,1024]{2,1,0:T(8,128)}, u32[]{:S(2)}) copy-start(f32[1,192,1024]{2,1,0:T(8,128)} %param.21) | copy-start | bytes 2359300
  11.2 34.7 %copy-start.35 = (bf16[1,192,1024]{2,1,0:T(8,128)(2,1)S(1)}, bf16[1,192,1024]{2,1,0:T(8,128)(2,1)}, u32[]{:S(2)}) copy-start(bf16[1,192,1024]{2,1,0:T(8,128)(2,1)} %param.20) | copy-start | bytes 1179652
  11.3 479.6 %all-gather.26.cloned.1.call-start = ((), (), s32[]{:S(2)}) async-start(), calls=%async_computation.5 | async-start | bytes 12582912 | tf_op jit(solution)/shard_map/all_gather | solution.py:353
  12.0 34.1 %copy-start.1 = (f32[1,192,1024]{2,1,0:T(8,128)S(1)}, f32[1,192,1024]{2,1,0:T(8,128)}, u32[]{:S(2)}) copy-start(f32[1,192,1024]{2,1,0:T(8,128)} %param.22) | copy-start | bytes 2359300
  12.0 1036.4 %all-reduce.6.cloned.1.call-start = ((), (), s32[]{:S(2)}) async-start(), calls=%async_computation.7 | async-start | bytes 134217728 | tf_op jit(solution)/shard_map/psum | solution.py:402
  46.1 103.0 %copy-start.43 = (f32[192,1024]{1,0:T(8,128)}, f32[192,1024]{1,0:T(8,128)S(1)}, u32[]{:S(2)}) copy-start(f32[192,1024]{1,0:T(8,128)S(1)} %get-tuple-element.121) | copy-start | bytes 2359300
  90.5 68.6 %copy-start.22 = (bf16[24,8,8,128]{3,2,1,0:T(8,128)(2,1)}, bf16[24,8,8,128]{3,2,1,0:T(8,128)(2,1)S(1)}, u32[]{:S(2)}) copy-start(bf16[24,8,8,128]{3,2,1,0:T(8,128)(2,1)S(1)} %get-tuple-element.117) | copy-start | bytes 1179652
  172.4 22.5 %copy-start.24 = (bf16[1,192,8,128]{3,2,1,0:T(8,128)(2,1)}, bf16[1,192,8,128]{3,2,1,0:T(8,128)(2,1)S(1)}, u32[]{:S(2)}) copy-start(bf16[1,192,8,128]{3,2,1,0:T(8,128)(2,1)S(1)} %copy.96) | copy-start | bytes 1179652
  194.9 77.8 %copy-start.60 = (f32[2,1,512]{2,1,0:T(1,128)S(1)}, f32[2,1,512]{2,1,0:T(1,128)}, u32[]{:S(2)}) copy-start(f32[2,1,512]{2,1,0:T(1,128)} %convert_element_type.329) | copy-start | bytes 12292
  272.6 4.6 copy-start.50
  290.0 91.7 %copy-start.57 = (f32[192]{0:T(256)S(1)}, f32[192]{0:T(256)}, u32[]{:S(2)}) copy-start(f32[192]{0:T(256)} %copy-done.56) | copy-start | bytes 2308
  290.0 91.7 %copy-start.59 = (f32[192]{0:T(256)S(1)}, f32[192]{0:T(256)}, u32[]{:S(2)}) copy-start(f32[192]{0:T(256)} %fusion.131) | copy-start | bytes 2308
  290.0 91.7 %copy-start.62 = (f32[4096]{0:T(1024)S(1)}, f32[4096]{0:T(1024)}, u32[]{:S(2)}) copy-start(f32[4096]{0:T(1024)} %convert_element_type.292) | copy-start | bytes 49156
  490.9 8.8 copy-start.81
  532.5 8.2 copy-start.37
  540.7 8.3 copy-start.39
  540.7 10.0 copy-start.15
  1048.4 6.6 copy-start.42
  1051.7 10.2 copy-start.20
  (60 other events, 137.3 us)
Sparse Core Ops, SparseCore 0:
  9.7 39.0 all-gather.19
  50.5 36.6 all-gather.17
  88.8 60.2 all-gather.15
  150.6 36.6 all-gather.21
  188.7 83.8 all-gather.27
  274.1 107.4 all-gather.23
  383.3 107.5 all-gather.25
  585.3 462.9 all-reduce.5
where the time goes:
time: 1100 us
  waiting for transfers between devices  703 us (64%)
  matrix products  143 us (13%)
  local copies, waits for them, and re-layouts  107 us (10%)
  blocking collectives  98.4 us (9%)
  other arithmetic  26.1 us (2%)
  between operations  17.3 us (2%)
    psum x1, waiting for transfers between devices, per_device(): lax.psum((sum_ln1_g, sum_ln1_b, sum_w_q, sum_w_kv, sum_w_r, sum_bias_u, s...  360 us
    all_gather x1, waiting for transfers between devices, per_device(): lax.all_gather(w_out, 'fsdp', axis=0, tiled=True)  102 us
    all_gather x1, waiting for transfers between devices, per_device(): lax.all_gather(w_in, 'fsdp', axis=0, tiled=True)  84.1 us
    all_gather x1, waiting for transfers between devices, per_device(): lax.all_gather(conv_w, 'fsdp', axis=0, tiled=True)  74.9 us
    psum x1, blocking collectives, per_device(): lax.psum((sum_ln1_g, sum_ln1_b, sum_w_q, sum_w_kv, sum_w_r, sum_bias_u, s...  67.5 us
    dynamic_slice x16, local copies, waits for them, and re-layouts, per_device(): lax.dynamic_slice_in_dim(gradient, pair_index * (gradient.shape[0] // pai...  37.6 us
    all_gather x1, waiting for transfers between devices, per_device(): lax.all_gather(w_kv, 'fsdp', axis=0, tiled=True)  34.9 us
    all_gather x1, waiting for transfers between devices, per_device(): lax.all_gather(w_q, 'fsdp', axis=0, tiled=True)  28 us
  transfers between devices with their start and end apart: 8, of which 7 were waited for; matrix products, arithmetic and copies ran while one was open for 12% of the time, Pallas kernels for 0%

commit v1 on v0

v1 whole, which is shorter than its diff:
```python
import jax
import jax.numpy as jnp
from jax import lax
from jax.sharding import Mesh, PartitionSpec as P

H = 8
f32 = jnp.float32
bf16 = jnp.bfloat16
AXES = ("yh", "x", "z", "c", "yl")


def layer_norm(values, scaling, offset):
    center = values - jnp.mean(values, axis=-1, keepdims=True)
    spread = jnp.mean(center * center, axis=-1, keepdims=True)
    return center * lax.rsqrt(spread + 1e-05) * scaling + offset


def sinusoid(key_count, model_dim):
    distance = (key_count - 1 - jnp.arange(key_count)).astype(jnp.float32)
    inverse = 1.0 / 10000.0 ** (jnp.arange(0, model_dim, 2).astype(jnp.float32) / model_dim)
    angles = distance[:, None] * inverse[None, :]
    return jnp.concatenate([jnp.sin(angles), jnp.cos(angles)], axis=-1)


def rel_shift(scores):
    padded = jnp.pad(scores, ((0, 0), (0, 0), (1, 0)))
    padded = padded.reshape(scores.shape[0], scores.shape[2] + 1, scores.shape[1])
    return padded[:, 1:, :].reshape(scores.shape)


def softmax_rows(scores):
    largest = jnp.max(scores, axis=-1, keepdims=True)
    exponent = jnp.exp(scores - largest)
    return exponent / jnp.sum(exponent, axis=-1, keepdims=True)


def split_heads(rows):
    model_dim = rows.shape[1] // 2
    head_size = model_dim // H
    keys_h = rows[:, :model_dim].reshape(rows.shape[0], H, head_size)
    values_h = rows[:, model_dim:].reshape(rows.shape[0], H, head_size)
    return (keys_h, values_h)


def content_attend(asking, rows):
    keys_h, values_h = split_heads(rows)
    scores = jnp.einsum("ihd,jhd->hij", asking, keys_h, preferred_element_type=f32)
    attn_probs = softmax_rows(scores)
    mixture = jnp.einsum(
        "hij,jhd->ihd", attn_probs.astype(bf16), values_h, preferred_element_type=f32
    )
    return (mixture.reshape(asking.shape[0], rows.shape[1] // 2), attn_probs)


def dot(a, b):
    return jnp.dot(a, b, preferred_element_type=f32)


def dot_t(a, b):
    return lax.dot_general(a, b, (((1,), (1,)), ((), ())), preferred_element_type=f32)


def core_swap(v):
    return lax.ppermute(v, "c", [(0, 1), (1, 0)])


RING = {"x": ("x", "c"), "z": ("z", "c"), "y": ("yh", "c", "yl")}


def exchange(v, ring, masks):
    def flat(i, c):
        return (i // 2 * 2 + c) * 2 + i % 2 if ring == "y" else 2 * i + c

    pairs = [(flat(i, c), flat(i ^ masks[c], c)) for i in range(4) for c in range(2)]
    return lax.ppermute(v, RING[ring], pairs)


def pick(v, index, axis):
    return lax.dynamic_index_in_dim(v, index, axis, keepdims=False)


def quarters(place, core):
    first = jnp.where(core == 0, 1, 3)
    second = jnp.where(core == 0, 3, 1)
    return place, place ^ first, place ^ 2, place ^ second


def halve(send, keep_own, keep_far, ring):
    got = exchange(send, ring, (1, 3))
    onward = (keep_far.astype(f32) + got[1].astype(f32)).astype(bf16)
    last = exchange(onward, ring, (3, 1))
    return keep_own.astype(f32) + got[0].astype(f32) + last.astype(f32)


def ring_stage(v, axis, ring, place, core):
    own, first, far, second = quarters(place, core)
    send = jnp.stack([pick(v, first, axis), pick(v, far, axis)]).astype(bf16)
    return halve(send, pick(v, own, axis), pick(v, second, axis), ring)


def per_device(
    tokens,
    memory,
    compressed,
    cotangent,
    ln1_g,
    ln1_b,
    w_q,
    w_kv,
    w_r,
    bias_u,
    bias_v,
    w_o,
    ln2_g,
    ln2_b,
    w_in,
    b_in,
    w_out,
    b_out,
    conv_w,
    conv_b,
):
    tokens, memory, compressed, cotangent = tokens[0], memory[0], compressed[0], cotangent[0]
    yl, core = lax.axis_index("yl"), lax.axis_index("c")
    place = {"x": lax.axis_index("x"), "z": lax.axis_index("z")}
    first_half = yl == 0

    def swap(v, axis=1):
        n = v.shape[axis] // 2
        low = lax.slice_in_dim(v, 0, n, axis=axis)
        high = lax.slice_in_dim(v, n, 2 * n, axis=axis)
        return jnp.where(first_half, v, jnp.concatenate([high, low], axis=axis))

    parts = [ln1_g, ln1_b, bias_u, bias_v, ln2_g, ln2_b, b_out, conv_b, b_in]
    flat = jnp.concatenate(parts)
    flat_other = lax.ppermute(flat.reshape(-1, 128), "yl", [(0, 1), (1, 0)]).reshape(-1)
    lows = jnp.where(first_half, flat, flat_other)
    highs = jnp.where(first_half, flat_other, flat)
    vectors, at = [], 0
    for part in parts:
        n = part.shape[0]
        vectors.append(jnp.concatenate([lows[at : at + n], highs[at : at + n]]).astype(f32))
        at += n
    ln1_g, ln1_b, bias_u, bias_v, ln2_g, ln2_b, b_out, conv_b, b_in = vectors

    def over_y(w):
        n = w.shape[0] // 2
        got = exchange(lax.dynamic_slice_in_dim(w, core * n, n, 0), "y", (1, 3))
        twin = core_swap(got)
        low = jnp.where(core == 0, got, twin)
        high = jnp.where(core == 0, twin, got)
        return jnp.concatenate([w, low, high], axis=0)

    w_kv = over_y(w_kv)
    w_q = over_y(w_q)
    w_r = over_y(w_r)
    w_o = over_y(w_o)
    conv_w = over_y(conv_w)

    spot = (place["x"] * 4 + place["z"]) * 2 + core
    n_in, n_out = w_in.shape[0] // 32, w_out.shape[0] // 32
    width = w_out.shape[1]
    chunks = w_in.shape[1] // width
    piece_in = lax.dynamic_slice_in_dim(w_in, spot * n_in, n_in, 0)
    piece_in = piece_in.reshape(n_in, chunks, width).transpose(1, 0, 2).reshape(-1, width)
    piece_out = lax.dynamic_slice_in_dim(w_out, spot * n_out, n_out, 0)
    piece = lax.ppermute(
        jnp.concatenate([piece_in, piece_out], axis=0), "yl", [(0, 1), (1, 0)]
    )
    spread = lax.all_gather(piece, ("x", "z", "c"), axis=0)
    got_in = spread[:, : n_in * chunks].reshape(32, chunks, n_in, width)
    got_in = got_in.transpose(0, 2, 1, 3).reshape(32 * n_in, chunks * width)
    w_in = jnp.concatenate([w_in, got_in], axis=0)
    w_out = jnp.concatenate([w_out, spread[:, n_in * chunks :].reshape(-1, width)], axis=0)

    seg_len = tokens.shape[0]
    model_dim = w_q.shape[0]
    head_size = model_dim // H
    key_count = compressed.shape[0] + memory.shape[0] + seg_len
    first_query = key_count - seg_len
    factor = head_size ** (-0.5)
    wide_tokens = tokens.astype(f32)
    joined = jnp.concatenate([compressed, memory, wide_tokens], axis=0)
    normed = layer_norm(joined, ln1_g, ln1_b).astype(bf16)
    normed_rel = swap(normed)
    queries = dot(normed_rel[first_query:], w_q)
    key_value = dot(normed_rel, w_kv).astype(bf16)
    sinus_table = sinusoid(key_count, model_dim).astype(bf16)
    relative = dot(swap(sinus_table), w_r).astype(bf16)
    content = ((queries + bias_u) * factor).astype(bf16).reshape(seg_len, H, head_size)
    located = ((queries + bias_v) * factor).astype(bf16).reshape(seg_len, H, head_size)
    keys_h, values_h = split_heads(key_value)
    relative_h = relative.reshape(key_count, H, head_size)
    raw_scores = jnp.einsum("ihd,jhd->hij", located, relative_h, preferred_element_type=f32)
    scores = jnp.einsum(
        "ihd,jhd->hij", content, keys_h, preferred_element_type=f32
    ) + rel_shift(raw_scores)
    row_ids = jnp.arange(seg_len)[:, None]
    col_ids = jnp.arange(key_count)[None, :]
    allowed = col_ids <= row_ids + first_query
    attn_probs = softmax_rows(jnp.where(allowed[None], scores, -1e30))
    probs_low = attn_probs.astype(bf16)
    mixture = jnp.einsum("hij,jhd->ihd", probs_low, values_h, preferred_element_type=f32)
    attended = mixture.reshape(seg_len, model_dim).astype(bf16)
    residual = wide_tokens + dot(swap(attended), w_o)
    normed2 = layer_norm(residual, ln2_g, ln2_b).astype(bf16)
    pre_act = dot(swap(normed2), w_in) + b_in
    hidden = jax.nn.gelu(pre_act).astype(bf16)
    mixed_out = (residual + dot(swap(hidden), w_out) + b_out).astype(bf16)

    oldest = memory.reshape(seg_len // 3, 3 * model_dim).astype(bf16)
    compact = dot(swap(oldest), conv_w) + conv_b
    comp_normed = layer_norm(compact, ln1_g, ln1_b).astype(bf16)
    comp_pair = dot(swap(comp_normed), w_kv).astype(bf16)
    asking = (queries * factor).astype(bf16).reshape(seg_len, H, head_size)
    start_old = compressed.shape[0]
    target = content_attend(asking, key_value[start_old : start_old + seg_len])[0]
    guess, guess_probs = content_attend(asking, comp_pair)
    mismatch = target - guess
    recon_loss = jnp.mean(mismatch * mismatch)
    compact_len = seg_len // 3
    compressed_next = jnp.concatenate([compressed[compact_len:], compact], axis=0)

    def rows_of(x, both=None):
        t = x.T.reshape(2, 2, 4, 4, x.shape[1] // 64, x.shape[0])
        return jnp.concatenate([pick(t, core, 1), core_swap(pick(t, 1 - core, 1))], axis=-1)

    def both(dy):
        return jnp.concatenate([dy, core_swap(dy)], axis=0)

    def reduce(rows, dy, ring):
        axis = 1 if ring == "x" else 2
        own, first, far, second = quarters(place[ring], core)

        def make(index):
            return jnp.einsum(
                "yauk,kc->yauc", pick(rows, index, axis), dy, preferred_element_type=f32
            ).astype(bf16)

        send = jnp.stack([make(first), make(far)])
        kept = halve(send, make(own), make(second), ring)
        other = "z" if ring == "x" else "x"
        return ring_stage(kept, 1, other, place[other], core)

    def finish(v):
        got = exchange(pick(v, 1 - yl, 0).astype(bf16), "y", (1, 3))
        mine = (pick(v, yl, 0) + got.astype(f32)).astype(bf16)
        far = lax.ppermute(mine, "yh", [(0, 1), (1, 0)])
        return (mine.astype(f32) + far.astype(f32)).astype(bf16)

    def rows1024(v):
        y, u, cols = v.shape
        return v.reshape(y, u, cols // width, width).transpose(0, 2, 1, 3).reshape(y, -1, width)

    def gather_sums(sums):
        counts = [v.shape[1] * v.shape[2] // width for v in sums]
        done = finish(jnp.concatenate([rows1024(v) for v in sums], axis=1))
        whole = lax.all_gather(done, ("c", "x", "z"), axis=0)
        outs, at = [], 0
        for v, n in zip(sums, counts):
            u, cols = v.shape[1], v.shape[2]
            part = whole[:, at : at + n].reshape(32, cols // width, u, width)
            outs.append(part.transpose(0, 2, 1, 3).reshape(32 * u, cols).astype(f32))
            at += n
        return outs

    d_guess = (
        (-2.0 / (seg_len * model_dim) * mismatch).astype(bf16).reshape(seg_len, H, head_size)
    )
    comp_keys, comp_values = split_heads(comp_pair)
    d_gprobs = jnp.einsum("ihd,jhd->hij", d_guess, comp_values, preferred_element_type=f32)
    d_comp_values = jnp.einsum(
        "hij,ihd->jhd", guess_probs.astype(bf16), d_guess, preferred_element_type=f32
    )
    d_gscores = (
        guess_probs * (d_gprobs - jnp.sum(guess_probs * d_gprobs, axis=-1, keepdims=True))
    ).astype(bf16)
    d_comp_keys = jnp.einsum("hij,ihd->jhd", d_gscores, asking, preferred_element_type=f32)
    d_comp_pair = jnp.concatenate(
        [
            d_comp_keys.reshape(compact_len, model_dim),
            d_comp_values.reshape(compact_len, model_dim),
        ],
        axis=1,
    ).astype(bf16)
    d_comp_normed = swap(dot_t(d_comp_pair, w_kv))
    unused, norm_back3 = jax.vjp(lambda values: layer_norm(values, ln1_g, ln1_b), compact)
    d_compact = norm_back3(d_comp_normed)[0].astype(bf16)
    d_conv_b = jnp.sum(d_compact.astype(f32), axis=0)
    part_conv = reduce(rows_of(oldest), both(d_compact), "z")

    cot_wide = cotangent.astype(f32)
    d_b_out = jnp.sum(cot_wide, axis=0)
    d_hidden = swap(dot_t(cotangent, w_out))
    part_w_out = reduce(rows_of(hidden), both(cotangent), "x")
    unused, gelu_back = jax.vjp(jax.nn.gelu, pre_act)
    d_pre = gelu_back(d_hidden)[0].astype(bf16)
    d_b_in = jnp.sum(d_pre.astype(f32), axis=0)
    part_w_in = reduce(rows_of(normed2), both(d_pre), "z")
    d_normed2 = swap(dot_t(d_pre, w_in))
    unused, norm_back2 = jax.vjp(layer_norm, residual, ln2_g, ln2_b)
    d_mid_norm, d_ln2_g, d_ln2_b = norm_back2(d_normed2)
    d_residual = cot_wide + d_mid_norm
    d_branch = d_residual.astype(bf16)
    part_w_o = reduce(rows_of(attended), both(d_branch), "x")
    d_attended = swap(dot_t(d_branch, w_o)).astype(bf16).reshape(seg_len, H, head_size)
    d_probs = jnp.einsum("ihd,jhd->hij", d_attended, values_h, preferred_element_type=f32)
    d_values = jnp.einsum("hij,ihd->jhd", probs_low, d_attended, preferred_element_type=f32)
    d_scores = (
        attn_probs * (d_probs - jnp.sum(attn_probs * d_probs, axis=-1, keepdims=True))
    ).astype(bf16)
    d_content = jnp.einsum("hij,jhd->ihd", d_scores, keys_h, preferred_element_type=f32)
    d_keys = jnp.einsum("hij,ihd->jhd", d_scores, content, preferred_element_type=f32)
    unused, shift_back = jax.vjp(rel_shift, raw_scores)
    d_raw = shift_back(d_scores.astype(f32))[0].astype(bf16)
    d_located = jnp.einsum("hij,jhd->ihd", d_raw, relative_h, preferred_element_type=f32)
    d_relative = jnp.einsum("hij,ihd->jhd", d_raw, located, preferred_element_type=f32)
    d_relative = d_relative.reshape(key_count, model_dim).astype(bf16)
    d_content = d_content.reshape(seg_len, model_dim) * factor
    d_located = d_located.reshape(seg_len, model_dim) * factor
    d_bias_u = jnp.sum(d_content, axis=0)
    d_bias_v = jnp.sum(d_located, axis=0)
    d_queries = (d_content + d_located).astype(bf16)
    part_w_q = reduce(rows_of(normed[first_query:]), both(d_queries), "z")
    part_w_r = reduce(rows_of(sinus_table), both(d_relative), "x")
    d_pair = jnp.concatenate(
        [d_keys.reshape(key_count, model_dim), d_values.reshape(key_count, model_dim)], axis=1
    ).astype(bf16)
    part_w_kv = reduce(rows_of(normed), both(d_pair), "x")
    d_normed = swap(dot_t(d_pair, w_kv))
    d_normed_q = swap(dot_t(d_queries, w_q))
    d_normed = jnp.concatenate(
        [d_normed[:first_query], d_normed[first_query:] + d_normed_q], axis=0
    )
    unused, norm_back1 = jax.vjp(layer_norm, joined, ln1_g, ln1_b)
    d_joined, d_ln1_g, d_ln1_b = norm_back1(d_normed)
    d_tokens = d_residual + d_joined[first_query:]

    g_conv, g_out, g_in = gather_sums([part_conv, part_w_out, part_w_in])
    g_o, g_q, g_r, g_kv = gather_sums([part_w_o, part_w_q, part_w_r, part_w_kv])

    small = [d_ln1_g, d_ln1_b, d_bias_u, d_bias_v, d_ln2_g, d_ln2_b, d_b_out, d_conv_b, d_b_in]
    total = jnp.concatenate(small).reshape(-1, 128)
    total = total + core_swap(total)
    for ring in ("x", "z", "y"):
        total = total + exchange(total, ring, (1, 1))
        total = total + exchange(total, ring, (2, 2) if ring == "y" else (3, 3))
    total = total.reshape(-1)
    halves, at = [], 0
    for v in small:
        n = v.shape[0]
        halves.append(lax.dynamic_slice_in_dim(total[at : at + n], yl * (n // 2), n // 2, 0))
        at += n
    t_ln1_g, t_ln1_b, t_bu, t_bv, t_ln2_g, t_ln2_b, t_bout, t_convb, t_bin = halves
    return (
        mixed_out[None],
        compressed_next[None],
        recon_loss[None],
        d_tokens[None],
        t_ln1_g,
        t_ln1_b,
        g_q,
        g_kv,
        g_r,
        t_bu,
        t_bv,
        g_o,
        t_ln2_g,
        t_ln2_b,
        g_in,
        t_bin,
        g_out,
        t_bout,
        g_conv,
        t_convb,
    )


def solution(mesh):
    fine = Mesh(mesh.devices.reshape(2, 4, 4, 2, 2), AXES)
    stream = P(AXES, None, None)
    vec, mat = P("yl"), P("yl", None)
    weights = (vec, vec, mat, mat, mat, vec, vec, mat, vec, vec, mat, vec, mat, vec, mat, vec)
    return jax.shard_map(
        per_device,
        mesh=fine,
        in_specs=(stream,) * 4 + weights,
        out_specs=(stream, stream, P(AXES), stream) + weights,
        check_vma=False,
    )
```

time: 1100 us -> 594 us (0.54)
  the two profiles are of different devices: /device:TPU:1 before, /device:TPU:16 now
where the time goes in v1:
time: 594 us; the launch traced here: 584 us
  local copies, waits for them, and re-layouts  173 us (29%)
  matrix products  131 us (22%)
  waiting for transfers between devices  125 us (21%)
  starting transfers between devices  73.4 us (12%)
  other arithmetic  62.4 us (11%)
  between operations  18.4 us (3%)
    ppermute x41, waiting for transfers between devices, exchange(): return lax.ppermute(v, RING[ring], pairs)  111 us
    ppermute x41, starting transfers between devices, exchange(): return lax.ppermute(v, RING[ring], pairs)  63.1 us
    unnamed x293, local copies, waits for them, and re-layouts  56.3 us
    dot_general x28, matrix products, make(): jnp.einsum('yauk,kc->yauc', pick(rows, index, axis), dy, preferred_elemen...  51 us
    dot_general x8, matrix products, dot(): return jnp.dot(a, b, preferred_element_type=f32)  28.1 us
    dot_general x6, matrix products, dot_t(): lax.dot_general(a, b, (((1,), (1,)), ((), ())), preferred_element_type=f32)  15.9 us
    reshape x2, local copies, waits for them, and re-layouts, rel_shift(): padded.reshape(scores.shape[0], scores.shape[2] + 1, scores.shape[1])  14.9 us
    convert_element_type x5, other arithmetic, gather_sums(): outs.append(part.transpose(0, 2, 1, 3).reshape(32 * u, cols).astype(f32))  13.3 us
  transfers between devices with their start and end apart: 68, of which 26 were waited for; matrix products, arithmetic and copies ran while one was open for 54% of the time, Pallas kernels for 0%

profile of v1, /device:TPU:16, one launch (start us, length us, event | category | flops | bytes accessed | tf_op | source)
XLA Modules:
  0.0 583.5 jit_solution(17747149972641007291)
XLA Ops:
  33.0 4.8 constant_dynamic-update-slice_fusion.1
  40.3 5.6 fusion.109
  88.8 7.6 %reshape.558 = f32[8,577,192]{2,1,0:T(8,128)} reshape(f32[8,192,577]{2,1,0:T(8,128)} %pad.13) | data formatting | bytes 7090176 | tf_op jit(solution)/shard_map/reshape | solution.py:27
  96.4 5.2 slice.474
  101.6 6.0 %reshape.559 = f32[8,192,576]{2,1,0:T(8,128)} reshape(f32[8,576,192]{2,1,0:T(8,128)} %slice.474) | data formatting | bytes 7077888 | tf_op jit(solution)/shard_map/reshape | solution.py:28
  125.7 6.2 %fusion.88 = bf16[8,24,8,128]{3,2,1,0:T(8,128)(2,1)S(1)} fusion(bf16[72,8,8,128]{3,2,1,0:T(8,128)(2,1)S(1)} %get-tuple-element.57, f32[8,192]{1,0:T(8,128)S(1)} %get-tuple-element.154, f32[8,192,576]{2,1,0:T(8,128)} %copy-done.6), kind=kOutput, calls=%fused_computation.169 | convolution fusion | flops 229345344 | bytes 5117952 | tf_op jit(solution)/shard_map/hij,jhd->ihd/dot_general | solution.py:203
  163.2 4.1 fusion.419
  180.0 11.6 %convert_reduce_fusion = (f32[4096]{0:T(1024)}, bf16[192,4096]{1,0:T(8,128)(2,1)}, bf16[192,4096]{1,0:T(8,128)(2,1)}, f32[192,4096]{1,0:T(8,128)}) fusion(f32[192,4096]{1,0:T(8,128)S(1)} %fusion.11, f32[192,2048]{1,0:T(8,128)S(1)} %get-tuple-element.47, f32[192,2048]{1,0:T(8,128)S(1)} %get-tuple-element.46, pred[]{:T(512)S(6)} %eq.4, ...), kind=kOutput, calls=%fused_computation.55 | convolution fusion | flops 1632825344 | bytes 21790720 | tf_op jit(solution)/shard_map/dot_general | solution.py:56
  191.5 4.3 fusion.453
  211.9 7.3 %reshape.574 = bf16[8,192,577]{2,1,0:T(8,128)(2,1)} reshape(bf16[8,577,192]{2,1,0:T(8,128)(2,1)} %pad.14) | data formatting | bytes 3545088 | tf_op jit(solution)/shard_map/transpose(jvp())/reshape | solution.py:27
  228.9 7.1 %fusion.72 = bf16[8,72,8,128]{3,2,1,0:T(8,128)(2,1)S(1)} fusion(f32[8,192]{1,0:T(8,128)S(1)} %copy-done.108, f32[8,192,576]{2,1,0:T(8,128)} %copy-done.6, bf16[192,1024]{1,0:T(8,128)(2,1)S(1)} %copy-done.84, bf16[192,512]{1,0:T(8,128)(2,1)} %copy-done.99, bf16[192,512]{1,0:T(8,128)(2,1)} %copy-done.98, pred[]{:T(512)S(6)} %eq.4), kind=kOutput, calls=%fused_computation.149 | convolution fusion | flops 230721600 | bytes 5511169 | tf_op jit(solution)/shard_map/hij,ihd->jhd/dot_general | solution.py:308
  281.5 4.9 collective-permute-done.23
  312.9 4.8 collective-permute-done.41
  338.3 4.0 collective-permute-done.44
  350.0 6.4 %collective-permute-done.47 = bf16[2,2,4,48,1024]{4,3,2,1,0:T(8,128)(2,1)} collective-permute-done((bf16[2,2,4,48,1024]{4,3,2,1,0:T(8,128)(2,1)}, bf16[2,2,4,48,1024]{4,3,2,1,0:T(8,128)(2,1)}, u32[]{:S(2)}, u32[]{:S(2)}) %collective-permute-start.47) | collective-permute-done | bytes 1572896 | tf_op jit(solution)/shard_map/ppermute | solution.py:75
  358.0 6.1 %collective-permute-start.48 = (bf16[2,4,48,1024]{3,2,1,0:T(8,128)(2,1)S(1)}, bf16[2,4,48,1024]{3,2,1,0:T(8,128)(2,1)S(1)}, u32[]{:S(2)}, u32[]{:S(2)}) collective-permute-start(bf16[2,4,48,1024]{3,2,1,0:T(8,128)(2,1)S(1)} %fusion.58), channel_id=1, source_target_pairs={{0,12},{2,6},{4,8},{6,2},{8,4},{10,14},{12,0},{14,10},{1,13},{3,7}... | collective-permute-start | bytes 2359304 | tf_op jit(solution)/shard_map/ppermute | solution.py:75
  364.1 6.0 %collective-permute-done.53 = bf16[2,2,4,64,1024]{4,3,2,1,0:T(8,128)(2,1)} collective-permute-done((bf16[2,2,4,64,1024]{4,3,2,1,0:T(8,128)(2,1)}, bf16[2,2,4,64,1024]{4,3,2,1,0:T(8,128)(2,1)}, u32[]{:S(2)}, u32[]{:S(2)}) %collective-permute-start.53) | collective-permute-done | bytes 2097184 | tf_op jit(solution)/shard_map/ppermute | solution.py:75
  373.8 30.5 %collective-permute-done.59 = bf16[2,2,4,16,4096]{4,3,2,1,0:T(8,128)(2,1)S(1)} collective-permute-done((bf16[2,2,4,16,4096]{4,3,2,1,0:T(8,128)(2,1)S(1)}, bf16[2,2,4,16,4096]{4,3,2,1,0:T(8,128)(2,1)S(1)}, u32[]{:S(2)}, u32[]{:S(2)}) %collective-permute-start.59) | collective-permute-done | bytes 2097184 | tf_op jit(solution)/shard_map/ppermute | solution.py:75
  407.0 5.7 collective-permute-start.60
  417.3 8.2 %collective-permute-done.60 = bf16[2,4,16,4096]{3,2,1,0:T(8,128)(2,1)S(1)} collective-permute-done((bf16[2,4,16,4096]{3,2,1,0:T(8,128)(2,1)S(1)}, bf16[2,4,16,4096]{3,2,1,0:T(8,128)(2,1)S(1)}, u32[]{:S(2)}, u32[]{:S(2)}) %collective-permute-start.60) | collective-permute-done | bytes 1048608 | tf_op jit(solution)/shard_map/ppermute | solution.py:75
  440.8 4.6 collective-permute-done.62
  445.9 7.4 %collective-permute-done.63 = bf16[176,1024]{1,0:T(8,128)(2,1)S(1)} collective-permute-done((bf16[176,1024]{1,0:T(8,128)(2,1)S(1)}, bf16[176,1024]{1,0:T(8,128)(2,1)S(1)}, u32[]{:S(2)}, u32[]{:S(2)}) %collective-permute-start.63) | collective-permute-done | bytes 360480 | tf_op jit(solution)/shard_map/ppermute | solution.py:75
  453.6 8.9 %collective-permute-done.64 = bf16[176,1024]{1,0:T(8,128)(2,1)S(1)} collective-permute-done((bf16[176,1024]{1,0:T(8,128)(2,1)S(1)}, bf16[176,1024]{1,0:T(8,128)(2,1)S(1)}, u32[]{:S(2)}, u32[]{:S(2)}) %collective-permute-start.64) | collective-permute-done | bytes 360480 | tf_op jit(solution)/shard_map/ppermute | solution.py:248
  491.5 6.3 %fusion.89 = bf16[1,192,1024]{2,1,0:T(8,128)(2,1)} fusion(f32[192,1024]{1,0:T(8,128)S(1)} %get-tuple-element.157, bf16[2048,1024]{1,0:T(8,128)(2,1)} %bitcast.769, bf16[2048,1024]{1,0:T(8,128)(2,1)} %param.36, bf16[192,4096]{1,0:T(8,128)(2,1)S(1)} %copy-done.42, bf16[192,2048]{1,0:T(8,128)(2,1)S(1)} %get-tuple-element.69, ...), kind=kOutput, calls=%fused_computation.170 | convolution fusion | flops 1631911936 | bytes 12718081 | tf_op jit(solution)/shard_map/dot_general | solution.py:56
  497.9 5.1 collective-permute-done.15
  514.8 4.4 collective-permute-done.18
  529.3 4.0 copy.205
  538.5 5.6 fusion.418
  544.1 4.0 slice.561
  548.1 7.1 %copy.168 = f32[32,4,16,1024]{3,1,2,0:T(4,128)S(1)} copy(bf16[32,4,16,1024]{3,2,1,0:T(8,128)(2,1)} %bitcast.741) | data formatting | bytes 12582912 | tf_op jit(solution)/shard_map/convert_element_type | solution.py:263
  555.3 11.8 %copy.206 = f32[64,8,4,1024]{3,1,2,0:T(8,128)} copy(f32[64,8,4,1024]{3,2,1,0:T(4,128)S(1)} %bitcast.729) | data formatting | bytes 16777216
  567.0 4.7 bitcast_convert_fusion
  (660 shorter events, 344.6 us)
Async XLA Ops:
  7.2 156.0 %all-gather.7.cloned.1.call-start = ((), (), s32[]{:S(2)}) async-start(), calls=%async_computation | async-start | bytes 8650752 | tf_op jit(solution)/shard_map/all_gather | solution.py:170
  9.2 72.1 %collective-permute-start.7 = (bf16[256,1024]{1,0:T(8,128)(2,1)}, bf16[256,1024]{1,0:T(8,128)(2,1)}, u32[]{:S(2)}, u32[]{:S(2)}) collective-permute-start(bf16[256,1024]{1,0:T(8,128)(2,1)} %constant_dynamic-slice_fusion.5), channel_id=1, source_target_pairs={{0,1},{2,67},{1,0},{3,66},{64,65},{66,3},{65,64},{67,2},{4,5},{6,7... | collective-permute-start | bytes 1572872 | tf_op jit(solution)/shard_map/ppermute | solution.py:75
  23.0 45.3 %collective-permute-start = (bf16[48,128]{1,0:T(8,128)(2,1)}, bf16[48,128]{1,0:T(8,128)(2,1)}, u32[]{:S(2)}, u32[]{:S(2)}) collective-permute-start(bf16[48,128]{1,0:T(8,128)(2,1)} %bitcast.4), channel_id=1, source_target_pairs={{0,1},{1,0},{2,3},{3,2},{4,5},{5,4},{6,7},{7,6},{8,9},{9,8},{10,11... | collective-permute-start | bytes 36872 | tf_op jit(solution)/shard_map/ppermute | solution.py:136
  26.1 55.7 %collective-permute-start.1 = (bf16[256,2048]{1,0:T(8,128)(2,1)}, bf16[256,2048]{1,0:T(8,128)(2,1)}, u32[]{:S(2)}, u32[]{:S(2)}) collective-permute-start(bf16[256,2048]{1,0:T(8,128)(2,1)} %constant_dynamic-slice_fusion.8), channel_id=1, source_target_pairs={{0,1},{2,67},{1,0},{3,66},{64,65},{66,3},{65,64},{67,2},{4,5},{6,7... | collective-permute-start | bytes 3145736 | tf_op jit(solution)/shard_map/ppermute | solution.py:75
  28.2 47.1 %collective-permute-start.5 = (bf16[256,1024]{1,0:T(8,128)(2,1)}, bf16[256,1024]{1,0:T(8,128)(2,1)}, u32[]{:S(2)}, u32[]{:S(2)}) collective-permute-start(bf16[256,1024]{1,0:T(8,128)(2,1)} %constant_dynamic-slice_fusion.6), channel_id=1, source_target_pairs={{0,1},{2,67},{1,0},{3,66},{64,65},{66,3},{65,64},{67,2},{4,5},{6,7... | collective-permute-start | bytes 1572872 | tf_op jit(solution)/shard_map/ppermute | solution.py:75
  31.6 20.8 %collective-permute-start.9 = (bf16[128,1024]{1,0:T(8,128)(2,1)}, bf16[128,1024]{1,0:T(8,128)(2,1)}, u32[]{:S(2)}, u32[]{:S(2)}) collective-permute-start(bf16[128,1024]{1,0:T(8,128)(2,1)} %pad_maximum_fusion.36), channel_id=1, source_target_pairs={{0,1},{1,0},{2,3},{3,2},{4,5},{5,4},{6,7},{7,6},{8,9},{9,8},{10,11... | collective-permute-start | bytes 786440 | tf_op jit(solution)/shard_map/ppermute | solution.py:167
  52.4 25.3 %collective-permute-start.3 = (bf16[256,1024]{1,0:T(8,128)(2,1)}, bf16[256,1024]{1,0:T(8,128)(2,1)}, u32[]{:S(2)}, u32[]{:S(2)}) collective-permute-start(bf16[256,1024]{1,0:T(8,128)(2,1)} %constant_dynamic-slice_fusion.7), channel_id=1, source_target_pairs={{0,1},{2,67},{1,0},{3,66},{64,65},{66,3},{65,64},{67,2},{4,5},{6,7... | collective-permute-start | bytes 1572872 | tf_op jit(solution)/shard_map/ppermute | solution.py:75
  53.7 471.3 %all-gather.9.cloned.1.call-start = ((), (), s32[]{:S(2)}) async-start(), calls=%async_computation.1 | async-start | bytes 5406720 | tf_op jit(solution)/shard_map/all_gather | solution.py:258
  68.4 42.4 %collective-permute-start.10 = (bf16[768,1024]{1,0:T(8,128)(2,1)}, bf16[768,1024]{1,0:T(8,128)(2,1)}, u32[]{:S(2)}, u32[]{:S(2)}) collective-permute-start(bf16[768,1024]{1,0:T(8,128)(2,1)} %constant_dynamic-slice_fusion.2), channel_id=1, source_target_pairs={{0,1},{2,67},{1,0},{3,66},{64,65},{66,3},{65,64},{67,2},{4,5},{6,7... | collective-permute-start | bytes 4718600 | tf_op jit(solution)/shard_map/ppermute | solution.py:75
  77.8 186.0 %collective-permute-start.31 = (bf16[2,4,4,16,576]{4,3,2,1,0:T(8,128)(2,1)}, bf16[2,4,4,16,576]{4,3,2,1,0:T(8,128)(2,1)}, u32[]{:S(2)}, u32[]{:S(2)}) collective-permute-start(bf16[2,4,4,16,576]{4,3,2,1,0:T(8,128)(2,1)} %get-tuple-element.70), channel_id=1, source_target_pairs={{0,2},{2,0},{1,3},{3,1},{4,6},{6,4},{5,7},{7,5},{8,10},{10,8},{9,1... | collective-permute-start | bytes 1769480 | tf_op jit(solution)/shard_map/ppermute | solution.py:64
  81.3 79.3 %collective-permute-start.45 = (bf16[2,4,4,48,64]{4,3,2,1,0:T(8,128)(2,1)}, bf16[2,4,4,48,64]{4,3,2,1,0:T(8,128)(2,1)S(1)}, u32[]{:S(2)}, u32[]{:S(2)}) collective-permute-start(bf16[2,4,4,48,64]{4,3,2,1,0:T(8,128)(2,1)} %bitcast.132), channel_id=1, source_target_pairs={{0,2},{2,0},{1,3},{3,1},{4,6},{6,4},{5,7},{7,5},{8,10},{10,8},{9,1... | collective-permute-start | bytes 589832 | tf_op jit(solution)/shard_map/ppermute | solution.py:64
  81.8 25.9 %collective-permute-start.8 = (bf16[256,1024]{1,0:T(8,128)(2,1)}, bf16[256,1024]{1,0:T(8,128)(2,1)S(1)}, u32[]{:S(2)}, u32[]{:S(2)}) collective-permute-start(bf16[256,1024]{1,0:T(8,128)(2,1)} %collective-permute-done.7), channel_id=1, source_target_pairs={{0,2},{2,0},{1,3},{3,1},{4,6},{6,4},{5,7},{7,5},{8,10},{10,8},{9,1... | collective-permute-start | bytes 1572872 | tf_op jit(solution)/shard_map/ppermute | solution.py:64
  81.9 29.6 %collective-permute-start.2 = (bf16[256,2048]{1,0:T(8,128)(2,1)}, bf16[256,2048]{1,0:T(8,128)(2,1)S(1)}, u32[]{:S(2)}, u32[]{:S(2)}) collective-permute-start(bf16[256,2048]{1,0:T(8,128)(2,1)} %collective-permute-done.1), channel_id=1, source_target_pairs={{0,2},{2,0},{1,3},{3,1},{4,6},{6,4},{5,7},{7,5},{8,10},{10,8},{9,1... | collective-permute-start | bytes 3145736 | tf_op jit(solution)/shard_map/ppermute | solution.py:64
  108.5 128.8 %collective-permute-start.25 = (bf16[2,4,4,16,192]{4,3,2,1,0:T(8,128)(2,1)}, bf16[2,4,4,16,192]{4,3,2,1,0:T(8,128)(2,1)}, u32[]{:S(2)}, u32[]{:S(2)}) collective-permute-start(bf16[2,4,4,16,192]{4,3,2,1,0:T(8,128)(2,1)} %get-tuple-element.104), channel_id=1, source_target_pairs={{0,2},{2,0},{1,3},{3,1},{4,6},{6,4},{5,7},{7,5},{8,10},{10,8},{9,1... | collective-permute-start | bytes 589832 | tf_op jit(solution)/shard_map/ppermute | solution.py:64
  110.8 32.8 %collective-permute-start.11 = (bf16[768,1024]{1,0:T(8,128)(2,1)}, bf16[768,1024]{1,0:T(8,128)(2,1)}, u32[]{:S(2)}, u32[]{:S(2)}) collective-permute-start(bf16[768,1024]{1,0:T(8,128)(2,1)} %collective-permute-done.10), channel_id=1, source_target_pairs={{0,2},{2,0},{1,3},{3,1},{4,6},{6,4},{5,7},{7,5},{8,10},{10,8},{9,1... | collective-permute-start | bytes 4718600 | tf_op jit(solution)/shard_map/ppermute | solution.py:64
  159.3 82.1 %collective-permute-start.19 = (bf16[2,4,4,16,192]{4,3,2,1,0:T(8,128)(2,1)}, bf16[2,4,4,16,192]{4,3,2,1,0:T(8,128)(2,1)}, u32[]{:S(2)}, u32[]{:S(2)}) collective-permute-start(bf16[2,4,4,16,192]{4,3,2,1,0:T(8,128)(2,1)} %get-tuple-element.100), channel_id=1, source_target_pairs={{0,2},{2,0},{1,3},{3,1},{4,6},{6,4},{5,7},{7,5},{8,10},{10,8},{9,1... | collective-permute-start | bytes 589832 | tf_op jit(solution)/shard_map/ppermute | solution.py:64
  224.3 19.0 %collective-permute-start.20 = (bf16[192,1024]{1,0:T(8,128)(2,1)}, bf16[192,1024]{1,0:T(8,128)(2,1)}, u32[]{:S(2)}, u32[]{:S(2)}) collective-permute-start(bf16[192,1024]{1,0:T(8,128)(2,1)} %get-tuple-element.111), channel_id=1, source_target_pairs={{0,2},{2,0},{1,3},{3,1},{4,6},{6,4},{5,7},{7,5},{8,10},{10,8},{9,1... | collective-permute-start | bytes 1179656 | tf_op jit(solution)/shard_map/ppermute | solution.py:64
  237.3 33.8 %collective-permute-start.38 = (bf16[576,2048]{1,0:T(8,128)(2,1)}, bf16[576,2048]{1,0:T(8,128)(2,1)}, u32[]{:S(2)}, u32[]{:S(2)}) collective-permute-start(bf16[576,2048]{1,0:T(8,128)(2,1)} %bitcast_dynamic-update-slice_fusion), channel_id=1, source_target_pairs={{0,2},{2,0},{1,3},{3,1},{4,6},{6,4},{5,7},{7,5},{8,10},{10,8},{9,1... | collective-permute-start | bytes 7077896 | tf_op jit(solution)/shard_map/ppermute | solution.py:64
  237.6 26.3 %collective-permute-start.32 = (bf16[576,1024]{1,0:T(8,128)(2,1)}, bf16[576,1024]{1,0:T(8,128)(2,1)}, u32[]{:S(2)}, u32[]{:S(2)}) collective-permute-start(bf16[576,1024]{1,0:T(8,128)(2,1)} %bitcast.721), channel_id=1, source_target_pairs={{0,2},{2,0},{1,3},{3,1},{4,6},{6,4},{5,7},{7,5},{8,10},{10,8},{9,1... | collective-permute-start | bytes 3538952 | tf_op jit(solution)/shard_map/ppermute | solution.py:64
  258.4 73.9 %collective-permute-start.52 = (bf16[192,1024]{1,0:T(8,128)(2,1)S(1)}, bf16[192,1024]{1,0:T(8,128)(2,1)S(1)}, u32[]{:S(2)}, u32[]{:S(2)}) collective-permute-start(bf16[192,1024]{1,0:T(8,128)(2,1)S(1)} %bitcast.746), channel_id=1, source_target_pairs={{0,2},{2,0},{1,3},{3,1},{4,6},{6,4},{5,7},{7,5},{8,10},{10,8},{9,1... | collective-permute-start | bytes 1179656 | tf_op jit(solution)/shard_map/ppermute | solution.py:64
  263.8 79.3 %collective-permute-start.57 = (bf16[2,4,4,16,192]{4,3,2,1,0:T(8,128)(2,1)}, bf16[2,4,4,16,192]{4,3,2,1,0:T(8,128)(2,1)}, u32[]{:S(2)}, u32[]{:S(2)}) collective-permute-start(bf16[2,4,4,16,192]{4,3,2,1,0:T(8,128)(2,1)} %get-tuple-element.96), channel_id=1, source_target_pairs={{0,2},{2,0},{1,3},{3,1},{4,6},{6,4},{5,7},{7,5},{8,10},{10,8},{9,1... | collective-permute-start | bytes 589832 | tf_op jit(solution)/shard_map/ppermute | solution.py:64
  270.7 15.7 %collective-permute-start.33 = (bf16[2,2,4,16,1024]{4,3,2,1,0:T(8,128)(2,1)S(1)}, bf16[2,2,4,16,1024]{4,3,2,1,0:T(8,128)(2,1)S(1)}, u32[]{:S(2)}, u32[]{:S(2)}) collective-permute-start(bf16[2,2,4,16,1024]{4,3,2,1,0:T(8,128)(2,1)S(1)} %pad_maximum_fusion.32), channel_id=1, source_target_pairs={{0,16},{2,50},{16,0},{18,34},{32,48},{34,18},{48,32},{50,2},{1,17}... | collective-permute-start | bytes 1572872 | tf_op jit(solution)/shard_map/ppermute | solution.py:75
  278.0 15.6 %collective-permute-start.39 = (bf16[2,2,4,16,2048]{4,3,2,1,0:T(8,128)(2,1)S(1)}, bf16[2,2,4,16,2048]{4,3,2,1,0:T(8,128)(2,1)S(1)}, u32[]{:S(2)}, u32[]{:S(2)}) collective-permute-start(bf16[2,2,4,16,2048]{4,3,2,1,0:T(8,128)(2,1)S(1)} %pad_maximum_fusion.23), channel_id=1, source_target_pairs={{0,16},{2,50},{16,0},{18,34},{32,48},{34,18},{48,32},{50,2},{1,17}... | collective-permute-start | bytes 3145736 | tf_op jit(solution)/shard_map/ppermute | solution.py:75
  286.3 56.8 %collective-permute-start.58 = (bf16[192,4096]{1,0:T(8,128)(2,1)}, bf16[192,4096]{1,0:T(8,128)(2,1)}, u32[]{:S(2)}, u32[]{:S(2)}) collective-permute-start(bf16[192,4096]{1,0:T(8,128)(2,1)} %get-tuple-element.26), channel_id=1, source_target_pairs={{0,2},{2,0},{1,3},{3,1},{4,6},{6,4},{5,7},{7,5},{8,10},{10,8},{9,1... | collective-permute-start | bytes 4718600 | tf_op jit(solution)/shard_map/ppermute | solution.py:64
  312.9 20.2 %collective-permute-start.51 = (bf16[2,4,4,64,192]{4,3,2,1,0:T(8,128)(2,1)S(1)}, bf16[2,4,4,64,192]{4,3,2,1,0:T(8,128)(2,1)S(1)}, u32[]{:S(2)}, u32[]{:S(2)}) collective-permute-start(bf16[2,4,4,64,192]{4,3,2,1,0:T(8,128)(2,1)S(1)} %get-tuple-element.60), channel_id=1, source_target_pairs={{0,2},{2,0},{1,3},{3,1},{4,6},{6,4},{5,7},{7,5},{8,10},{10,8},{9,1... | collective-permute-start | bytes 2359304 | tf_op jit(solution)/shard_map/ppermute | solution.py:64
  332.3 24.1 %collective-permute-start.47 = (bf16[2,2,4,48,1024]{4,3,2,1,0:T(8,128)(2,1)}, bf16[2,2,4,48,1024]{4,3,2,1,0:T(8,128)(2,1)}, u32[]{:S(2)}, u32[]{:S(2)}) collective-permute-start(bf16[2,2,4,48,1024]{4,3,2,1,0:T(8,128)(2,1)} %pad_maximum_fusion.12), channel_id=1, source_target_pairs={{0,4},{2,14},{4,0},{6,10},{8,12},{10,6},{12,8},{14,2},{1,5},{3,15}... | collective-permute-start | bytes 4718600 | tf_op jit(solution)/shard_map/ppermute | solution.py:75
  338.3 31.8 %collective-permute-start.53 = (bf16[2,2,4,64,1024]{4,3,2,1,0:T(8,128)(2,1)}, bf16[2,2,4,64,1024]{4,3,2,1,0:T(8,128)(2,1)}, u32[]{:S(2)}, u32[]{:S(2)}) collective-permute-start(bf16[2,2,4,64,1024]{4,3,2,1,0:T(8,128)(2,1)} %pad_maximum_fusion.10), channel_id=1, source_target_pairs={{0,16},{2,50},{16,0},{18,34},{32,48},{34,18},{48,32},{50,2},{1,17}... | collective-permute-start | bytes 6291464 | tf_op jit(solution)/shard_map/ppermute | solution.py:75
  343.1 195.4 %all-gather.11.cloned.1.call-start = ((), (), s32[]{:S(2)}) async-start(), calls=%async_computation.2 | async-start | bytes 11894784 | tf_op jit(solution)/shard_map/all_gather | solution.py:258
  348.8 55.5 %collective-permute-start.59 = (bf16[2,2,4,16,4096]{4,3,2,1,0:T(8,128)(2,1)S(1)}, bf16[2,2,4,16,4096]{4,3,2,1,0:T(8,128)(2,1)S(1)}, u32[]{:S(2)}, u32[]{:S(2)}) collective-permute-start(bf16[2,2,4,16,4096]{4,3,2,1,0:T(8,128)(2,1)S(1)} %pad_maximum_fusion.11), channel_id=1, source_target_pairs={{0,4},{2,14},{4,0},{6,10},{8,12},{10,6},{12,8},{14,2},{1,5},{3,15}... | collective-permute-start | bytes 6291464 | tf_op jit(solution)/shard_map/ppermute | solution.py:75
  358.0 54.8 %collective-permute-start.48 = (bf16[2,4,48,1024]{3,2,1,0:T(8,128)(2,1)S(1)}, bf16[2,4,48,1024]{3,2,1,0:T(8,128)(2,1)S(1)}, u32[]{:S(2)}, u32[]{:S(2)}) collective-permute-start(bf16[2,4,48,1024]{3,2,1,0:T(8,128)(2,1)S(1)} %fusion.58), channel_id=1, source_target_pairs={{0,12},{2,6},{4,8},{6,2},{8,4},{10,14},{12,0},{14,10},{1,13},{3,7}... | collective-permute-start | bytes 2359304 | tf_op jit(solution)/shard_map/ppermute | solution.py:75
  372.1 43.1 %collective-permute-start.54 = (bf16[2,4,64,1024]{3,2,1,0:T(8,128)(2,1)S(1)}, bf16[2,4,64,1024]{3,2,1,0:T(8,128)(2,1)S(1)}, u32[]{:S(2)}, u32[]{:S(2)}) collective-permute-start(bf16[2,4,64,1024]{3,2,1,0:T(8,128)(2,1)S(1)} %fusion.49), channel_id=1, source_target_pairs={{0,48},{2,18},{16,32},{18,2},{32,16},{34,50},{48,0},{50,34},{1,49}... | collective-permute-start | bytes 3145736 | tf_op jit(solution)/shard_map/ppermute | solution.py:75
  407.0 18.5 %collective-permute-start.60 = (bf16[2,4,16,4096]{3,2,1,0:T(8,128)(2,1)S(1)}, bf16[2,4,16,4096]{3,2,1,0:T(8,128)(2,1)S(1)}, u32[]{:S(2)}, u32[]{:S(2)}) collective-permute-start(bf16[2,4,16,4096]{3,2,1,0:T(8,128)(2,1)S(1)} %fusion.14), channel_id=1, source_target_pairs={{0,12},{2,6},{4,8},{6,2},{8,4},{10,14},{12,0},{14,10},{1,13},{3,7}... | collective-permute-start | bytes 3145736 | tf_op jit(solution)/shard_map/ppermute | solution.py:75
  (171 other events, 1044.3 us)
Sparse Core Ops, SparseCore 0:
  53.9 55.2 all-gather.6
  343.2 58.2 all-gather.8
  463.6 63.1 all-gather.10

commit v2 on v1

v2 whole, which is shorter than its diff:
```python
import jax
import jax.numpy as jnp
from jax import lax
from jax.experimental import pallas as pl
from jax.experimental.pallas import tpu as pltpu
from jax.sharding import Mesh, PartitionSpec as P

H = 8
HD = 128
D = 1024
T = 192
KEYS = 576
PAD = 640
FF = 4096
FACTOR = HD ** (-0.5)
f32 = jnp.float32
bf16 = jnp.bfloat16
AXES = ("yh", "x", "z", "c", "yl")
RING = {"x": ("x", "c"), "z": ("z", "c"), "y": ("yh", "c", "yl")}


def sinusoid(key_count, model_dim):
    distance = (key_count - 1 - jnp.arange(key_count)).astype(f32)
    inverse = 1.0 / 10000.0 ** (jnp.arange(0, model_dim, 2).astype(f32) / model_dim)
    angles = distance[:, None] * inverse[None, :]
    return jnp.concatenate([jnp.sin(angles), jnp.cos(angles)], axis=-1)


def dot(a, b):
    return jnp.dot(a, b, preferred_element_type=f32)


def dot_t(a, b):
    return lax.dot_general(a, b, (((1,), (1,)), ((), ())), preferred_element_type=f32)


def t_dot(a, b):
    return lax.dot_general(a, b, (((0,), (0,)), ((), ())), preferred_element_type=f32)


def call(kernel, out, grid, in_specs, out_specs, scalars, args, scratch=()):
    return pl.pallas_call(
        kernel,
        out_shape=out,
        grid_spec=pltpu.PrefetchScalarGridSpec(
            num_scalar_prefetch=1,
            grid=grid,
            in_specs=in_specs,
            out_specs=out_specs,
            scratch_shapes=list(scratch),
        ),
        compiler_params=pltpu.CompilerParams(vmem_limit_bytes=56 << 20),
    )(scalars, *args)


def whole(a):
    zeros = (0,) * a.ndim
    return pl.BlockSpec(a.shape, lambda *_: zeros)


def shape(dims, dtype):
    return jax.ShapeDtypeStruct(dims, dtype)


def at(offset):
    return pl.multiple_of(offset, 128)


def center_scale(v):
    mid = v - jnp.mean(v, axis=-1, keepdims=True)
    r = lax.rsqrt(jnp.mean(mid * mid, axis=-1, keepdims=True) + 1e-5)
    return mid * r, r


def norm_back(xhat, r, g, dn):
    gd = dn * g
    return r * (
        gd
        - jnp.mean(gd, axis=-1, keepdims=True)
        - xhat * jnp.mean(gd * xhat, axis=-1, keepdims=True)
    )


def softmax(s):
    e = jnp.exp(s - jnp.max(s, axis=-1, keepdims=True))
    return e / jnp.sum(e, axis=-1, keepdims=True)


def first_norm(compressed, memory, tokens, g, b, none):
    def kernel(_, comp, mem, tok, g, b, out, old):
        gain, bias = g[...], b[...]

        def part(ref, base):
            for i in range(0, T, 32):
                xhat, r = center_scale(ref[i : i + 32, :].astype(f32))
                out[base + i : base + i + 32, :] = (xhat * gain + bias).astype(bf16)

        part(comp, 0)
        part(mem, T)
        part(tok, 2 * T)
        row = lax.broadcasted_iota(jnp.int32, (T // 3, T), 0)
        col = lax.broadcasted_iota(jnp.int32, (T // 3, T), 1)
        low = mem[...].astype(bf16)
        for tap in range(3):
            take = jnp.where(col == 3 * row + tap, 1.0, 0.0).astype(bf16)
            old[:, tap * D : (tap + 1) * D] = dot(take, low).astype(bf16)

    args = (compressed, memory, tokens, g, b)
    out = (shape((KEYS, D), bf16), shape((T // 3, 3 * D), bf16))
    return call(
        kernel, out, (1,), [whole(a) for a in args], [whole(o) for o in out], none, args
    )


def project(x, pieces, offsets, block, dtype, rows=None, row_block=0):
    rows = rows or x.shape[0]
    depth, n = x.shape[1], pieces[0].shape[1]

    def kernel(s, x_ref, *refs):
        total = None
        for i, w in enumerate(refs[:-1]):
            part = dot(x_ref[:, pl.ds(at(s[i]), w.shape[0])], w[...])
            total = part if total is None else total + part
        refs[-1][...] = total.astype(dtype)

    return call(
        kernel,
        shape((rows, n), dtype),
        (n // block,),
        [pl.BlockSpec((rows, depth), lambda j, s: (row_block, 0))]
        + [pl.BlockSpec((w.shape[0], block), lambda j, s: (0, j)) for w in pieces],
        pl.BlockSpec((rows, block), lambda j, s: (0, j)),
        offsets,
        (x, *pieces),
    )


def head(rows, row_block=0, first=0):
    return pl.BlockSpec((rows, HD), lambda h, s: (row_block, first + h))


def vec_head():
    return pl.BlockSpec((1, HD), lambda h, s: (0, h))


def attend(queries, key_value, relative, bias_u, bias_v, none):
    def kernel(_, q, k, v, rel, bu, bv, probs, out):
        pad = jnp.zeros((PAD - KEYS, HD), bf16)
        content = ((q[...] + bu[...]) * FACTOR).astype(bf16)
        located = ((q[...] + bv[...]) * FACTOR).astype(bf16)
        raw = dot_t(located, jnp.concatenate([rel[...], pad], axis=0))
        raw = pltpu.roll(raw, PAD - T + 1, 1, stride=1, stride_axis=0)
        s = dot_t(content, jnp.concatenate([k[...], pad], axis=0)) + raw
        row = lax.broadcasted_iota(jnp.int32, (T, PAD), 0)
        col = lax.broadcasted_iota(jnp.int32, (T, PAD), 1)
        p = softmax(jnp.where(col <= row + (KEYS - T), s, -1e30))
        probs[0] = p
        low = p.astype(bf16)
        out[...] = dot(low, jnp.concatenate([v[...], pad], axis=0)).astype(bf16)

    return call(
        kernel,
        (shape((H, T, PAD), f32), shape((T, D), bf16)),
        (H,),
        [head(T), head(KEYS), head(KEYS, 0, H), head(KEYS), vec_head(), vec_head()],
        [pl.BlockSpec((1, T, PAD), lambda h, s: (h, 0, 0)), head(T)],
        none,
        (queries, key_value, key_value, relative, bias_u, bias_v),
    )


def attend_back(queries, key_value, relative, bias_u, bias_v, probs, d_attended, none):
    def kernel(_, q, k, v, rel, bu, bv, probs, d_att, d_kv, d_rel, d_q, d_bu, d_bv):
        pad = jnp.zeros((PAD - KEYS, HD), bf16)
        content = ((q[...] + bu[...]) * FACTOR).astype(bf16)
        located = ((q[...] + bv[...]) * FACTOR).astype(bf16)
        p, da = probs[0], d_att[...]
        d_p = dot_t(da, jnp.concatenate([v[...], pad], axis=0))
        d_kv[1] = t_dot(p.astype(bf16), da)[:KEYS].astype(bf16)
        d_s = (p * (d_p - jnp.sum(p * d_p, axis=-1, keepdims=True))).astype(bf16)
        d_c = dot(d_s, jnp.concatenate([k[...], pad], axis=0)) * FACTOR
        d_kv[0] = t_dot(d_s, content)[:KEYS].astype(bf16)
        row = lax.broadcasted_iota(jnp.int32, (T, T), 0)
        col = lax.broadcasted_iota(jnp.int32, (T, T), 1)
        flip = jnp.where(row + col == T - 1, 1.0, 0.0).astype(bf16)
        d_raw = pltpu.roll(dot(flip, d_s), 0, 1, stride=1, stride_axis=0)
        d_raw = dot(flip, d_raw.astype(bf16)).astype(bf16)
        d_l = dot(d_raw, jnp.concatenate([rel[...], pad], axis=0)) * FACTOR
        d_rel[...] = t_dot(d_raw, located)[:KEYS].astype(bf16)
        d_q[...] = (d_c + d_l).astype(bf16)
        d_bu[...] = jnp.sum(d_c, axis=0, keepdims=True)
        d_bv[...] = jnp.sum(d_l, axis=0, keepdims=True)

    return call(
        kernel,
        (
            shape((2, KEYS, D), bf16),
            shape((KEYS, D), bf16),
            shape((T, D), bf16),
            shape((1, D), f32),
            shape((1, D), f32),
        ),
        (H,),
        [
            head(T),
            head(KEYS),
            head(KEYS, 0, H),
            head(KEYS),
            vec_head(),
            vec_head(),
            pl.BlockSpec((1, T, PAD), lambda h, s: (h, 0, 0)),
            head(T),
        ],
        [
            pl.BlockSpec((2, KEYS, HD), lambda h, s: (0, 0, h)),
            head(KEYS),
            head(T),
            vec_head(),
            vec_head(),
        ],
        none,
        (queries, key_value, key_value, relative, bias_u, bias_v, probs, d_attended),
    )


def out_and_norm(attended, pieces, offsets, tokens, g, b):
    def kernel(s, att, w0, w1, w2, tok, g, b, res, n2):
        total = tok[...].astype(f32)
        for i, w in enumerate((w0, w1, w2)):
            total = total + dot(att[:, pl.ds(at(s[i]), w.shape[0])], w[...])
        res[...] = total
        xhat, r = center_scale(total)
        n2[...] = (xhat * g[...] + b[...]).astype(bf16)

    args = (attended, *pieces, tokens, g, b)
    out = (shape((T, D), f32), shape((T, D), bf16))
    return call(
        kernel, out, (1,), [whole(a) for a in args], [whole(o) for o in out], offsets, args
    )


STEP = 512
HALF = FF // 2 // STEP


def feed_forward(n2, residual, cotangent, w_in, w_out, spread, b_in, b_out, scalars):
    n_in = w_in.shape[0] // 32
    n_out = w_out.shape[0] // 32
    skip = FF // D * n_in
    per = STEP // n_out
    K_NORM = 0.7978845608028654

    def natural(j, s):
        return lax.rem(j + s[0] * HALF, 2 * HALF)

    def kernel(s, n2, res, cot, wi0, wi1, wo0, wo1, bi, bo, hid, dpre, mixed, dn2, dbi, acc):
        j = pl.program_id(0)
        n = natural(j, s)
        mine = at(s[0] * (D // 2))
        theirs = at((1 - s[0]) * (D // 2))

        @pl.when(j == 0)
        def _():
            acc[...] = jnp.zeros_like(acc)
            dn2[...] = jnp.zeros_like(dn2)

        win0 = wi0[...]
        win1 = wi1[...].reshape(D // 2, STEP)
        pre = (
            dot(n2[:, pl.ds(mine, D // 2)], win0)
            + dot(n2[:, pl.ds(theirs, D // 2)], win1)
            + bi[pl.ds(n, 1), :]
        )
        cube = K_NORM * (pre + 0.044715 * (pre * pre * pre))
        t = jnp.tanh(cube)
        hidden = (0.5 * pre * (1.0 + t)).astype(bf16)
        slope = 0.5 * (1.0 + t) + (0.5 * K_NORM) * pre * (1.0 - t * t) * (
            1.0 + (3 * 0.044715) * (pre * pre)
        )
        hid[...] = hidden

        def rest(wo):
            d_pre = (dot_t(cot[...], wo) * slope).astype(bf16)
            dpre[...] = d_pre
            dbi[pl.ds(n, 1), :] = jnp.sum(d_pre.astype(f32), axis=0, keepdims=True)
            acc[...] += dot(hidden, wo)
            dn2[:, pl.ds(mine, D // 2)] += dot_t(d_pre, win0)
            dn2[:, pl.ds(theirs, D // 2)] += dot_t(d_pre, win1)

        @pl.when(j < HALF)
        def _():
            rest(wo0[...])

        @pl.when(j >= HALF)
        def _():
            rest(wo1[...].reshape(STEP, D))

        @pl.when(j == 2 * HALF - 1)
        def _():
            mixed[...] = (res[...] + acc[...] + bo[...]).astype(bf16)

    sub = D // STEP

    def in_other(j, s):
        n = natural(j, s)
        return (0, n // sub, lax.rem(n, sub))

    out = (
        shape((T, FF), bf16),
        shape((T, FF), bf16),
        shape((T, D), bf16),
        shape((T, D), f32),
        shape((2 * HALF, STEP), f32),
    )
    by_unit = pl.BlockSpec((T, STEP), lambda j, s: (0, natural(j, s)))
    return call(
        kernel,
        out,
        (2 * HALF,),
        [
            whole(n2),
            whole(residual),
            whole(cotangent),
            pl.BlockSpec((D // 2, STEP), lambda j, s: (0, natural(j, s))),
            pl.BlockSpec((32, n_in, STEP), in_other),
            pl.BlockSpec((STEP, D), lambda j, s: (jnp.minimum(j, HALF - 1), 0)),
            pl.BlockSpec(
                (per, n_out, D), lambda j, s: (jnp.maximum(j - HALF, 0), skip // n_out, 0)
            ),
            whole(b_in),
            whole(b_out),
        ],
        [by_unit, by_unit, whole(out[2]), whole(out[3]), whole(out[4])],
        scalars,
        (n2, residual, cotangent, w_in, spread, w_out, spread, b_in, b_out),
        [pltpu.VMEM((T, D), f32)],
    )


def second_norm_back(cotangent, d_n2, residual, g, pieces, offsets):
    def kernel(s, cot, dn, res, g, w0, w1, w2, d_res, d_br, d_att, dg, db, dbo):
        xhat, r = center_scale(res[...])
        dn, wide = dn[...], cot[...].astype(f32)
        dg[...] = jnp.sum(dn * xhat, axis=0, keepdims=True)
        db[...] = jnp.sum(dn, axis=0, keepdims=True)
        dbo[...] = jnp.sum(wide, axis=0, keepdims=True)
        total = wide + norm_back(xhat, r, g[...], dn)
        d_res[...] = total
        low = total.astype(bf16)
        d_br[...] = low
        for i, w in enumerate((w0, w1, w2)):
            d_att[:, pl.ds(at(s[i]), w.shape[0])] = dot_t(low, w[...]).astype(bf16)

    args = (cotangent, d_n2, residual, g, *pieces)
    out = (
        shape((T, D), f32),
        shape((T, D), bf16),
        shape((T, D), bf16),
        shape((1, D), f32),
        shape((1, D), f32),
        shape((1, D), f32),
    )
    return call(
        kernel, out, (1,), [whole(a) for a in args], [whole(o) for o in out], offsets, args
    )


def first_norm_back(d_kv, d_q, kv_pieces, q_pieces, compressed, memory, tokens, g, d_res, offsets):
    steps = 8
    wide, slim = 2 * D // steps, D // steps

    def kernel(s, dkv, dq, k0, k1, k2, q0, q1, q2, comp, mem, tok, g, dres, dtok, dg, db, acc):
        j = pl.program_id(0)

        @pl.when(j == 0)
        def _():
            acc[...] = jnp.zeros_like(acc)

        for i, (kw, qw) in enumerate(((k0, q0), (k1, q1), (k2, q2))):
            columns = pl.ds(at(s[i]), kw.shape[0])
            acc[:, columns] += dot_t(dkv[0], kw[...])
            acc[2 * T :, columns] += dot_t(dq[...], qw[...])

        @pl.when(j == steps - 1)
        def _():
            gain = g[...]
            sum_g = jnp.zeros((1, D), f32)
            sum_b = jnp.zeros((1, D), f32)
            for block, ref in enumerate((comp, mem, tok)):
                for i in range(0, T, 32):
                    xhat, r = center_scale(ref[i : i + 32, :].astype(f32))
                    dn = acc[block * T + i : block * T + i + 32, :]
                    sum_g += jnp.sum(dn * xhat, axis=0, keepdims=True)
                    sum_b += jnp.sum(dn, axis=0, keepdims=True)
                    if block == 2:
                        dtok[i : i + 32, :] = dres[i : i + 32, :] + norm_back(xhat, r, gain, dn)
            dg[...] = sum_g
            db[...] = sum_b

    rest = (compressed, memory, tokens, g, d_res)
    out = (shape((T, D), f32), shape((1, D), f32), shape((1, D), f32))
    return call(
        kernel,
        out,
        (steps,),
        [
            pl.BlockSpec((1, KEYS, wide), lambda j, s: (j // (steps // 2), 0, lax.rem(j, steps // 2))),
            pl.BlockSpec((T, slim), lambda j, s: (0, j)),
        ]
        + [pl.BlockSpec((w.shape[0], wide), lambda j, s: (0, j)) for w in kv_pieces]
        + [pl.BlockSpec((w.shape[0], slim), lambda j, s: (0, j)) for w in q_pieces]
        + [whole(a) for a in rest],
        [whole(o) for o in out],
        offsets,
        (d_kv, d_q, *kv_pieces, *q_pieces, *rest),
        [pltpu.VMEM((KEYS, D), f32)],
    )


def compress(oldest, pieces, offsets, bias, g, b):
    block = 256
    rows = T // 3

    def kernel(s, x, w0, w1, w2, bias, g, b, compact, normed):
        j = pl.program_id(0)
        total = bias[:, pl.ds(at(j * block), block)]
        for i, w in enumerate((w0, w1, w2)):
            total = total + dot(x[:, pl.ds(at(s[i]), w.shape[0])], w[...])
        compact[:, pl.ds(at(j * block), block)] = total

        @pl.when(j == D // block - 1)
        def _():
            xhat, r = center_scale(compact[...])
            normed[...] = (xhat * g[...] + b[...]).astype(bf16)

    rest = (bias, g, b)
    out = (shape((rows, D), f32), shape((rows, D), bf16))
    return call(
        kernel,
        out,
        (D // block,),
        [whole(oldest)]
        + [pl.BlockSpec((w.shape[0], block), lambda j, s: (0, j)) for w in pieces]
        + [whole(a) for a in rest],
        [whole(o) for o in out],
        offsets,
        (oldest, *pieces, *rest),
    )


def reconstruct(queries, key_value, comp_pair, none):
    rows = T // 3

    def kernel(_, q, k, v, ck, cv, loss, dck, dcv):
        h = pl.program_id(0)
        asking = (q[...] * FACTOR).astype(bf16)
        p = softmax(dot_t(asking, k[...])).astype(bf16)
        gp = softmax(dot_t(asking, ck[...]))
        low = gp.astype(bf16)
        miss = dot(p, v[...]) - dot(low, cv[...])

        @pl.when(h == 0)
        def _():
            loss[...] = jnp.zeros_like(loss)

        loss[...] += jnp.sum(miss * miss, axis=0, keepdims=True)
        d_guess = ((-2.0 / (T * D)) * miss).astype(bf16)
        d_gp = dot_t(d_guess, cv[...])
        dcv[...] = t_dot(low, d_guess).astype(bf16)
        d_gs = (gp * (d_gp - jnp.sum(gp * d_gp, axis=-1, keepdims=True))).astype(bf16)
        dck[...] = t_dot(d_gs, asking).astype(bf16)

    return call(
        kernel,
        (shape((1, HD), f32), shape((rows, D), bf16), shape((rows, D), bf16)),
        (H,),
        [head(T), head(T, 1), head(T, 1, H), head(rows), head(rows, 0, H)],
        [pl.BlockSpec((1, HD), lambda h, s: (0, 0)), head(rows), head(rows)],
        none,
        (queries, key_value, key_value, comp_pair, comp_pair),
    )


def compress_back(dck, dcv, pieces, offsets, compact, g):
    rows = T // 3

    def kernel(s, dck, dcv, w0, w1, w2, compact, g, d_compact, d_bias, dn):
        for i, w in enumerate((w0, w1, w2)):
            dn[:, pl.ds(at(s[i]), w.shape[0])] = dot_t(dck[...], w[:, :D]) + dot_t(
                dcv[...], w[:, D:]
            )
        xhat, r = center_scale(compact[...])
        low = norm_back(xhat, r, g[...], dn[...]).astype(bf16)
        d_compact[...] = low
        d_bias[...] = jnp.sum(low.astype(f32), axis=0, keepdims=True)

    args = (dck, dcv, *pieces, compact, g)
    out = (shape((rows, D), bf16), shape((1, D), f32))
    return call(
        kernel,
        out,
        (1,),
        [whole(a) for a in args],
        [whole(o) for o in out],
        offsets,
        args,
        [pltpu.VMEM((rows, D), f32)],
    )


def weight_grad(jobs, scalars):
    total = sum(j[3][0].shape[1] // (1 if j[4] else 2) for j in jobs)
    block = jobs[0][0][0].shape[1] // 8
    in_specs, args, widths = [], [], []
    for xs, row_block, rows, dys, ready in jobs:
        width = dys[0].shape[1] // (1 if ready else 2)
        widths.append(width)
        for x in xs:
            in_specs.append(
                pl.BlockSpec((rows, block), lambda q, y, s, r=row_block: (r, y * 4 + s[q]))
            )
        for dy in dys:
            in_specs.append(
                pl.BlockSpec((rows, width), lambda q, y, s, r=ready: (0, 0 if r else s[2]))
            )
        args += [*xs, *dys]

    def kernel(s, *refs):
        out = refs[-1]
        start = 0
        for i, width in enumerate(widths):
            xa, xb, da, db = refs[4 * i : 4 * i + 4]
            out[0, 0, :, start : start + width] = (
                t_dot(xa[...], da[...]) + t_dot(xb[...], db[...])
            ).astype(bf16)
            start += width

    return call(
        kernel,
        shape((2, 2, block, total), bf16),
        (2, 2),
        in_specs,
        pl.BlockSpec((1, 1, block, total), lambda q, y, s: (q, y, 0, 0)),
        scalars,
        args,
    )


def widen(gathered, start, rows, columns, swapped, none):
    u = rows // 16
    sub = u // 32
    chunks = columns // 2 // STEP
    order = [x * 4 + z for z in range(4) for x in range(4)] if swapped else list(range(16))

    def kernel(_, src, out):
        for to, frm in enumerate(order):
            out[to] = src[frm].astype(f32)

    return call(
        kernel,
        shape((16, u, columns), f32),
        (sub, 2, chunks),
        [
            pl.BlockSpec(
                (16, 32, STEP), lambda i, c, k, s: (c, start // 32 + k * sub + i, 0)
            )
        ],
        pl.BlockSpec((16, 32, STEP), lambda i, c, k, s: (0, i, c * chunks + k)),
        none,
        (gathered,),
    ).reshape(rows, columns)


def core_swap(v):
    return lax.ppermute(v, "c", [(0, 1), (1, 0)])


def pair_swap(v):
    return lax.ppermute(v, "yl", [(0, 1), (1, 0)])


def exchange(v, ring, masks):
    def flat(i, c):
        return (i // 2 * 2 + c) * 2 + i % 2 if ring == "y" else 2 * i + c

    pairs = [(flat(i, c), flat(i ^ masks[c], c)) for i in range(4) for c in range(2)]
    return lax.ppermute(v, RING[ring], pairs)


def pick(v, index, axis):
    return lax.dynamic_index_in_dim(v, index, axis, keepdims=False)


def quarters(place, core):
    first = jnp.where(core == 0, 1, 3)
    second = jnp.where(core == 0, 3, 1)
    return place, place ^ first, place ^ 2, place ^ second


def halve(send, keep, ring):
    got = exchange(send, ring, (1, 3))
    onward = (keep[1].astype(f32) + got[1].astype(f32)).astype(bf16)
    last = exchange(onward, ring, (3, 1))
    return keep[0].astype(f32) + got[0].astype(f32) + last.astype(f32)


def ring_stage(v, axis, ring, place, core):
    own, first, far, second = quarters(place, core)
    send = jnp.stack([pick(v, first, axis), pick(v, far, axis)]).astype(bf16)
    return halve(send, (pick(v, own, axis), pick(v, second, axis)), ring)


def per_device(
    tokens,
    memory,
    compressed,
    cotangent,
    ln1_g,
    ln1_b,
    w_q,
    w_kv,
    w_r,
    bias_u,
    bias_v,
    w_o,
    ln2_g,
    ln2_b,
    w_in,
    b_in,
    w_out,
    b_out,
    conv_w,
    conv_b,
):
    tokens, memory, compressed, cotangent = tokens[0], memory[0], compressed[0], cotangent[0]
    yl, core = lax.axis_index("yl"), lax.axis_index("c")
    place = {"x": lax.axis_index("x"), "z": lax.axis_index("z")}
    none = jnp.zeros((1,), jnp.int32)
    ints = lambda *v: jnp.stack([jnp.asarray(i, jnp.int32) for i in v])

    def thirds(rows):
        half = rows // 2
        other = (1 - yl) * half
        return ints(yl * half, other + core * (half // 2), other + (1 - core) * (half // 2))

    flat = jnp.concatenate(
        [ln1_g, ln1_b, bias_u, bias_v, ln2_g, ln2_b, b_out, conv_b, b_in]
    ).reshape(-1, STEP)
    flat_other = pair_swap(flat)
    low = jnp.where(yl == 0, flat, flat_other).astype(f32)
    high = jnp.where(yl == 0, flat_other, flat).astype(f32)
    full = jnp.concatenate([low[:8], high[:8]], axis=1)
    ln1_g, ln1_b, bias_u, bias_v, ln2_g, ln2_b, b_out, conv_b = [full[i : i + 1] for i in range(8)]
    b_in = jnp.concatenate([low[8:], high[8:]], axis=0)

    def over_y(w):
        n = w.shape[0] // 2
        got = exchange(lax.dynamic_slice_in_dim(w, core * n, n, 0), "y", (1, 3))
        return w, got, core_swap(got)

    kv_pieces = over_y(w_kv)
    q_pieces = over_y(w_q)
    r_pieces = over_y(w_r)
    o_pieces = over_y(w_o)
    conv_pieces = over_y(conv_w)
    thirds_d, thirds_c = thirds(D), thirds(3 * D)

    spot = (place["x"] * 4 + place["z"]) * 2 + core
    n_in, n_out = w_in.shape[0] // 32, w_out.shape[0] // 32
    piece_in = lax.dynamic_slice_in_dim(w_in, spot * n_in, n_in, 0)
    piece_out = lax.dynamic_slice_in_dim(w_out, spot * n_out, n_out, 0)
    piece = pair_swap(
        jnp.concatenate(
            [piece_in[:, i * D : (i + 1) * D] for i in range(FF // D)] + [piece_out], axis=0
        )
    )
    spread = lax.all_gather(piece, ("x", "z", "c"), axis=0)

    normed, oldest = first_norm(compressed, memory, tokens, ln1_g, ln1_b, none)
    key_value = project(normed, kv_pieces, thirds_d, 512, bf16)
    queries = project(normed, q_pieces, thirds_d, 512, f32, T, 2)
    sinus_table = sinusoid(KEYS, D).astype(bf16)
    relative = project(sinus_table, r_pieces, thirds_d, 512, bf16)
    probs, attended = attend(queries, key_value, relative, bias_u, bias_v, none)
    residual, normed2 = out_and_norm(attended, o_pieces, thirds_d, tokens, ln2_g, ln2_b)

    compact, comp_normed = compress(oldest, conv_pieces, thirds_c, conv_b, ln1_g, ln1_b)
    comp_pair = project(comp_normed, kv_pieces, thirds_d, 512, bf16)
    loss, d_ck, d_cv = reconstruct(queries, key_value, comp_pair, none)
    recon_loss = jnp.sum(loss) / (T * D)
    compressed_next = jnp.concatenate([compressed[T // 3 :], compact], axis=0)
    d_compact, d_conv_b = compress_back(d_ck, d_cv, kv_pieces, thirds_d, compact, ln1_g)

    def both(v):
        return (v, core_swap(v))

    def reduce(jobs, ring):
        own, first, far, second = quarters(place[ring], core)
        send = weight_grad(jobs, ints(first, far, core))
        keep = weight_grad(jobs, ints(own, second, core))
        kept = halve(send, keep, ring)
        other = "z" if ring == "x" else "x"
        y, rows, columns = kept.shape
        kept = kept.reshape(y, 4, rows // 4, columns)
        return ring_stage(kept, 1, other, place[other], core)

    def finish(sums):
        flat = [
            v.reshape(2, v.shape[1], -1, STEP).transpose(0, 2, 1, 3).reshape(2, -1, STEP)
            for v in sums
        ]
        v = jnp.concatenate(flat, axis=1)
        got = exchange(pick(v, 1 - yl, 0).astype(bf16), "y", (1, 3))
        mine = (pick(v, yl, 0) + got.astype(f32)).astype(bf16)
        far = lax.ppermute(mine, "yh", [(0, 1), (1, 0)])
        done = (mine.astype(f32) + far.astype(f32)).astype(bf16)
        return lax.all_gather(done, ("c", "x", "z"), axis=0)

    both_normed = both(normed)
    both_cot = both(cotangent)
    sum_conv = reduce([(both(oldest), 0, T // 3, both(d_compact), False)], "z")

    hidden, d_pre, mixed_out, d_normed2, d_b_in = feed_forward(
        normed2, residual, cotangent, w_in, w_out, spread, b_in, b_out, ints(yl)
    )
    sum_out = reduce([(both(hidden), 0, T, both_cot, False)], "x")
    sum_in = reduce([(both(normed2), 0, T, both(d_pre), False)], "z")
    d_residual, d_branch, d_attended, d_ln2_g, d_ln2_b, d_b_out = second_norm_back(
        cotangent, d_normed2, residual, ln2_g, o_pieces, thirds_d
    )
    sum_o = reduce([(both(attended), 0, T, both(d_branch), False)], "x")
    d_kv, d_relative, d_queries, d_bias_u, d_bias_v = attend_back(
        queries, key_value, relative, bias_u, bias_v, probs, d_attended, none
    )
    both_kv = (pick(d_kv, core, 0), core_swap(pick(d_kv, 1 - core, 0)))
    sum_kv = reduce([(both_normed, 0, KEYS, both_kv, True)], "x")
    sum_qr = reduce(
        [
            (both_normed, 2, T, both(d_queries), False),
            ((sinus_table, sinus_table), 0, KEYS, both(d_relative), False),
        ],
        "z",
    )
    d_tokens, d_ln1_g, d_ln1_b = first_norm_back(
        d_kv, d_queries, kv_pieces, q_pieces, compressed, memory, tokens, ln1_g, d_residual,
        thirds_d,
    )

    early = finish([sum_out, sum_in, sum_conv, sum_o])
    late = finish([sum_kv, sum_qr])
    g_out = widen(early, 0, FF // 2, D, False, none)
    g_in = widen(early, 128, D // 2, FF, True, none)
    g_conv = widen(early, 256, 3 * D // 2, D, True, none)
    g_o = widen(early, 352, D // 2, D, False, none)
    g_kv = widen(late, 0, D // 2, 2 * D, False, none)
    g_q = widen(late, 64, D // 2, D, True, none)
    g_r = widen(late, 96, D // 2, D, True, none)

    total = jnp.concatenate(
        [d_ln1_g, d_ln1_b, d_bias_u, d_bias_v, d_ln2_g, d_ln2_b, d_b_out, d_conv_b]
        + [d_b_in.reshape(4, D), jnp.zeros((4, D), f32)]
    )
    total = total + core_swap(total)
    for ring in ("x", "z", "y"):
        total = total + exchange(total, ring, (1, 1))
        total = total + exchange(total, ring, (2, 2) if ring == "y" else (3, 3))
    half = lax.dynamic_slice_in_dim(total[:8], yl * (D // 2), D // 2, 1)
    t_ln1_g, t_ln1_b, t_bu, t_bv, t_ln2_g, t_ln2_b, t_bout, t_convb = [half[i] for i in range(8)]
    t_bin = lax.dynamic_slice_in_dim(total[8:12], yl * 2, 2, 0).reshape(-1)
    return (
        mixed_out[None],
        compressed_next[None],
        recon_loss[None],
        d_tokens[None],
        t_ln1_g,
        t_ln1_b,
        g_q,
        g_kv,
        g_r,
        t_bu,
        t_bv,
        g_o,
        t_ln2_g,
        t_ln2_b,
        g_in,
        t_bin,
        g_out,
        t_bout,
        g_conv,
        t_convb,
    )


def solution(mesh):
    fine = Mesh(mesh.devices.reshape(2, 4, 4, 2, 2), AXES)
    stream = P(AXES, None, None)
    vec, mat = P("yl"), P("yl", None)
    weights = (vec, vec, mat, mat, mat, vec, vec, mat, vec, vec, mat, vec, mat, vec, mat, vec)
    return jax.shard_map(
        per_device,
        mesh=fine,
        in_specs=(stream,) * 4 + weights,
        out_specs=(stream, stream, P(AXES), stream) + weights,
        check_vma=False,
    )
```

time: 594 us -> 487 us (0.82)
  the two profiles are of different devices: /device:TPU:16 before, /device:TPU:1 now
where the time goes in v2:
time: 487 us; the launch traced here: 477 us
  Pallas kernels  203 us (42%)
  waiting for transfers between devices  121 us (25%)
  starting transfers between devices  71.9 us (15%)
  other arithmetic  33.3 us (7%)
  local copies, waits for them, and re-layouts  31.1 us (6%)
  between operations  17.1 us (4%)
    pallas_call x33, Pallas kernels, call(): pl.pallas_call(kernel, out_shape=out, grid_spec=pltpu.PrefetchScalarGridS...  203 us
    ppermute x37, waiting for transfers between devices, exchange(): return lax.ppermute(v, RING[ring], pairs)  89.6 us
    ppermute x37, starting transfers between devices, exchange(): return lax.ppermute(v, RING[ring], pairs)  51.7 us
    unnamed x128, local copies, waits for them, and re-layouts  17.3 us
    ppermute x18, starting transfers between devices, core_swap(): return lax.ppermute(v, 'c', [(0, 1), (1, 0)])  13.9 us
    all_gather x2, waiting for transfers between devices, finish(): return lax.all_gather(done, ('c', 'x', 'z'), axis=0)  11.2 us
    ppermute x2, waiting for transfers between devices, finish(): far = lax.ppermute(mine, 'yh', [(0, 1), (1, 0)])  10.9 us
    convert_element_type x12, other arithmetic, halve(): onward = (keep[1].astype(f32) + got[1].astype(f32)).astype(bf16)  9.86 us
  transfers between devices with their start and end apart: 62, of which 25 were waited for; matrix products, arithmetic and copies ran while one was open for 10% of the time, Pallas kernels for 38%

profile of v2, /device:TPU:1, one launch (start us, length us, event | category | flops | bytes accessed | tf_op | source)
XLA Modules:
  0.0 477.1 jit_solution(3739582901527367738)
XLA Ops:
  13.7 5.6 %collective-permute-done.9 = bf16[128,1024]{1,0:T(8,128)(2,1)S(1)} collective-permute-done((bf16[128,1024]{1,0:T(8,128)(2,1)S(1)}, bf16[128,1024]{1,0:T(8,128)(2,1)S(1)}, u32[]{:S(2)}, u32[]{:S(2)}) %collective-permute-start.9) | collective-permute-done | bytes 262176 | tf_op jit(solution)/shard_map/ppermute | solution.py:579
  72.8 7.1 %shard_map.349.k.v = bf16[576,2048]{1,0:T(8,128)(2,1)} custom-call(s32[3]{0:T(128)} %pad_add_fusion.s, bf16[576,1024]{1,0:T(8,128)(2,1)} %get-tuple-element.52.x_ref.refs_0_, bf16[512,2048]{1,0:T(8,128)(2,1)} %w0.7, bf16[256,2048]{1,0:T(8,128)(2,1)} %copy-done.1, bf16[256,2048]{1,0:T(8,128)(2,1)} %copy-done.2), custom_call_target="tpu_custom_call" | custom-call | tf_op jit(solution)/shard_map/pallas_call | solution.py:42
  79.9 9.0 %shard_map.351 = (f32[8,192,640]{2,1,0:T(8,128)}, bf16[192,1024]{1,0:T(8,128)(2,1)}) custom-call(s32[1]{0:T(128)} %constant.117.clone.1._, f32[192,1024]{1,0:T(8,128)} %shard_map.348.q, bf16[576,2048]{1,0:T(8,128)(2,1)} %shard_map.349.k.v, bf16[576,2048]{1,0:T(8,128)(2,1)} %shard_map.349.k.v, bf16[576,1024]{1,0:T(8,128)(2,1)} %shard_map.350.rel, ...), custom_call_target="tpu_custom_call" | custom-call | tf_op jit(solution)/shard_map/pallas_call | solution.py:42
  93.8 18.2 %shard_map.353 = (bf16[192,4096]{1,0:T(8,128)(2,1)}, bf16[192,4096]{1,0:T(8,128)(2,1)}, bf16[192,1024]{1,0:T(8,128)(2,1)}, f32[192,1024]{1,0:T(8,128)}, f32[8,512]{1,0:T(8,128)}) custom-call(s32[1]{0:T(128)} %bitcast.s, bf16[192,1024]{1,0:T(8,128)(2,1)} %get-tuple-element.54.n2.refs_0_, f32[192,1024]{1,0:T(8,128)} %get-tuple-element.55.res, ...), custom_call_target="tpu_custom_call" | custom-call | tf_op jit(solution)/shard_map/pallas_call | solution.py:42
  111.9 4.9 %shard_map.357 = (f32[192,1024]{1,0:T(8,128)}, bf16[192,1024]{1,0:T(8,128)(2,1)}, bf16[192,1024]{1,0:T(8,128)(2,1)}, f32[1,1024]{1,0:T(1,128)}, f32[1,1024]{1,0:T(1,128)}, /*index=5*/f32[1,1024]{1,0:T(1,128)}) custom-call(s32[3]{0:T(128)} %pad_add_fusion.s, bf16[192,1024]{1,0:T(8,128)(2,1)} %bitcast.282, f32[192,1024]{1,0:T(8,128)} %get-tuple-element.62.dn, ...), custom_call_target="tpu_custom_call" | custom-call | tf_op jit(solution)/shard_map/pallas_call | solution.py:42
  116.8 12.2 %shard_map.358 = (bf16[2,576,1024]{2,1,0:T(8,128)(2,1)}, bf16[576,1024]{1,0:T(8,128)(2,1)}, bf16[192,1024]{1,0:T(8,128)(2,1)}, f32[1,1024]{1,0:T(1,128)}, f32[1,1024]{1,0:T(1,128)}) custom-call(s32[1]{0:T(128)} %constant.117.clone.1._, f32[192,1024]{1,0:T(8,128)} %shard_map.348.q, bf16[576,2048]{1,0:T(8,128)(2,1)} %shard_map.349.k.v, ...), custom_call_target="tpu_custom_call" | custom-call | tf_op jit(solution)/shard_map/pallas_call | solution.py:42
  138.3 5.8 %shard_map.364 = bf16[2,2,128,1024]{3,2,1,0:T(8,128)(2,1)} custom-call(s32[3]{0:T(128)} %add_add_fusion.3.s, bf16[576,1024]{1,0:T(8,128)(2,1)} %get-tuple-element.52.x_ref.refs_0_, bf16[576,1024]{1,0:T(8,128)(2,1)} %copy-done, bf16[192,1024]{1,0:T(8,128)(2,1)} %get-tuple-element.65.dq.refs_2_, bf16[192,1024]{1,0:T(8,128)(2,1)} %copy-done.24, ...), custom_call_target="tpu_custom_call" | custom-call | tf_op jit(solution)/shard_map/pallas_call | solution.py:42
  148.5 6.3 %shard_map.362 = bf16[2,2,128,1024]{3,2,1,0:T(8,128)(2,1)} custom-call(s32[3]{0:T(128)} %add_add_fusion.1.s, bf16[576,1024]{1,0:T(8,128)(2,1)} %get-tuple-element.52.x_ref.refs_0_, bf16[576,1024]{1,0:T(8,128)(2,1)} %copy-done, bf16[576,1024]{1,0:T(8,128)(2,1)} %get-tuple-element.85.refs_2_, bf16[576,1024]{1,0:T(8,128)(2,1)} %collective-permute-done.20.refs_3_), custom_call_target="tpu_custom_call" | custom-call | tf_op jit(solution)/shard_map/pallas_call | solution.py:42
  158.9 6.1 %shard_map.354 = (f32[64,1024]{1,0:T(8,128)}, bf16[64,1024]{1,0:T(8,128)(2,1)}) custom-call(s32[3]{0:T(128)} %pad_add_fusion.1.s, bf16[64,3072]{1,0:T(8,128)(2,1)} %get-tuple-element.57.x.refs_0_, bf16[1536,1024]{1,0:T(8,128)(2,1)} %w0.5, bf16[768,1024]{1,0:T(8,128)(2,1)} %collective-permute-done.10.w1, bf16[768,1024]{1,0:T(8,128)(2,1)} %collective-permute-done.11.w2, ...), custom_call_target="tpu_custom_call" | custom-call | tf_op jit(solution)/shard_map/pallas_call | solution.py:42
  164.9 5.1 %shard_map.355.ck.cv = bf16[64,2048]{1,0:T(8,128)(2,1)} custom-call(s32[3]{0:T(128)} %pad_add_fusion.s, bf16[64,1024]{1,0:T(8,128)(2,1)} %get-tuple-element.59.x_ref, bf16[512,2048]{1,0:T(8,128)(2,1)} %w0.7, bf16[256,2048]{1,0:T(8,128)(2,1)} %copy-done.1, bf16[256,2048]{1,0:T(8,128)(2,1)} %copy-done.2), custom_call_target="tpu_custom_call" | custom-call | tf_op jit(solution)/shard_map/pallas_call | solution.py:42
  170.1 9.8 %shard_map.356 = (f32[1,128]{1,0:T(1,128)}, bf16[64,1024]{1,0:T(8,128)(2,1)}, bf16[64,1024]{1,0:T(8,128)(2,1)}) custom-call(s32[1]{0:T(128)} %constant.117.clone.1._, f32[192,1024]{1,0:T(8,128)} %shard_map.348.q, bf16[576,2048]{1,0:T(8,128)(2,1)} %shard_map.349.k.v, bf16[576,2048]{1,0:T(8,128)(2,1)} %shard_map.349.k.v, bf16[64,2048]{1,0:T(8,128)(2,1)} %shard_map.355.ck.cv, ...), custom_call_target="tpu_custom_call" | custom-call | tf_op jit(solution)/shard_map/pallas_call | solution.py:42
  179.8 5.2 %shard_map.360 = (bf16[64,1024]{1,0:T(8,128)(2,1)}, f32[1,1024]{1,0:T(1,128)}) custom-call(s32[3]{0:T(128)} %pad_add_fusion.s, bf16[64,1024]{1,0:T(8,128)(2,1)} %get-tuple-element.75.dck, bf16[64,1024]{1,0:T(8,128)(2,1)} %get-tuple-element.76.dcv, bf16[512,2048]{1,0:T(8,128)(2,1)} %w0.7, bf16[256,2048]{1,0:T(8,128)(2,1)} %copy-done.1, ...), custom_call_target="tpu_custom_call" | custom-call | tf_op jit(solution)/shard_map/pallas_call | solution.py:42
  185.6 5.8 %shard_map.363 = bf16[2,2,128,1024]{3,2,1,0:T(8,128)(2,1)} custom-call(s32[3]{0:T(128)} %add_add_fusion.2.s, bf16[576,1024]{1,0:T(8,128)(2,1)} %get-tuple-element.52.x_ref.refs_0_, bf16[576,1024]{1,0:T(8,128)(2,1)} %copy-done, bf16[192,1024]{1,0:T(8,128)(2,1)} %get-tuple-element.65.dq.refs_2_, bf16[192,1024]{1,0:T(8,128)(2,1)} %copy-done.24, ...), custom_call_target="tpu_custom_call" | custom-call | tf_op jit(solution)/shard_map/pallas_call | solution.py:42
  206.4 6.3 %shard_map.361 = bf16[2,2,128,1024]{3,2,1,0:T(8,128)(2,1)} custom-call(s32[3]{0:T(128)} %add_add_fusion.s, bf16[576,1024]{1,0:T(8,128)(2,1)} %get-tuple-element.52.x_ref.refs_0_, bf16[576,1024]{1,0:T(8,128)(2,1)} %copy-done, bf16[576,1024]{1,0:T(8,128)(2,1)} %get-tuple-element.85.refs_2_, bf16[576,1024]{1,0:T(8,128)(2,1)} %collective-permute-done.20.refs_3_), custom_call_target="tpu_custom_call" | custom-call | tf_op jit(solution)/shard_map/pallas_call | solution.py:42
  218.7 4.9 %collective-permute-done.22 = bf16[2,128,1024]{2,1,0:T(8,128)(2,1)S(1)} collective-permute-done((bf16[2,128,1024]{2,1,0:T(8,128)(2,1)S(1)}, bf16[2,128,1024]{2,1,0:T(8,128)(2,1)S(1)}, u32[]{:S(2)}, u32[]{:S(2)}) %collective-permute-start.22) | collective-permute-done | bytes 524320 | tf_op jit(solution)/shard_map/ppermute | solution.py:587
  236.3 8.9 %collective-permute-done.24 = bf16[2,32,1024]{2,1,0:T(8,128)(2,1)S(1)} collective-permute-done((bf16[2,32,1024]{2,1,0:T(8,128)(2,1)S(1)}, bf16[2,32,1024]{2,1,0:T(8,128)(2,1)S(1)}, u32[]{:S(2)}, u32[]{:S(2)}) %collective-permute-start.24) | collective-permute-done | bytes 131104 | tf_op jit(solution)/shard_map/ppermute | solution.py:587
  251.9 5.5 %shard_map.371 = bf16[2,2,128,2048]{3,2,1,0:T(8,128)(2,1)} custom-call(s32[3]{0:T(128)} %add_add_fusion.3.s, bf16[192,1024]{1,0:T(8,128)(2,1)} %get-tuple-element.54.n2.refs_0_, bf16[192,1024]{1,0:T(8,128)(2,1)} %copy-done.25, bf16[192,4096]{1,0:T(8,128)(2,1)} %get-tuple-element.81.refs_2_, bf16[192,4096]{1,0:T(8,128)(2,1)} %copy-done.9), custom_call_target="tpu_custom_call" | custom-call | tf_op jit(solution)/shard_map/pallas_call | solution.py:42
  279.1 5.5 %shard_map.369 = bf16[2,2,512,512]{3,2,1,0:T(8,128)(2,1)} custom-call(s32[3]{0:T(128)} %add_add_fusion.1.s, bf16[192,4096]{1,0:T(8,128)(2,1)} %get-tuple-element.80.refs_0_, bf16[192,4096]{1,0:T(8,128)(2,1)} %collective-permute-done.33.refs_1_, bf16[192,1024]{1,0:T(8,128)(2,1)} %bitcast.283, bf16[192,1024]{1,0:T(8,128)(2,1)} %copy-done.26), custom_call_target="tpu_custom_call" | custom-call | tf_op jit(solution)/shard_map/pallas_call | solution.py:42
  292.6 5.5 %shard_map.370 = bf16[2,2,128,2048]{3,2,1,0:T(8,128)(2,1)} custom-call(s32[3]{0:T(128)} %add_add_fusion.2.s, bf16[192,1024]{1,0:T(8,128)(2,1)} %get-tuple-element.54.n2.refs_0_, bf16[192,1024]{1,0:T(8,128)(2,1)} %copy-done.25, bf16[192,4096]{1,0:T(8,128)(2,1)} %get-tuple-element.81.refs_2_, bf16[192,4096]{1,0:T(8,128)(2,1)} %copy-done.9), custom_call_target="tpu_custom_call" | custom-call | tf_op jit(solution)/shard_map/pallas_call | solution.py:42
  303.5 7.0 %collective-permute-done.55 = bf16[2,2,32,512]{3,2,1,0:T(8,128)(2,1)S(1)} collective-permute-done((bf16[2,2,32,512]{3,2,1,0:T(8,128)(2,1)S(1)}, bf16[2,2,32,512]{3,2,1,0:T(8,128)(2,1)S(1)}, u32[]{:S(2)}, u32[]{:S(2)}) %collective-permute-start.55) | collective-permute-done | bytes 131104 | tf_op jit(solution)/shard_map/ppermute | solution.py:587
  311.0 5.6 %shard_map.368 = bf16[2,2,512,512]{3,2,1,0:T(8,128)(2,1)} custom-call(s32[3]{0:T(128)} %add_add_fusion.s, bf16[192,4096]{1,0:T(8,128)(2,1)} %get-tuple-element.80.refs_0_, bf16[192,4096]{1,0:T(8,128)(2,1)} %collective-permute-done.33.refs_1_, bf16[192,1024]{1,0:T(8,128)(2,1)} %bitcast.284, bf16[192,1024]{1,0:T(8,128)(2,1)} %copy-done.26), custom_call_target="tpu_custom_call" | custom-call | tf_op jit(solution)/shard_map/pallas_call | solution.py:42
  316.5 7.7 %collective-permute-done.35 = bf16[2,2,512,512]{3,2,1,0:T(8,128)(2,1)S(1)} collective-permute-done((bf16[2,2,512,512]{3,2,1,0:T(8,128)(2,1)}, bf16[2,2,512,512]{3,2,1,0:T(8,128)(2,1)S(1)}, u32[]{:S(2)}, u32[]{:S(2)}) %collective-permute-start.35) | collective-permute-done | bytes 2097184 | tf_op jit(solution)/shard_map/ppermute | solution.py:587
  328.8 16.6 %collective-permute-done.36 = bf16[2,512,512]{2,1,0:T(8,128)(2,1)S(1)} collective-permute-done((bf16[2,512,512]{2,1,0:T(8,128)(2,1)S(1)}, bf16[2,512,512]{2,1,0:T(8,128)(2,1)S(1)}, u32[]{:S(2)}, u32[]{:S(2)}) %collective-permute-start.36) | collective-permute-done | bytes 1048608 | tf_op jit(solution)/shard_map/ppermute | solution.py:587
  348.3 7.1 %collective-permute-done.37 = bf16[2,2,128,512]{3,2,1,0:T(8,128)(2,1)S(1)} collective-permute-done((bf16[2,2,128,512]{3,2,1,0:T(8,128)(2,1)S(1)}, bf16[2,2,128,512]{3,2,1,0:T(8,128)(2,1)S(1)}, u32[]{:S(2)}, u32[]{:S(2)}) %collective-permute-start.37) | collective-permute-done | bytes 524320 | tf_op jit(solution)/shard_map/ppermute | solution.py:587
  355.8 5.1 %collective-permute-done.38 = bf16[2,128,512]{2,1,0:T(8,128)(2,1)S(1)} collective-permute-done((bf16[2,128,512]{2,1,0:T(8,128)(2,1)S(1)}, bf16[2,128,512]{2,1,0:T(8,128)(2,1)S(1)}, u32[]{:S(2)}, u32[]{:S(2)}) %collective-permute-start.38) | collective-permute-done | bytes 262176 | tf_op jit(solution)/shard_map/ppermute | solution.py:587
  363.0 6.0 %collective-permute-done.57 = bf16[384,512]{1,0:T(8,128)(2,1)S(1)} collective-permute-done((bf16[384,512]{1,0:T(8,128)(2,1)S(1)}, bf16[384,512]{1,0:T(8,128)(2,1)S(1)}, u32[]{:S(2)}, u32[]{:S(2)}) %collective-permute-start.57) | collective-permute-done | bytes 393248 | tf_op jit(solution)/shard_map/ppermute | solution.py:587
  370.5 8.0 %collective-permute-done.58 = bf16[384,512]{1,0:T(8,128)(2,1)S(1)} collective-permute-done((bf16[384,512]{1,0:T(8,128)(2,1)S(1)}, bf16[384,512]{1,0:T(8,128)(2,1)S(1)}, u32[]{:S(2)}, u32[]{:S(2)}) %collective-permute-start.58) | collective-permute-done | bytes 393248 | tf_op jit(solution)/shard_map/ppermute | solution.py:715
  379.4 13.0 %shard_map.359 = (f32[192,1024]{1,0:T(8,128)}, f32[1,1024]{1,0:T(1,128)}, f32[1,1024]{1,0:T(1,128)}) custom-call(s32[3]{0:T(128)} %pad_add_fusion.s, bf16[2,576,1024]{2,1,0:T(8,128)(2,1)} %get-tuple-element.64.dkv, bf16[192,1024]{1,0:T(8,128)(2,1)} %get-tuple-element.65.dq.refs_2_, bf16[512,2048]{1,0:T(8,128)(2,1)} %w0.7, bf16[256,2048]{1,0:T(8,128)(2,1)} %copy-done.1, ...), custom_call_target="tpu_custom_call" | custom-call | tf_op jit(solution)/shard_map/pallas_call | solution.py:42
  435.0 11.2 %all-gather.11.cloned.1.call-done = bf16[12288,512]{1,0:T(8,128)(2,1)} async-done(((bf16[384,512]{1,0:T(8,128)(2,1)}), bf16[12288,512]{1,0:T(8,128)(2,1)}) %all-gather.11.cloned.1.call-update) | async-done | bytes 12582928 | tf_op jit(solution)/shard_map/all_gather | solution.py:717
  448.6 5.8 %shard_map.379 = f32[16,96,1024]{2,1,0:T(8,128)} custom-call(s32[1]{0:T(128)} %constant.117.clone.1._, bf16[32,384,512]{2,1,0:T(8,128)(2,1)} %bitcast.264), custom_call_target="tpu_custom_call" | custom-call | tf_op jit(solution)/shard_map/pallas_call | solution.py:42
  454.3 7.3 %shard_map.378 = f32[16,128,1024]{2,1,0:T(8,128)} custom-call(s32[1]{0:T(128)} %constant.117.clone.1._, bf16[32,384,512]{2,1,0:T(8,128)(2,1)} %bitcast.265), custom_call_target="tpu_custom_call" | custom-call | tf_op jit(solution)/shard_map/pallas_call | solution.py:42
  461.7 7.3 %shard_map.377 = f32[16,32,4096]{2,1,0:T(8,128)} custom-call(s32[1]{0:T(128)} %constant.117.clone.1._, bf16[32,384,512]{2,1,0:T(8,128)(2,1)} %bitcast.266), custom_call_target="tpu_custom_call" | custom-call | tf_op jit(solution)/shard_map/pallas_call | solution.py:42
  (345 shorter events, 214.7 us)
Async XLA Ops:
  7.3 86.5 %all-gather.7.cloned.1.call-start = ((), (), s32[]{:S(2)}) async-start(), calls=%async_computation | async-start | bytes 8650752 | tf_op jit(solution)/shard_map/all_gather | solution.py:677
  20.0 405.8 %all-gather.9.cloned.1.call-start = ((), (), s32[]{:S(2)}) async-start(), calls=%async_computation.1 | async-start | bytes 4325376 | tf_op jit(solution)/shard_map/all_gather | solution.py:717
  22.4 15.4 %collective-permute-start.3 = (bf16[256,2048]{1,0:T(8,128)(2,1)}, bf16[256,2048]{1,0:T(8,128)(2,1)S(1)}, u32[]{:S(2)}, u32[]{:S(2)}) collective-permute-start(bf16[256,2048]{1,0:T(8,128)(2,1)} %constant_dynamic-slice_fusion.5), channel_id=1, source_target_pairs={{0,1},{2,67},{1,0},{3,66},{64,65},{66,3},{65,64},{67,2},{4,5},{6,7... | collective-permute-start | bytes 3145736 | tf_op jit(solution)/shard_map/ppermute | solution.py:587
  28.1 19.8 %collective-permute-start.7 = (bf16[256,1024]{1,0:T(8,128)(2,1)}, bf16[256,1024]{1,0:T(8,128)(2,1)}, u32[]{:S(2)}, u32[]{:S(2)}) collective-permute-start(bf16[256,1024]{1,0:T(8,128)(2,1)} %constant_dynamic-slice_fusion.3), channel_id=1, source_target_pairs={{0,1},{2,67},{1,0},{3,66},{64,65},{66,3},{65,64},{67,2},{4,5},{6,7... | collective-permute-start | bytes 1572872 | tf_op jit(solution)/shard_map/ppermute | solution.py:587
  29.5 19.6 %collective-permute-start.1 = (bf16[256,1024]{1,0:T(8,128)(2,1)}, bf16[256,1024]{1,0:T(8,128)(2,1)}, u32[]{:S(2)}, u32[]{:S(2)}) collective-permute-start(bf16[256,1024]{1,0:T(8,128)(2,1)} %constant_dynamic-slice_fusion.6), channel_id=1, source_target_pairs={{0,1},{2,67},{1,0},{3,66},{64,65},{66,3},{65,64},{67,2},{4,5},{6,7... | collective-permute-start | bytes 1572872 | tf_op jit(solution)/shard_map/ppermute | solution.py:587
  32.4 22.3 %collective-permute-start.5 = (bf16[256,1024]{1,0:T(8,128)(2,1)}, bf16[256,1024]{1,0:T(8,128)(2,1)}, u32[]{:S(2)}, u32[]{:S(2)}) collective-permute-start(bf16[256,1024]{1,0:T(8,128)(2,1)} %constant_dynamic-slice_fusion.4), channel_id=1, source_target_pairs={{0,1},{2,67},{1,0},{3,66},{64,65},{66,3},{65,64},{67,2},{4,5},{6,7... | collective-permute-start | bytes 1572872 | tf_op jit(solution)/shard_map/ppermute | solution.py:587
  37.8 34.0 %collective-permute-start.4 = (bf16[256,2048]{1,0:T(8,128)(2,1)S(1)}, bf16[256,2048]{1,0:T(8,128)(2,1)S(1)}, u32[]{:S(2)}, u32[]{:S(2)}) collective-permute-start(bf16[256,2048]{1,0:T(8,128)(2,1)S(1)} %collective-permute-done.3.refs_1_.k1.w1), channel_id=1, source_target_pairs={{0,2},{2,0},{1,3},{3,1},{4,6},{6,4},{5,7},{7,5},{8,10},{10,8},{9,1... | collective-permute-start | bytes 3145736 | tf_op jit(solution)/shard_map/ppermute | solution.py:575
  39.2 93.7 %collective-permute-start.10 = (bf16[768,1024]{1,0:T(8,128)(2,1)}, bf16[768,1024]{1,0:T(8,128)(2,1)}, u32[]{:S(2)}, u32[]{:S(2)}) collective-permute-start(bf16[768,1024]{1,0:T(8,128)(2,1)} %constant_dynamic-slice_fusion.2), channel_id=1, source_target_pairs={{0,1},{2,67},{1,0},{3,66},{64,65},{66,3},{65,64},{67,2},{4,5},{6,7... | collective-permute-start | bytes 4718600 | tf_op jit(solution)/shard_map/ppermute | solution.py:587
  47.9 41.0 %collective-permute-start.8 = (bf16[256,1024]{1,0:T(8,128)(2,1)}, bf16[256,1024]{1,0:T(8,128)(2,1)S(1)}, u32[]{:S(2)}, u32[]{:S(2)}) collective-permute-start(bf16[256,1024]{1,0:T(8,128)(2,1)} %collective-permute-done.7.w1), channel_id=1, source_target_pairs={{0,2},{2,0},{1,3},{3,1},{4,6},{6,4},{5,7},{7,5},{8,10},{10,8},{9,1... | collective-permute-start | bytes 1572872 | tf_op jit(solution)/shard_map/ppermute | solution.py:575
  61.7 72.4 %collective-permute-start.19 = (bf16[576,1024]{1,0:T(8,128)(2,1)}, bf16[576,1024]{1,0:T(8,128)(2,1)S(1)}, u32[]{:S(2)}, u32[]{:S(2)}) collective-permute-start(bf16[576,1024]{1,0:T(8,128)(2,1)} %get-tuple-element.52.x_ref.refs_0_), channel_id=1, source_target_pairs={{0,2},{2,0},{1,3},{3,1},{4,6},{6,4},{5,7},{7,5},{8,10},{10,8},{9,1... | collective-permute-start | bytes 3538952 | tf_op jit(solution)/shard_map/ppermute | solution.py:575
  132.5 16.0 %collective-permute-start.20 = (bf16[576,1024]{1,0:T(8,128)(2,1)}, bf16[576,1024]{1,0:T(8,128)(2,1)}, u32[]{:S(2)}, u32[]{:S(2)}) collective-permute-start(bf16[576,1024]{1,0:T(8,128)(2,1)} %get-tuple-element.84), channel_id=1, source_target_pairs={{0,2},{2,0},{1,3},{3,1},{4,6},{6,4},{5,7},{7,5},{8,10},{10,8},{9,1... | collective-permute-start | bytes 3538952 | tf_op jit(solution)/shard_map/ppermute | solution.py:575
  132.9 26.0 %collective-permute-start.11 = (bf16[768,1024]{1,0:T(8,128)(2,1)}, bf16[768,1024]{1,0:T(8,128)(2,1)}, u32[]{:S(2)}, u32[]{:S(2)}) collective-permute-start(bf16[768,1024]{1,0:T(8,128)(2,1)} %collective-permute-done.10.w1), channel_id=1, source_target_pairs={{0,2},{2,0},{1,3},{3,1},{4,6},{6,4},{5,7},{7,5},{8,10},{10,8},{9,1... | collective-permute-start | bytes 4718600 | tf_op jit(solution)/shard_map/ppermute | solution.py:575
  144.0 47.4 %collective-permute-start.27 = (bf16[2,2,128,1024]{3,2,1,0:T(8,128)(2,1)}, bf16[2,2,128,1024]{3,2,1,0:T(8,128)(2,1)S(1)}, u32[]{:S(2)}, u32[]{:S(2)}) collective-permute-start(bf16[2,2,128,1024]{3,2,1,0:T(8,128)(2,1)} %shard_map.364), channel_id=1, source_target_pairs={{0,4},{2,14},{4,0},{6,10},{8,12},{10,6},{12,8},{14,2},{1,5},{3,15}... | collective-permute-start | bytes 3145736 | tf_op jit(solution)/shard_map/ppermute | solution.py:587
  154.8 57.9 %collective-permute-start.21 = (bf16[2,2,128,1024]{3,2,1,0:T(8,128)(2,1)}, bf16[2,2,128,1024]{3,2,1,0:T(8,128)(2,1)}, u32[]{:S(2)}, u32[]{:S(2)}) collective-permute-start(bf16[2,2,128,1024]{3,2,1,0:T(8,128)(2,1)} %shard_map.362), channel_id=1, source_target_pairs={{0,16},{2,50},{16,0},{18,34},{32,48},{34,18},{48,32},{50,2},{1,17}... | collective-permute-start | bytes 3145736 | tf_op jit(solution)/shard_map/ppermute | solution.py:587
  157.5 36.4 %collective-permute-start.45 = (bf16[64,3072]{1,0:T(8,128)(2,1)S(1)}, bf16[64,3072]{1,0:T(8,128)(2,1)S(1)}, u32[]{:S(2)}, u32[]{:S(2)}) collective-permute-start(bf16[64,3072]{1,0:T(8,128)(2,1)S(1)} %copy-done.17), channel_id=1, source_target_pairs={{0,2},{2,0},{1,3},{3,1},{4,6},{6,4},{5,7},{7,5},{8,10},{10,8},{9,1... | collective-permute-start | bytes 1179656 | tf_op jit(solution)/shard_map/ppermute | solution.py:575
  193.8 20.6 %collective-permute-start.28 = (bf16[2,128,1024]{2,1,0:T(8,128)(2,1)}, bf16[2,128,1024]{2,1,0:T(8,128)(2,1)}, u32[]{:S(2)}, u32[]{:S(2)}) collective-permute-start(bf16[2,128,1024]{2,1,0:T(8,128)(2,1)} %fusion.7), channel_id=1, source_target_pairs={{0,12},{2,6},{4,8},{6,2},{8,4},{10,14},{12,0},{14,10},{1,13},{3,7}... | collective-permute-start | bytes 1572872 | tf_op jit(solution)/shard_map/ppermute | solution.py:587
  199.9 28.6 %collective-permute-start.47 = (bf16[2,2,384,512]{3,2,1,0:T(8,128)(2,1)}, bf16[2,2,384,512]{3,2,1,0:T(8,128)(2,1)S(1)}, u32[]{:S(2)}, u32[]{:S(2)}) collective-permute-start(bf16[2,2,384,512]{3,2,1,0:T(8,128)(2,1)} %shard_map.373), channel_id=1, source_target_pairs={{0,4},{2,14},{4,0},{6,10},{8,12},{10,6},{12,8},{14,2},{1,5},{3,15}... | collective-permute-start | bytes 4718600 | tf_op jit(solution)/shard_map/ppermute | solution.py:587
  201.1 48.9 %collective-permute-start.39 = (bf16[192,1024]{1,0:T(8,128)(2,1)}, bf16[192,1024]{1,0:T(8,128)(2,1)S(1)}, u32[]{:S(2)}, u32[]{:S(2)}) collective-permute-start(bf16[192,1024]{1,0:T(8,128)(2,1)} %get-tuple-element.54.n2.refs_0_), channel_id=1, source_target_pairs={{0,2},{2,0},{1,3},{3,1},{4,6},{6,4},{5,7},{7,5},{8,10},{10,8},{9,1... | collective-permute-start | bytes 1179656 | tf_op jit(solution)/shard_map/ppermute | solution.py:575
  206.3 43.7 %collective-permute-start.40 = (bf16[192,4096]{1,0:T(8,128)(2,1)S(1)}, bf16[192,4096]{1,0:T(8,128)(2,1)S(1)}, u32[]{:S(2)}, u32[]{:S(2)}) collective-permute-start(bf16[192,4096]{1,0:T(8,128)(2,1)S(1)} %copy-done.8), channel_id=1, source_target_pairs={{0,2},{2,0},{1,3},{3,1},{4,6},{6,4},{5,7},{7,5},{8,10},{10,8},{9,1... | collective-permute-start | bytes 4718600 | tf_op jit(solution)/shard_map/ppermute | solution.py:575
  216.0 15.9 %collective-permute-start.29 = (bf16[2,2,32,1024]{3,2,1,0:T(8,128)(2,1)S(1)}, bf16[2,2,32,1024]{3,2,1,0:T(8,128)(2,1)S(1)}, u32[]{:S(2)}, u32[]{:S(2)}) collective-permute-start(bf16[2,2,32,1024]{3,2,1,0:T(8,128)(2,1)S(1)} %pad_maximum_fusion.6), channel_id=1, source_target_pairs={{0,16},{2,50},{16,0},{18,34},{32,48},{34,18},{48,32},{50,2},{1,17}... | collective-permute-start | bytes 786440 | tf_op jit(solution)/shard_map/ppermute | solution.py:587
  230.8 37.2 %collective-permute-start.48 = (bf16[2,384,512]{2,1,0:T(8,128)(2,1)}, bf16[2,384,512]{2,1,0:T(8,128)(2,1)}, u32[]{:S(2)}, u32[]{:S(2)}) collective-permute-start(bf16[2,384,512]{2,1,0:T(8,128)(2,1)} %fusion.4), channel_id=1, source_target_pairs={{0,12},{2,6},{4,8},{6,2},{8,4},{10,14},{12,0},{14,10},{1,13},{3,7}... | collective-permute-start | bytes 2359304 | tf_op jit(solution)/shard_map/ppermute | solution.py:587
  246.0 14.2 %collective-permute-start.31 = (bf16[128,512]{1,0:T(8,128)(2,1)}, bf16[128,512]{1,0:T(8,128)(2,1)}, u32[]{:S(2)}, u32[]{:S(2)}) collective-permute-start(bf16[128,512]{1,0:T(8,128)(2,1)} %fusion.36), channel_id=1, source_target_pairs={{0,1},{2,67},{1,0},{3,66},{64,65},{66,3},{65,64},{67,2},{4,5},{6,7... | collective-permute-start | bytes 393224 | tf_op jit(solution)/shard_map/ppermute | solution.py:587
  248.6 29.7 %collective-permute-start.33 = (bf16[192,4096]{1,0:T(8,128)(2,1)S(1)}, bf16[192,4096]{1,0:T(8,128)(2,1)}, u32[]{:S(2)}, u32[]{:S(2)}) collective-permute-start(bf16[192,4096]{1,0:T(8,128)(2,1)S(1)} %copy-done.7), channel_id=1, source_target_pairs={{0,2},{2,0},{1,3},{3,1},{4,6},{6,4},{5,7},{7,5},{8,10},{10,8},{9,1... | collective-permute-start | bytes 4718600 | tf_op jit(solution)/shard_map/ppermute | solution.py:575
  257.4 40.7 %collective-permute-start.41 = (bf16[2,2,128,2048]{3,2,1,0:T(8,128)(2,1)}, bf16[2,2,128,2048]{3,2,1,0:T(8,128)(2,1)}, u32[]{:S(2)}, u32[]{:S(2)}) collective-permute-start(bf16[2,2,128,2048]{3,2,1,0:T(8,128)(2,1)} %shard_map.371), channel_id=1, source_target_pairs={{0,4},{2,14},{4,0},{6,10},{8,12},{10,6},{12,8},{14,2},{1,5},{3,15}... | collective-permute-start | bytes 6291464 | tf_op jit(solution)/shard_map/ppermute | solution.py:587
  267.3 178.8 %all-gather.11.cloned.1.call-start = ((), (), s32[]{:S(2)}) async-start(), calls=%async_computation.2 | async-start | bytes 12976128 | tf_op jit(solution)/shard_map/all_gather | solution.py:717
  270.1 15.2 %collective-permute-start.49 = (bf16[2,2,96,512]{3,2,1,0:T(8,128)(2,1)S(1)}, bf16[2,2,96,512]{3,2,1,0:T(8,128)(2,1)S(1)}, u32[]{:S(2)}, u32[]{:S(2)}) collective-permute-start(bf16[2,2,96,512]{3,2,1,0:T(8,128)(2,1)S(1)} %pad_maximum_fusion.4), channel_id=1, source_target_pairs={{0,16},{2,50},{16,0},{18,34},{32,48},{34,18},{48,32},{50,2},{1,17}... | collective-permute-start | bytes 1179656 | tf_op jit(solution)/shard_map/ppermute | solution.py:587
  284.6 39.6 %collective-permute-start.35 = (bf16[2,2,512,512]{3,2,1,0:T(8,128)(2,1)}, bf16[2,2,512,512]{3,2,1,0:T(8,128)(2,1)S(1)}, u32[]{:S(2)}, u32[]{:S(2)}) collective-permute-start(bf16[2,2,512,512]{3,2,1,0:T(8,128)(2,1)} %shard_map.369), channel_id=1, source_target_pairs={{0,16},{2,50},{16,0},{18,34},{32,48},{34,18},{48,32},{50,2},{1,17}... | collective-permute-start | bytes 6291464 | tf_op jit(solution)/shard_map/ppermute | solution.py:587
  285.4 18.1 %collective-permute-start.50 = (bf16[2,96,512]{2,1,0:T(8,128)(2,1)S(1)}, bf16[2,96,512]{2,1,0:T(8,128)(2,1)S(1)}, u32[]{:S(2)}, u32[]{:S(2)}) collective-permute-start(bf16[2,96,512]{2,1,0:T(8,128)(2,1)S(1)} %fusion.13), channel_id=1, source_target_pairs={{0,48},{2,18},{16,32},{18,2},{32,16},{34,50},{48,0},{50,34},{1,49}... | collective-permute-start | bytes 589832 | tf_op jit(solution)/shard_map/ppermute | solution.py:587
  300.2 25.7 %collective-permute-start.42 = (bf16[2,128,2048]{2,1,0:T(8,128)(2,1)S(1)}, bf16[2,128,2048]{2,1,0:T(8,128)(2,1)S(1)}, u32[]{:S(2)}, u32[]{:S(2)}) collective-permute-start(bf16[2,128,2048]{2,1,0:T(8,128)(2,1)S(1)} %fusion.3), channel_id=1, source_target_pairs={{0,12},{2,6},{4,8},{6,2},{8,4},{10,14},{12,0},{14,10},{1,13},{3,7}... | collective-permute-start | bytes 3145736 | tf_op jit(solution)/shard_map/ppermute | solution.py:587
  310.6 37.7 %collective-permute-start.56 = (bf16[2,32,512]{2,1,0:T(8,128)(2,1)S(1)}, bf16[2,32,512]{2,1,0:T(8,128)(2,1)S(1)}, u32[]{:S(2)}, u32[]{:S(2)}) collective-permute-start(bf16[2,32,512]{2,1,0:T(8,128)(2,1)S(1)} %fusion.37), channel_id=1, source_target_pairs={{0,12},{2,6},{4,8},{6,2},{8,4},{10,14},{12,0},{14,10},{1,13},{3,7}... | collective-permute-start | bytes 196616 | tf_op jit(solution)/shard_map/ppermute | solution.py:587
  325.8 19.6 %collective-permute-start.36 = (bf16[2,512,512]{2,1,0:T(8,128)(2,1)S(1)}, bf16[2,512,512]{2,1,0:T(8,128)(2,1)S(1)}, u32[]{:S(2)}, u32[]{:S(2)}) collective-permute-start(bf16[2,512,512]{2,1,0:T(8,128)(2,1)S(1)} %fusion.2), channel_id=1, source_target_pairs={{0,48},{2,18},{16,32},{18,2},{32,16},{34,50},{48,0},{50,34},{1,49}... | collective-permute-start | bytes 3145736 | tf_op jit(solution)/shard_map/ppermute | solution.py:587
  327.8 20.3 %collective-permute-start.43 = (bf16[2,2,32,2048]{3,2,1,0:T(8,128)(2,1)S(1)}, bf16[2,2,32,2048]{3,2,1,0:T(8,128)(2,1)S(1)}, u32[]{:S(2)}, u32[]{:S(2)}) collective-permute-start(bf16[2,2,32,2048]{3,2,1,0:T(8,128)(2,1)S(1)} %pad_maximum_fusion.3), channel_id=1, source_target_pairs={{0,16},{2,50},{16,0},{18,34},{32,48},{34,18},{48,32},{50,2},{1,17}... | collective-permute-start | bytes 1572872 | tf_op jit(solution)/shard_map/ppermute | solution.py:587
  (87 other events, 862.1 us)
Sparse Core Ops, SparseCore 0:
  20.2 56.9 all-gather.6
  267.5 47.9 all-gather.8
  379.4 66.6 all-gather.10

commit v3 on v2

--- a/solution.py
+++ b/solution.py
@@ -38,7 +38,32 @@
     return lax.dot_general(a, b, (((0,), (0,)), ((), ())), preferred_element_type=f32)
 
 
+class Line:
+    def __init__(self):
+        self.held = []
+
+    def hold(self, *values):
+        self.held += values
+
+    def later(self, value):
+        return lax.optimization_barrier((value, *self.held))[0] if self.held else value
+
+    def ran(self, value):
+        self.held = [value]
+
+
+line = Line()
+
+
 def call(kernel, out, grid, in_specs, out_specs, scalars, args, scratch=()):
+    result = run_kernel(
+        kernel, out, grid, in_specs, out_specs, line.later(scalars), args, scratch
+    )
+    line.ran(jax.tree.leaves(result)[0])
+    return result
+
+
+def run_kernel(kernel, out, grid, in_specs, out_specs, scalars, args, scratch):
     return pl.pallas_call(
         kernel,
         out_shape=out,
@@ -86,8 +111,8 @@
     return e / jnp.sum(e, axis=-1, keepdims=True)
 
 
-def first_norm(compressed, memory, tokens, g, b, none):
-    def kernel(_, comp, mem, tok, g, b, out, old):
+def first_norm(compressed, memory, tokens, g, b, offsets):
+    def kernel(s, comp, mem, tok, g, b, out, out_rel, old):
         gain, bias = g[...], b[...]
 
         def part(ref, base):
@@ -98,6 +123,10 @@
         part(comp, 0)
         part(mem, T)
         part(tok, 2 * T)
+        start = 0
+        for i, width in enumerate((D // 2, D // 4, D // 4)):
+            out_rel[:, start : start + width] = out[:, pl.ds(at(s[i]), width)]
+            start += width
         row = lax.broadcasted_iota(jnp.int32, (T // 3, T), 0)
         col = lax.broadcasted_iota(jnp.int32, (T // 3, T), 1)
         low = mem[...].astype(bf16)
@@ -106,64 +135,55 @@
             old[:, tap * D : (tap + 1) * D] = dot(take, low).astype(bf16)
 
     args = (compressed, memory, tokens, g, b)
-    out = (shape((KEYS, D), bf16), shape((T // 3, 3 * D), bf16))
-    return call(
-        kernel, out, (1,), [whole(a) for a in args], [whole(o) for o in out], none, args
-    )
-
-
-def project(x, pieces, offsets, block, dtype, rows=None, row_block=0):
-    rows = rows or x.shape[0]
-    depth, n = x.shape[1], pieces[0].shape[1]
-
-    def kernel(s, x_ref, *refs):
-        total = None
-        for i, w in enumerate(refs[:-1]):
-            part = dot(x_ref[:, pl.ds(at(s[i]), w.shape[0])], w[...])
-            total = part if total is None else total + part
-        refs[-1][...] = total.astype(dtype)
-
-    return call(
-        kernel,
-        shape((rows, n), dtype),
-        (n // block,),
-        [pl.BlockSpec((rows, depth), lambda j, s: (row_block, 0))]
-        + [pl.BlockSpec((w.shape[0], block), lambda j, s: (0, j)) for w in pieces],
-        pl.BlockSpec((rows, block), lambda j, s: (0, j)),
-        offsets,
-        (x, *pieces),
-    )
+    out = (shape((KEYS, D), bf16), shape((KEYS, D), bf16), shape((T // 3, 3 * D), bf16))
+    return call(
+        kernel, out, (1,), [whole(a) for a in args], [whole(o) for o in out], offsets, args
+    )
+
+
+PAIR = 2
+STEPS = H // PAIR
 
 
 def head(rows, row_block=0, first=0):
-    return pl.BlockSpec((rows, HD), lambda h, s: (row_block, first + h))
+    return pl.BlockSpec((rows, PAIR * HD), lambda h, s: (row_block, first // PAIR + h))
 
 
 def vec_head():
-    return pl.BlockSpec((1, HD), lambda h, s: (0, h))
+    return pl.BlockSpec((1, PAIR * HD), lambda h, s: (0, h))
+
+
+def each_head(body):
+    for i in range(PAIR):
+        body(i, slice(i * HD, (i + 1) * HD))
 
 
 def attend(queries, key_value, relative, bias_u, bias_v, none):
     def kernel(_, q, k, v, rel, bu, bv, probs, out):
         pad = jnp.zeros((PAD - KEYS, HD), bf16)
-        content = ((q[...] + bu[...]) * FACTOR).astype(bf16)
-        located = ((q[...] + bv[...]) * FACTOR).astype(bf16)
-        raw = dot_t(located, jnp.concatenate([rel[...], pad], axis=0))
-        raw = pltpu.roll(raw, PAD - T + 1, 1, stride=1, stride_axis=0)
-        s = dot_t(content, jnp.concatenate([k[...], pad], axis=0)) + raw
         row = lax.broadcasted_iota(jnp.int32, (T, PAD), 0)
         col = lax.broadcasted_iota(jnp.int32, (T, PAD), 1)
-        p = softmax(jnp.where(col <= row + (KEYS - T), s, -1e30))
-        probs[0] = p
-        low = p.astype(bf16)
-        out[...] = dot(low, jnp.concatenate([v[...], pad], axis=0)).astype(bf16)
+        seen = col <= row + (KEYS - T)
+
+        def body(i, cut):
+            content = ((q[:, cut] + bu[:, cut]) * FACTOR).astype(bf16)
+            located = ((q[:, cut] + bv[:, cut]) * FACTOR).astype(bf16)
+            raw = dot_t(located, jnp.concatenate([rel[:, cut], pad], axis=0))
+            raw = pltpu.roll(raw, PAD - T + 1, 1, stride=1, stride_axis=0)
+            s = dot_t(content, jnp.concatenate([k[:, cut], pad], axis=0)) + raw
+            p = softmax(jnp.where(seen, s, -1e30))
+            probs[i] = p
+            low = p.astype(bf16)
+            out[:, cut] = dot(low, jnp.concatenate([v[:, cut], pad], axis=0)).astype(bf16)
+
+        each_head(body)
 
     return call(
         kernel,
         (shape((H, T, PAD), f32), shape((T, D), bf16)),
-        (H,),
+        (STEPS,),
         [head(T), head(KEYS), head(KEYS, 0, H), head(KEYS), vec_head(), vec_head()],
-        [pl.BlockSpec((1, T, PAD), lambda h, s: (h, 0, 0)), head(T)],
+        [pl.BlockSpec((PAIR, T, PAD), lambda h, s: (h, 0, 0)), head(T)],
         none,
         (queries, key_value, key_value, relative, bias_u, bias_v),
     )
@@ -172,24 +192,28 @@
 def attend_back(queries, key_value, relative, bias_u, bias_v, probs, d_attended, none):
     def kernel(_, q, k, v, rel, bu, bv, probs, d_att, d_kv, d_rel, d_q, d_bu, d_bv):
         pad = jnp.zeros((PAD - KEYS, HD), bf16)
-        content = ((q[...] + bu[...]) * FACTOR).astype(bf16)
-        located = ((q[...] + bv[...]) * FACTOR).astype(bf16)
-        p, da = probs[0], d_att[...]
-        d_p = dot_t(da, jnp.concatenate([v[...], pad], axis=0))
-        d_kv[1] = t_dot(p.astype(bf16), da)[:KEYS].astype(bf16)
-        d_s = (p * (d_p - jnp.sum(p * d_p, axis=-1, keepdims=True))).astype(bf16)
-        d_c = dot(d_s, jnp.concatenate([k[...], pad], axis=0)) * FACTOR
-        d_kv[0] = t_dot(d_s, content)[:KEYS].astype(bf16)
         row = lax.broadcasted_iota(jnp.int32, (T, T), 0)
         col = lax.broadcasted_iota(jnp.int32, (T, T), 1)
         flip = jnp.where(row + col == T - 1, 1.0, 0.0).astype(bf16)
-        d_raw = pltpu.roll(dot(flip, d_s), 0, 1, stride=1, stride_axis=0)
-        d_raw = dot(flip, d_raw.astype(bf16)).astype(bf16)
-        d_l = dot(d_raw, jnp.concatenate([rel[...], pad], axis=0)) * FACTOR
-        d_rel[...] = t_dot(d_raw, located)[:KEYS].astype(bf16)
-        d_q[...] = (d_c + d_l).astype(bf16)
-        d_bu[...] = jnp.sum(d_c, axis=0, keepdims=True)
-        d_bv[...] = jnp.sum(d_l, axis=0, keepdims=True)
+
+        def body(i, cut):
+            content = ((q[:, cut] + bu[:, cut]) * FACTOR).astype(bf16)
+            located = ((q[:, cut] + bv[:, cut]) * FACTOR).astype(bf16)
+            p, da = probs[i], d_att[:, cut]
+            d_p = dot_t(da, jnp.concatenate([v[:, cut], pad], axis=0))
+            d_kv[1, :, cut] = t_dot(p.astype(bf16), da)[:KEYS].astype(bf16)
+            d_s = (p * (d_p - jnp.sum(p * d_p, axis=-1, keepdims=True))).astype(bf16)
+            d_c = dot(d_s, jnp.concatenate([k[:, cut], pad], axis=0)) * FACTOR
+            d_kv[0, :, cut] = t_dot(d_s, content)[:KEYS].astype(bf16)
+            d_raw = pltpu.roll(dot(flip, d_s), 0, 1, stride=1, stride_axis=0)
+            d_raw = dot(flip, d_raw.astype(bf16)).astype(bf16)
+            d_l = dot(d_raw, jnp.concatenate([rel[:, cut], pad], axis=0)) * FACTOR
+            d_rel[:, cut] = t_dot(d_raw, located)[:KEYS].astype(bf16)
+            d_q[:, cut] = (d_c + d_l).astype(bf16)
+            d_bu[:, cut] = jnp.sum(d_c, axis=0, keepdims=True)
+            d_bv[:, cut] = jnp.sum(d_l, axis=0, keepdims=True)
+
+        each_head(body)
 
     return call(
         kernel,
@@ -200,7 +224,7 @@
             shape((1, D), f32),
             shape((1, D), f32),
         ),
-        (H,),
+        (STEPS,),
         [
             head(T),
             head(KEYS),
@@ -208,11 +232,11 @@
             head(KEYS),
             vec_head(),
             vec_head(),
-            pl.BlockSpec((1, T, PAD), lambda h, s: (h, 0, 0)),
+            pl.BlockSpec((PAIR, T, PAD), lambda h, s: (h, 0, 0)),
             head(T),
         ],
         [
-            pl.BlockSpec((2, KEYS, HD), lambda h, s: (0, 0, h)),
+            pl.BlockSpec((2, KEYS, PAIR * HD), lambda h, s: (0, 0, h)),
             head(KEYS),
             head(T),
             vec_head(),
@@ -421,7 +445,7 @@
     block = 256
     rows = T // 3
 
-    def kernel(s, x, w0, w1, w2, bias, g, b, compact, normed):
+    def kernel(s, x, w0, w1, w2, bias, g, b, compact, normed, natural):
         j = pl.program_id(0)
         total = bias[:, pl.ds(at(j * block), block)]
         for i, w in enumerate((w0, w1, w2)):
@@ -431,7 +455,11 @@
         @pl.when(j == D // block - 1)
         def _():
             xhat, r = center_scale(compact[...])
-            normed[...] = (xhat * g[...] + b[...]).astype(bf16)
+            natural[...] = (xhat * g[...] + b[...]).astype(bf16)
+            start = 0
+            for i, width in enumerate((D // 2, D // 4, D // 4)):
+                normed[:, start : start + width] = natural[:, pl.ds(at(s[3 + i]), width)]
+                start += width
 
     rest = (bias, g, b)
     out = (shape((rows, D), f32), shape((rows, D), bf16))
@@ -445,6 +473,7 @@
         [whole(o) for o in out],
         offsets,
         (oldest, *pieces, *rest),
+        [pltpu.VMEM((rows, D), bf16)],
     )
 
 
@@ -452,28 +481,30 @@
     rows = T // 3
 
     def kernel(_, q, k, v, ck, cv, loss, dck, dcv):
-        h = pl.program_id(0)
-        asking = (q[...] * FACTOR).astype(bf16)
-        p = softmax(dot_t(asking, k[...])).astype(bf16)
-        gp = softmax(dot_t(asking, ck[...]))
-        low = gp.astype(bf16)
-        miss = dot(p, v[...]) - dot(low, cv[...])
-
-        @pl.when(h == 0)
+        @pl.when(pl.program_id(0) == 0)
         def _():
             loss[...] = jnp.zeros_like(loss)
 
-        loss[...] += jnp.sum(miss * miss, axis=0, keepdims=True)
-        d_guess = ((-2.0 / (T * D)) * miss).astype(bf16)
-        d_gp = dot_t(d_guess, cv[...])
-        dcv[...] = t_dot(low, d_guess).astype(bf16)
-        d_gs = (gp * (d_gp - jnp.sum(gp * d_gp, axis=-1, keepdims=True))).astype(bf16)
-        dck[...] = t_dot(d_gs, asking).astype(bf16)
+        def body(i, cut):
+            asking = (q[:, cut] * FACTOR).astype(bf16)
+            cvh = cv[:, cut]
+            p = softmax(dot_t(asking, k[:, cut])).astype(bf16)
+            gp = softmax(dot_t(asking, ck[:, cut]))
+            low = gp.astype(bf16)
+            miss = dot(p, v[:, cut]) - dot(low, cvh)
+            loss[...] += jnp.sum(miss * miss, axis=0, keepdims=True)
+            d_guess = ((-2.0 / (T * D)) * miss).astype(bf16)
+            d_gp = dot_t(d_guess, cvh)
+            dcv[:, cut] = t_dot(low, d_guess).astype(bf16)
+            d_gs = (gp * (d_gp - jnp.sum(gp * d_gp, axis=-1, keepdims=True))).astype(bf16)
+            dck[:, cut] = t_dot(d_gs, asking).astype(bf16)
+
+        each_head(body)
 
     return call(
         kernel,
         (shape((1, HD), f32), shape((rows, D), bf16), shape((rows, D), bf16)),
-        (H,),
+        (STEPS,),
         [head(T), head(T, 1), head(T, 1, H), head(rows), head(rows, 0, H)],
         [pl.BlockSpec((1, HD), lambda h, s: (0, 0)), head(rows), head(rows)],
         none,
@@ -508,42 +539,62 @@
     )
 
 
-def weight_grad(jobs, scalars):
-    total = sum(j[3][0].shape[1] // (1 if j[4] else 2) for j in jobs)
-    block = jobs[0][0][0].shape[1] // 8
-    in_specs, args, widths = [], [], []
-    for xs, row_block, rows, dys, ready in jobs:
-        width = dys[0].shape[1] // (1 if ready else 2)
-        widths.append(width)
-        for x in xs:
-            in_specs.append(
-                pl.BlockSpec((rows, block), lambda q, y, s, r=row_block: (r, y * 4 + s[q]))
-            )
-        for dy in dys:
-            in_specs.append(
-                pl.BlockSpec((rows, width), lambda q, y, s, r=ready: (0, 0 if r else s[2]))
-            )
-        args += [*xs, *dys]
+def weight_grads(groups, scalars):
+    in_specs, args, outs, out_specs, layout = [], [], [], [], []
+    for ring, jobs in groups:
+        first = 1 if ring == "x" else 5
+        block = jobs[0][0][0].shape[1] // 8
+        widths = []
+        for xs, row_block, rows, dys, ready in jobs:
+            width = dys[0].shape[1] // (1 if ready else 2)
+            widths.append(width)
+            for x in xs:
+                for y in range(2):
+                    in_specs.append(
+                        pl.BlockSpec(
+                            (rows, block),
+                            lambda q, s, r=row_block, f=first, y=y: (r, y * 4 + s[f + q]),
+                        )
+                    )
+                    args.append(x)
+            for dy in dys:
+                in_specs.append(
+                    pl.BlockSpec((rows, width), lambda q, s, r=ready: (0, 0 if r else s[0]))
+                )
+                args.append(dy)
+        dims = (1, 2, block, sum(widths))
+        outs += [shape((2, *dims[1:]), bf16)] * 2
+        out_specs += [
+            pl.BlockSpec(dims, lambda q, s: (jnp.minimum(q, 1), 0, 0, 0)),
+            pl.BlockSpec(dims, lambda q, s: (jnp.maximum(q - 2, 0), 0, 0, 0)),
+        ]
+        layout.append(widths)
 
     def kernel(s, *refs):
-        out = refs[-1]
-        start = 0
-        for i, width in enumerate(widths):
-            xa, xb, da, db = refs[4 * i : 4 * i + 4]
-            out[0, 0, :, start : start + width] = (
-                t_dot(xa[...], da[...]) + t_dot(xb[...], db[...])
-            ).astype(bf16)
-            start += width
-
-    return call(
-        kernel,
-        shape((2, 2, block, total), bf16),
-        (2, 2),
-        in_specs,
-        pl.BlockSpec((1, 1, block, total), lambda q, y, s: (q, y, 0, 0)),
-        scalars,
-        args,
-    )
+        q = pl.program_id(0)
+        place = 0
+        results = refs[len(in_specs) :]
+        for i, widths in enumerate(layout):
+            start = 0
+            for width in widths:
+                a0, a1, b0, b1, da, db = refs[place : place + 6]
+                place += 6
+                for y, (xa, xb) in enumerate(((a0, b0), (a1, b1))):
+                    value = (t_dot(xa[...], da[...]) + t_dot(xb[...], db[...])).astype(bf16)
+                    columns = slice(start, start + width)
+
+                    @pl.when(q < 2)
+                    def _(i=i, y=y, columns=columns, value=value):
+                        results[2 * i][0, y, :, columns] = value
+
+                    @pl.when(q >= 2)
+                    def _(i=i, y=y, columns=columns, value=value):
+                        results[2 * i + 1][0, y, :, columns] = value
+
+                start += width
+
+    flat = call(kernel, tuple(outs), (4,), in_specs, out_specs, scalars, args)
+    return [(flat[2 * i], flat[2 * i + 1]) for i in range(len(groups))]
 
 
 def widen(gathered, start, rows, columns, swapped, none):
@@ -552,22 +603,23 @@
     chunks = columns // 2 // STEP
     order = [x * 4 + z for z in range(4) for x in range(4)] if swapped else list(range(16))
 
-    def kernel(_, src, out):
-        for to, frm in enumerate(order):
-            out[to] = src[frm].astype(f32)
+    def kernel(_, *refs):
+        out = refs[-1]
+        for k, src in enumerate(refs[:-1]):
+            for to, frm in enumerate(order):
+                out[to, :, k * STEP : (k + 1) * STEP] = src[frm].astype(f32)
 
     return call(
         kernel,
         shape((16, u, columns), f32),
-        (sub, 2, chunks),
+        (sub, 2),
         [
-            pl.BlockSpec(
-                (16, 32, STEP), lambda i, c, k, s: (c, start // 32 + k * sub + i, 0)
-            )
+            pl.BlockSpec((16, 32, STEP), lambda i, c, s, k=k: (c, start // 32 + k * sub + i, 0))
+            for k in range(chunks)
         ],
-        pl.BlockSpec((16, 32, STEP), lambda i, c, k, s: (0, i, c * chunks + k)),
+        pl.BlockSpec((16, 32, STEP * chunks), lambda i, c, s: (0, i, c)),
         none,
-        (gathered,),
+        (gathered,) * chunks,
     ).reshape(rows, columns)
 
 
@@ -597,17 +649,65 @@
     return place, place ^ first, place ^ 2, place ^ second
 
 
-def halve(send, keep, ring):
-    got = exchange(send, ring, (1, 3))
-    onward = (keep[1].astype(f32) + got[1].astype(f32)).astype(bf16)
-    last = exchange(onward, ring, (3, 1))
-    return keep[0].astype(f32) + got[0].astype(f32) + last.astype(f32)
-
-
-def ring_stage(v, axis, ring, place, core):
-    own, first, far, second = quarters(place, core)
-    send = jnp.stack([pick(v, first, axis), pick(v, far, axis)]).astype(bf16)
-    return halve(send, (pick(v, own, axis), pick(v, second, axis)), ring)
+class Flow:
+    def __init__(self, ring, pair, place, core):
+        self.rings = (ring, "z" if ring == "x" else "x")
+        self.place, self.core = place, core
+        send, self.keep = pair
+        self.got = exchange(send, ring, (1, 3))
+
+    def onward(self, ring):
+        got = line.later(self.got)
+        self.near = got[0]
+        value = (self.keep[1].astype(f32) + got[1].astype(f32)).astype(bf16)
+        self.last = exchange(value, ring, (3, 1))
+        line.hold(value)
+
+    def settle(self):
+        last = line.later(self.last)
+        return self.keep[0].astype(f32) + self.near.astype(f32) + last.astype(f32)
+
+    def second(self):
+        self.onward(self.rings[0])
+
+    def third(self):
+        v = self.settle()
+        y, rows, columns = v.shape
+        v = v.reshape(y, 4, rows // 4, columns)
+        ring = self.rings[1]
+        own, first, far, second = quarters(self.place[ring], self.core)
+        send = jnp.stack([pick(v, first, 1), pick(v, far, 1)]).astype(bf16)
+        self.keep = (pick(v, own, 1), pick(v, second, 1))
+        self.got = exchange(send, ring, (1, 3))
+        line.hold(send, *self.keep)
+
+    def fourth(self):
+        self.onward(self.rings[1])
+
+    def rows(self):
+        v = self.settle()
+        y, u, columns = v.shape
+        v = v.reshape(y, u, columns // STEP, STEP).transpose(0, 2, 1, 3)
+        return v.reshape(y, -1, STEP)
+
+
+class Finish:
+    def __init__(self, parts, yl):
+        v = jnp.concatenate(parts, axis=1)
+        self.mine = pick(v, yl, 0)
+        send = pick(v, 1 - yl, 0).astype(bf16)
+        self.got = exchange(send, "y", (1, 3))
+        line.hold(send, self.mine)
+
+    def second(self):
+        got = line.later(self.got)
+        self.mine = (self.mine + got.astype(f32)).astype(bf16)
+        self.far = lax.ppermute(self.mine, "yh", [(0, 1), (1, 0)])
+        line.hold(self.mine)
+
+    def done(self):
+        far = line.later(self.far)
+        return (self.mine.astype(f32) + far.astype(f32)).astype(bf16)
 
 
 def per_device(
@@ -632,6 +732,7 @@
     conv_w,
     conv_b,
 ):
+    line.held = []
     tokens, memory, compressed, cotangent = tokens[0], memory[0], compressed[0], cotangent[0]
     yl, core = lax.axis_index("yl"), lax.axis_index("c")
     place = {"x": lax.axis_index("x"), "z": lax.axis_index("z")}
@@ -655,15 +756,7 @@
 
     def over_y(w):
         n = w.shape[0] // 2
-        got = exchange(lax.dynamic_slice_in_dim(w, core * n, n, 0), "y", (1, 3))
-        return w, got, core_swap(got)
-
-    kv_pieces = over_y(w_kv)
-    q_pieces = over_y(w_q)
-    r_pieces = over_y(w_r)
-    o_pieces = over_y(w_o)
-    conv_pieces = over_y(conv_w)
-    thirds_d, thirds_c = thirds(D), thirds(3 * D)
+        return exchange(lax.dynamic_slice_in_dim(w, core * n, n, 0), "y", (1, 3))
 
     spot = (place["x"] * 4 + place["z"]) * 2 + core
     n_in, n_out = w_in.shape[0] // 32, w_out.shape[0] // 32
@@ -675,98 +768,144 @@
         )
     )
     spread = lax.all_gather(piece, ("x", "z", "c"), axis=0)
-
-    normed, oldest = first_norm(compressed, memory, tokens, ln1_g, ln1_b, none)
-    key_value = project(normed, kv_pieces, thirds_d, 512, bf16)
-    queries = project(normed, q_pieces, thirds_d, 512, f32, T, 2)
+    kv_got, q_got, r_got, o_got = over_y(w_kv), over_y(w_q), over_y(w_r), over_y(w_o)
+    conv_got = over_y(conv_w)
+    thirds_d = thirds(D)
+    thirds_c = jnp.concatenate([thirds(3 * D), thirds_d])
+
+    def both(v):
+        return (v, core_swap(v))
+
+    both_cot = both(cotangent)
+    normed, normed_rel, oldest = first_norm(
+        compressed, memory, tokens, ln1_g, ln1_b, thirds_d
+    )
+    both_normed = both(normed)
+    both_oldest = both(oldest)
     sinus_table = sinusoid(KEYS, D).astype(bf16)
-    relative = project(sinus_table, r_pieces, thirds_d, 512, bf16)
+    sinus_rel = jnp.concatenate(
+        [
+            lax.dynamic_slice_in_dim(sinus_table, thirds_d[i], width, 1)
+            for i, width in enumerate((D // 2, D // 4, D // 4))
+        ],
+        axis=1,
+    )
+
+    def joined(w, got):
+        return jnp.concatenate([w, got, core_swap(got)], axis=0)
+
+    kv_whole = joined(w_kv, kv_got)
+    key_value = dot(line.later(normed_rel), kv_whole).astype(bf16)
+    line.hold(key_value)
+    queries = dot(line.later(normed_rel[2 * T :]), joined(w_q, q_got))
+    line.hold(queries)
+    relative = dot(line.later(sinus_rel), joined(w_r, r_got)).astype(bf16)
+    line.hold(relative)
+    kv_pieces = (w_kv, kv_got, core_swap(kv_got))
+    q_pieces = (w_q, q_got, core_swap(q_got))
+    o_pieces = (w_o, o_got, core_swap(o_got))
+    conv_pieces = (conv_w, conv_got, core_swap(conv_got))
     probs, attended = attend(queries, key_value, relative, bias_u, bias_v, none)
     residual, normed2 = out_and_norm(attended, o_pieces, thirds_d, tokens, ln2_g, ln2_b)
+    both_n2, both_att = both(normed2), both(attended)
 
     compact, comp_normed = compress(oldest, conv_pieces, thirds_c, conv_b, ln1_g, ln1_b)
-    comp_pair = project(comp_normed, kv_pieces, thirds_d, 512, bf16)
+    comp_pair = dot(comp_normed, kv_whole).astype(bf16)
     loss, d_ck, d_cv = reconstruct(queries, key_value, comp_pair, none)
     recon_loss = jnp.sum(loss) / (T * D)
     compressed_next = jnp.concatenate([compressed[T // 3 :], compact], axis=0)
     d_compact, d_conv_b = compress_back(d_ck, d_cv, kv_pieces, thirds_d, compact, ln1_g)
-
-    def both(v):
-        return (v, core_swap(v))
-
-    def reduce(jobs, ring):
+    both_compact = both(d_compact)
+
+    cuts = []
+    for ring in ("x", "z"):
         own, first, far, second = quarters(place[ring], core)
-        send = weight_grad(jobs, ints(first, far, core))
-        keep = weight_grad(jobs, ints(own, second, core))
-        kept = halve(send, keep, ring)
-        other = "z" if ring == "x" else "x"
-        y, rows, columns = kept.shape
-        kept = kept.reshape(y, 4, rows // 4, columns)
-        return ring_stage(kept, 1, other, place[other], core)
-
-    def finish(sums):
-        flat = [
-            v.reshape(2, v.shape[1], -1, STEP).transpose(0, 2, 1, 3).reshape(2, -1, STEP)
-            for v in sums
-        ]
-        v = jnp.concatenate(flat, axis=1)
-        got = exchange(pick(v, 1 - yl, 0).astype(bf16), "y", (1, 3))
-        mine = (pick(v, yl, 0) + got.astype(f32)).astype(bf16)
-        far = lax.ppermute(mine, "yh", [(0, 1), (1, 0)])
-        done = (mine.astype(f32) + far.astype(f32)).astype(bf16)
-        return lax.all_gather(done, ("c", "x", "z"), axis=0)
-
-    both_normed = both(normed)
-    both_cot = both(cotangent)
-    sum_conv = reduce([(both(oldest), 0, T // 3, both(d_compact), False)], "z")
+        cuts += [first, far, own, second]
+    cuts = ints(core, *cuts)
+
+    def flows(groups):
+        pairs = weight_grads(groups, cuts)
+        return [Flow(ring, pair, place, core) for (ring, _), pair in zip(groups, pairs)]
 
     hidden, d_pre, mixed_out, d_normed2, d_b_in = feed_forward(
         normed2, residual, cotangent, w_in, w_out, spread, b_in, b_out, ints(yl)
     )
-    sum_out = reduce([(both(hidden), 0, T, both_cot, False)], "x")
-    sum_in = reduce([(both(normed2), 0, T, both(d_pre), False)], "z")
+    both_hidden, both_pre = both(hidden), both(d_pre)
+    (conv_flow,) = flows([("x", [(both_oldest, 0, T // 3, both_compact, False)])])
     d_residual, d_branch, d_attended, d_ln2_g, d_ln2_b, d_b_out = second_norm_back(
         cotangent, d_normed2, residual, ln2_g, o_pieces, thirds_d
     )
-    sum_o = reduce([(both(attended), 0, T, both(d_branch), False)], "x")
+    both_branch = both(d_branch)
+    out_flow, in_flow = flows(
+        [
+            ("x", [(both_hidden, 0, T, both_cot, False)]),
+            ("z", [(both_n2, 0, T, both_pre, False)]),
+        ]
+    )
     d_kv, d_relative, d_queries, d_bias_u, d_bias_v = attend_back(
         queries, key_value, relative, bias_u, bias_v, probs, d_attended, none
     )
     both_kv = (pick(d_kv, core, 0), core_swap(pick(d_kv, 1 - core, 0)))
-    sum_kv = reduce([(both_normed, 0, KEYS, both_kv, True)], "x")
-    sum_qr = reduce(
-        [
-            (both_normed, 2, T, both(d_queries), False),
-            ((sinus_table, sinus_table), 0, KEYS, both(d_relative), False),
-        ],
-        "z",
-    )
+    both_q, both_rel = both(d_queries), both(d_relative)
+    conv_flow.second()
     d_tokens, d_ln1_g, d_ln1_b = first_norm_back(
         d_kv, d_queries, kv_pieces, q_pieces, compressed, memory, tokens, ln1_g, d_residual,
         thirds_d,
     )
-
-    early = finish([sum_out, sum_in, sum_conv, sum_o])
-    late = finish([sum_kv, sum_qr])
-    g_out = widen(early, 0, FF // 2, D, False, none)
-    g_in = widen(early, 128, D // 2, FF, True, none)
-    g_conv = widen(early, 256, 3 * D // 2, D, True, none)
-    g_o = widen(early, 352, D // 2, D, False, none)
-    g_kv = widen(late, 0, D // 2, 2 * D, False, none)
-    g_q = widen(late, 64, D // 2, D, True, none)
-    g_r = widen(late, 96, D // 2, D, True, none)
+    out_flow.second()
+    in_flow.second()
+    conv_flow.third()
+    x_flow, z_flow = flows(
+        [
+            (
+                "x",
+                [(both_normed, 0, KEYS, both_kv, True), (both_att, 0, T, both_branch, False)],
+            ),
+            (
+                "z",
+                [
+                    (both_normed, 2, T, both_q, False),
+                    ((sinus_table, sinus_table), 0, KEYS, both_rel, False),
+                ],
+            ),
+        ]
+    )
+    conv_flow.fourth()
+    out_flow.third()
+    in_flow.third()
+    x_flow.second()
+    z_flow.second()
+    out_flow.fourth()
+    in_flow.fourth()
+    early = Finish([out_flow.rows(), in_flow.rows(), conv_flow.rows()], yl)
+    x_flow.third()
+    z_flow.third()
+    early.second()
+    x_flow.fourth()
+    z_flow.fourth()
+    early_sums = lax.all_gather(early.done(), ("c", "x", "z"), axis=0)
 
     total = jnp.concatenate(
         [d_ln1_g, d_ln1_b, d_bias_u, d_bias_v, d_ln2_g, d_ln2_b, d_b_out, d_conv_b]
-        + [d_b_in.reshape(4, D), jnp.zeros((4, D), f32)]
-    )
-    total = total + core_swap(total)
-    for ring in ("x", "z", "y"):
-        total = total + exchange(total, ring, (1, 1))
-        total = total + exchange(total, ring, (2, 2) if ring == "y" else (3, 3))
-    half = lax.dynamic_slice_in_dim(total[:8], yl * (D // 2), D // 2, 1)
+        + [d_b_in.reshape(4, D)]
+    )
+    total = jnp.concatenate(
+        [total[:8].reshape(8, 2, STEP).transpose(1, 0, 2), total[8:].reshape(2, 4, STEP)], axis=1
+    )
+    late = Finish([x_flow.rows(), z_flow.rows(), total, jnp.zeros((2, 4, STEP), f32)], yl)
+    late.second()
+    late_sums = lax.all_gather(late.done(), ("c", "x", "z"), axis=0)
+
+    g_in = widen(early_sums, 128, D // 2, FF, True, none)
+    g_out = widen(early_sums, 0, FF // 2, D, False, none)
+    g_conv = widen(early_sums, 256, 3 * D // 2, D, False, none)
+    g_kv = widen(late_sums, 0, D // 2, 2 * D, False, none)
+    g_o = widen(late_sums, 64, D // 2, D, False, none)
+    g_q = widen(late_sums, 96, D // 2, D, True, none)
+    g_r = widen(late_sums, 128, D // 2, D, True, none)
+    half = jnp.sum(late_sums[:, 160:172].astype(f32), axis=0)
     t_ln1_g, t_ln1_b, t_bu, t_bv, t_ln2_g, t_ln2_b, t_bout, t_convb = [half[i] for i in range(8)]
-    t_bin = lax.dynamic_slice_in_dim(total[8:12], yl * 2, 2, 0).reshape(-1)
+    t_bin = half[8:].reshape(-1)
     return (
         mixed_out[None],
         compressed_next[None],

time: 487 us -> 520 us (1.068)
  waiting for transfers between devices: 121 us -> 198 us
  Pallas kernels: 203 us -> 152 us
  starting transfers between devices: 71.9 us -> 57.6 us
  matrix products: 0 us -> 13.7 us
  local copies, waits for them, and re-layouts: 31.1 us -> 37.7 us
    all_gather x2, waiting for transfers between devices: 11.2 us -> 102 us  [the longest x1 60.1 us: per_device(): early_sums = lax.all_gather(early.done(), ('c', 'x', 'z'), axis=0)]
    pallas_call x33 -> x20, Pallas kernels: 203 us -> 152 us  [run_kernel(): pl.pallas_call(kernel, out_shape=out, grid_spec=pltpu.PrefetchScalarGridS...]
    ppermute x37 -> x27, waiting for transfers between devices: 89.6 us -> 73.4 us  [exchange(): return lax.ppermute(v, RING[ring], pairs)]
    ppermute x37 -> x27, starting transfers between devices: 51.7 us -> 37.4 us  [exchange(): return lax.ppermute(v, RING[ring], pairs)]
    dot_general x0 -> x4, matrix products: none -> 13.7 us  [dot(): return jnp.dot(a, b, preferred_element_type=f32)]
    ppermute x18 -> x17, starting transfers between devices: 13.9 us -> 11.6 us  [core_swap(): return lax.ppermute(v, 'c', [(0, 1), (1, 0)])]
    convert_element_type x17 -> x14, other arithmetic: 13.3 us -> 14.8 us  [the longest x10 11.3 us: onward(): value = (self.keep[1].astype(f32) + got[1].astype(f32)).astype(bf16)]
  transfers between devices with their start and end apart: 62 -> 51, of which waited for: 25 -> 19; matrix products, arithmetic and copies ran while one was open for 10% -> 15% of each run, Pallas kernels for 38% -> 18%
where the time goes in v3:
time: 520 us; the launch traced here: 512 us
  waiting for transfers between devices  198 us (38%)
  Pallas kernels  152 us (29%)
  starting transfers between devices  57.6 us (11%)
  local copies, waits for them, and re-layouts  37.7 us (7%)
  other arithmetic  35.3 us (7%)
  between operations  16.8 us (3%)
  matrix products  13.7 us (3%)
    pallas_call x20, Pallas kernels, run_kernel(): pl.pallas_call(kernel, out_shape=out, grid_spec=pltpu.PrefetchScalarGridS...  152 us
    ppermute x27, waiting for transfers between devices, exchange(): return lax.ppermute(v, RING[ring], pairs)  73.4 us
    all_gather x1, waiting for transfers between devices, per_device(): early_sums = lax.all_gather(early.done(), ('c', 'x', 'z'), axis=0)  60.1 us
    all_gather x1, waiting for transfers between devices, per_device(): late_sums = lax.all_gather(late.done(), ('c', 'x', 'z'), axis=0)  42.4 us
    ppermute x27, starting transfers between devices, exchange(): return lax.ppermute(v, RING[ring], pairs)  37.4 us
    unnamed x128, local copies, waits for them, and re-layouts  19.1 us
    dot_general x4, matrix products, dot(): return jnp.dot(a, b, preferred_element_type=f32)  13.7 us
    ppermute x17, starting transfers between devices, core_swap(): return lax.ppermute(v, 'c', [(0, 1), (1, 0)])  11.6 us
  transfers between devices with their start and end apart: 51, of which 19 were waited for; matrix products, arithmetic and copies ran while one was open for 15% of the time, Pallas kernels for 18%

profile of v3, /device:TPU:1, one launch (start us, length us, event | category | flops | bytes accessed | tf_op | source)
XLA Modules:
  0.0 511.5 jit_solution(5943628298122646831)
XLA Ops:
  13.6 5.6 %collective-permute-done.11 = bf16[128,1024]{1,0:T(8,128)(2,1)S(1)} collective-permute-done((bf16[128,1024]{1,0:T(8,128)(2,1)S(1)}, bf16[128,1024]{1,0:T(8,128)(2,1)S(1)}, u32[]{:S(2)}, u32[]{:S(2)}) %collective-permute-start.11) | collective-permute-done | bytes 262176 | tf_op jit(solution)/shard_map/ppermute | solution.py:631
  42.0 4.7 fusion.16
  48.6 8.8 %collective-permute-done.1.w1.k1 = bf16[256,2048]{1,0:T(8,128)(2,1)} collective-permute-done((bf16[256,2048]{1,0:T(8,128)(2,1)}, bf16[256,2048]{1,0:T(8,128)(2,1)}, u32[]{:S(2)}, u32[]{:S(2)}) %collective-permute-start.1) | collective-permute-done | bytes 1048608 | tf_op jit(solution)/shard_map/ppermute | solution.py:639
  64.1 4.6 shard_map.347
  70.8 9.0 %collective-permute-done.5 = bf16[256,1024]{1,0:T(8,128)(2,1)S(1)} collective-permute-done((bf16[256,1024]{1,0:T(8,128)(2,1)}, bf16[256,1024]{1,0:T(8,128)(2,1)S(1)}, u32[]{:S(2)}, u32[]{:S(2)}) %collective-permute-start.5) | collective-permute-done | bytes 524320 | tf_op jit(solution)/shard_map/ppermute | solution.py:639
  85.2 6.1 %convolution_convert_fusion.k.v = bf16[576,2048]{1,0:T(8,128)(2,1)} fusion(bf16[576,1024]{1,0:T(8,128)(2,1)S(1)} %copy-done.43, bf16[1024,2048]{1,0:T(8,128)(2,1)} %constant_dynamic-update-slice_fusion), kind=kOutput, calls=%fused_computation | convolution fusion | flops 2417098752 | bytes 7733248 | tf_op jit(solution)/shard_map/dot_general | solution.py:30
  96.5 7.5 %shard_map.348 = (f32[8,192,640]{2,1,0:T(8,128)}, bf16[192,1024]{1,0:T(8,128)(2,1)}) custom-call(s32[1]{0:T(128)} %constant.109.clone.1._, f32[192,1024]{1,0:T(8,128)} %fusion.q, bf16[576,2048]{1,0:T(8,128)(2,1)} %convolution_convert_fusion.k.v, bf16[576,2048]{1,0:T(8,128)(2,1)} %convolution_convert_fusion.k.v, bf16[576,1024]{1,0:T(8,128)(2,1)} %fusion.12.rel, ...), custom_call_target="tpu_custom_call" | custom-call | tf_op jit(solution)/shard_map/pallas_call | solution.py:67
  104.8 4.0 shard_map.349
  110.0 6.6 %shard_map.350 = (f32[64,1024]{1,0:T(8,128)}, bf16[64,1024]{1,0:T(8,128)(2,1)}) custom-call(s32[6]{0:T(128)} %concatenate.44.s, bf16[64,3072]{1,0:T(8,128)(2,1)} %get-tuple-element.120.x.refs_0_.refs_1_, bf16[1536,1024]{1,0:T(8,128)(2,1)} %w0.5, bf16[768,1024]{1,0:T(8,128)(2,1)} %collective-permute-done.9.w1, bf16[768,1024]{1,0:T(8,128)(2,1)} %copy-done.18, ...), custom_call_target="tpu_custom_call" | custom-call | tf_op jit(solution)/shard_map/pallas_call | solution.py:67
  119.0 8.4 %shard_map.351 = (f32[1,128]{1,0:T(1,128)}, bf16[64,1024]{1,0:T(8,128)(2,1)}, bf16[64,1024]{1,0:T(8,128)(2,1)}) custom-call(s32[1]{0:T(128)} %constant.109.clone.1._, f32[192,1024]{1,0:T(8,128)} %fusion.q, bf16[576,2048]{1,0:T(8,128)(2,1)} %convolution_convert_fusion.k.v, bf16[576,2048]{1,0:T(8,128)(2,1)} %convolution_convert_fusion.k.v, ...), custom_call_target="tpu_custom_call" | custom-call | tf_op jit(solution)/shard_map/pallas_call | solution.py:67
  127.5 5.2 %shard_map.352 = (bf16[64,1024]{1,0:T(8,128)(2,1)}, f32[1,1024]{1,0:T(1,128)}) custom-call(s32[3]{0:T(128)} %pad_add_fusion.s, bf16[64,1024]{1,0:T(8,128)(2,1)} %get-tuple-element.126.dck, bf16[64,1024]{1,0:T(8,128)(2,1)} %get-tuple-element.127.dcv, bf16[512,2048]{1,0:T(8,128)(2,1)} %k0.1, bf16[256,2048]{1,0:T(8,128)(2,1)} %collective-permute-done.1.w1.k1, ...), custom_call_target="tpu_custom_call" | custom-call | tf_op jit(solution)/shard_map/pallas_call | solution.py:67
  132.7 18.3 %shard_map.353 = (bf16[192,4096]{1,0:T(8,128)(2,1)}, bf16[192,4096]{1,0:T(8,128)(2,1)}, bf16[192,1024]{1,0:T(8,128)(2,1)}, f32[192,1024]{1,0:T(8,128)}, f32[8,512]{1,0:T(8,128)}) custom-call(s32[1]{0:T(128)} %bitcast.s, bf16[192,1024]{1,0:T(8,128)(2,1)} %get-tuple-element.130.n2.refs_6_.refs_7_, f32[192,1024]{1,0:T(8,128)} %get-tuple-element.118.res, ...), custom_call_target="tpu_custom_call" | custom-call | tf_op jit(solution)/shard_map/pallas_call | solution.py:67
  152.6 3.7 collective-permute-done.12.refs_2_.refs_3_
  159.4 6.7 %shard_map.354 = (bf16[2,2,384,512]{3,2,1,0:T(8,128)(2,1)}, bf16[2,2,384,512]{3,2,1,0:T(8,128)(2,1)}) custom-call(s32[9]{0:T(128)} %stack.131.s, bf16[64,3072]{1,0:T(8,128)(2,1)} %get-tuple-element.120.x.refs_0_.refs_1_, bf16[64,3072]{1,0:T(8,128)(2,1)} %get-tuple-element.120.x.refs_0_.refs_1_, bf16[64,3072]{1,0:T(8,128)(2,1)} %copy-done.19, ...), custom_call_target="tpu_custom_call" | custom-call | tf_op jit(solution)/shard_map/pallas_call | solution.py:67
  166.1 4.9 shard_map.355
  171.0 14.0 %shard_map.356 = (bf16[2,2,512,512]{3,2,1,0:T(8,128)(2,1)}, bf16[2,2,512,512]{3,2,1,0:T(8,128)(2,1)}, bf16[2,2,128,2048]{3,2,1,0:T(8,128)(2,1)}, bf16[2,2,128,2048]{3,2,1,0:T(8,128)(2,1)}) custom-call(s32[9]{0:T(128)} %stack.131.s, bf16[192,4096]{1,0:T(8,128)(2,1)} %get-tuple-element.132.refs_0_.refs_1_, ...), custom_call_target="tpu_custom_call" | custom-call | tf_op jit(solution)/shard_map/pallas_call | solution.py:67
  187.7 3.8 collective-permute-start.20
  192.0 11.5 %shard_map.357 = (bf16[2,576,1024]{2,1,0:T(8,128)(2,1)}, bf16[576,1024]{1,0:T(8,128)(2,1)}, bf16[192,1024]{1,0:T(8,128)(2,1)}, f32[1,1024]{1,0:T(1,128)}, f32[1,1024]{1,0:T(1,128)}) custom-call(s32[1]{0:T(128)} %constant.109.clone.1._, f32[192,1024]{1,0:T(8,128)} %fusion.q, bf16[576,2048]{1,0:T(8,128)(2,1)} %convolution_convert_fusion.k.v, ...), custom_call_target="tpu_custom_call" | custom-call | tf_op jit(solution)/shard_map/pallas_call | solution.py:67
  203.5 24.8 %collective-permute-done.18 = bf16[2,2,384,512]{3,2,1,0:T(8,128)(2,1)} collective-permute-done((bf16[2,2,384,512]{3,2,1,0:T(8,128)(2,1)}, bf16[2,2,384,512]{3,2,1,0:T(8,128)(2,1)}, u32[]{:S(2)}, u32[]{:S(2)}) %collective-permute-start.18) | collective-permute-done | bytes 1572896 | tf_op jit(solution)/shard_map/ppermute | solution.py:639
  230.0 13.0 %shard_map.358 = (f32[192,1024]{1,0:T(8,128)}, f32[1,1024]{1,0:T(1,128)}, f32[1,1024]{1,0:T(1,128)}) custom-call(s32[3]{0:T(128)} %pad_add_fusion.s, bf16[2,576,1024]{2,1,0:T(8,128)(2,1)} %get-tuple-element.143.dkv, bf16[192,1024]{1,0:T(8,128)(2,1)} %get-tuple-element.147.dq.refs_16_, bf16[512,2048]{1,0:T(8,128)(2,1)} %k0.1, ...), custom_call_target="tpu_custom_call" | custom-call | tf_op jit(solution)/shard_map/pallas_call | solution.py:67
  258.3 3.8 collective-permute-start.29
  263.7 19.0 %shard_map.359 = (bf16[2,2,128,1536]{3,2,1,0:T(8,128)(2,1)}, bf16[2,2,128,1536]{3,2,1,0:T(8,128)(2,1)}, bf16[2,2,128,1024]{3,2,1,0:T(8,128)(2,1)}, bf16[2,2,128,1024]{3,2,1,0:T(8,128)(2,1)}) custom-call(s32[9]{0:T(128)} %stack.131.s, bf16[576,1024]{1,0:T(8,128)(2,1)} %get-tuple-element.109.refs_0_.refs_1_.refs_12_.refs_13_, ...), custom_call_target="tpu_custom_call" | custom-call | tf_op jit(solution)/shard_map/pallas_call | solution.py:67
  294.4 9.2 %collective-permute-done.28 = bf16[2,2,128,1536]{3,2,1,0:T(8,128)(2,1)S(1)} collective-permute-done((bf16[2,2,128,1536]{3,2,1,0:T(8,128)(2,1)}, bf16[2,2,128,1536]{3,2,1,0:T(8,128)(2,1)S(1)}, u32[]{:S(2)}, u32[]{:S(2)}) %collective-permute-start.28) | collective-permute-done | bytes 1572896 | tf_op jit(solution)/shard_map/ppermute | solution.py:639
  318.9 5.3 %collective-permute-done.32 = bf16[2,128,1536]{2,1,0:T(8,128)(2,1)S(1)} collective-permute-done((bf16[2,128,1536]{2,1,0:T(8,128)(2,1)}, bf16[2,128,1536]{2,1,0:T(8,128)(2,1)S(1)}, u32[]{:S(2)}, u32[]{:S(2)}) %collective-permute-start.32) | collective-permute-done | bytes 786464 | tf_op jit(solution)/shard_map/ppermute | solution.py:639
  335.0 5.0 collective-permute-done.44
  350.8 4.1 collective-permute-done.46
  358.5 7.3 %collective-permute-done.47 = bf16[352,512]{1,0:T(8,128)(2,1)S(1)} collective-permute-done((bf16[352,512]{1,0:T(8,128)(2,1)}, bf16[352,512]{1,0:T(8,128)(2,1)S(1)}, u32[]{:S(2)}, u32[]{:S(2)}) %collective-permute-start.47) | collective-permute-done | bytes 360480 | tf_op jit(solution)/shard_map/ppermute | solution.py:705
  370.0 42.4 %all-gather.9.cloned.1.call-done = bf16[5632,512]{1,0:T(8,128)(2,1)} async-done(((bf16[176,512]{1,0:T(8,128)(2,1)}), bf16[5632,512]{1,0:T(8,128)(2,1)}) %all-gather.9.cloned.1.call-update) | async-done | bytes 5767184 | tf_op jit(solution)/shard_map/all_gather | solution.py:897
  414.7 60.1 %all-gather.11.cloned.1.call-done = bf16[11264,512]{1,0:T(8,128)(2,1)} async-done(((bf16[352,512]{1,0:T(8,128)(2,1)}), bf16[11264,512]{1,0:T(8,128)(2,1)}) %all-gather.11.cloned.1.call-update) | async-done | bytes 11534352 | tf_op jit(solution)/shard_map/all_gather | solution.py:886
  474.8 5.2 %shard_map.360 = f32[16,32,4096]{2,1,0:T(8,128)} custom-call(s32[1]{0:T(128)} %constant.109.clone.1._, bf16[32,352,512]{2,1,0:T(8,128)(2,1)} %bitcast.218, bf16[32,352,512]{2,1,0:T(8,128)(2,1)} %bitcast.219, bf16[32,352,512]{2,1,0:T(8,128)(2,1)} %bitcast.220, bf16[32,352,512]{2,1,0:T(8,128)(2,1)} %bitcast.221), custom_call_target="tpu_custom_call" | custom-call | tf_op jit(solution)/shard_map/pallas_call | solution.py:67
  480.0 7.3 %shard_map.361 = f32[16,128,1024]{2,1,0:T(8,128)} custom-call(s32[1]{0:T(128)} %constant.109.clone.1._, bf16[32,352,512]{2,1,0:T(8,128)(2,1)} %bitcast.222), custom_call_target="tpu_custom_call" | custom-call | tf_op jit(solution)/shard_map/pallas_call | solution.py:67
  487.3 5.8 %shard_map.362 = f32[16,96,1024]{2,1,0:T(8,128)} custom-call(s32[1]{0:T(128)} %constant.109.clone.1._, bf16[32,352,512]{2,1,0:T(8,128)(2,1)} %bitcast.223), custom_call_target="tpu_custom_call" | custom-call | tf_op jit(solution)/shard_map/pallas_call | solution.py:67
  (309 shorter events, 149.3 us)
Async XLA Ops:
  7.2 125.5 %all-gather.7.cloned.1.call-start = ((), (), s32[]{:S(2)}) async-start(), calls=%async_computation | async-start | bytes 8650752 | tf_op jit(solution)/shard_map/all_gather | solution.py:770
  19.9 392.4 %all-gather.9.cloned.1.call-start = ((), (), s32[]{:S(2)}) async-start(), calls=%async_computation.1 | async-start | bytes 5947392 | tf_op jit(solution)/shard_map/all_gather | solution.py:897
  27.6 33.4 %collective-permute-start = (bf16[12,512]{1,0:T(8,128)(2,1)S(1)}, bf16[12,512]{1,0:T(8,128)(2,1)S(1)}, u32[]{:S(2)}, u32[]{:S(2)}) collective-permute-start(bf16[12,512]{1,0:T(8,128)(2,1)S(1)} %reshape.184), channel_id=1, source_target_pairs={{0,1},{1,0},{2,3},{3,2},{4,5},{5,4},{6,7},{7,6},{8,9},{9,8},{10,11... | collective-permute-start | bytes 36872 | tf_op jit(solution)/shard_map/ppermute | solution.py:631
  31.1 39.3 %collective-permute-start.7 = (bf16[256,1024]{1,0:T(8,128)(2,1)}, bf16[256,1024]{1,0:T(8,128)(2,1)}, u32[]{:S(2)}, u32[]{:S(2)}) collective-permute-start(bf16[256,1024]{1,0:T(8,128)(2,1)} %constant_dynamic-slice_fusion.1), channel_id=1, source_target_pairs={{0,1},{2,67},{1,0},{3,66},{64,65},{66,3},{65,64},{67,2},{4,5},{6,7... | collective-permute-start | bytes 1572872 | tf_op jit(solution)/shard_map/ppermute | solution.py:639
  34.9 35.5 %collective-permute-start.3 = (bf16[256,1024]{1,0:T(8,128)(2,1)}, bf16[256,1024]{1,0:T(8,128)(2,1)}, u32[]{:S(2)}, u32[]{:S(2)}) collective-permute-start(bf16[256,1024]{1,0:T(8,128)(2,1)} %constant_dynamic-slice_fusion.3), channel_id=1, source_target_pairs={{0,1},{2,67},{1,0},{3,66},{64,65},{66,3},{65,64},{67,2},{4,5},{6,7... | collective-permute-start | bytes 1572872 | tf_op jit(solution)/shard_map/ppermute | solution.py:639
  36.7 20.8 %collective-permute-start.1 = (bf16[256,2048]{1,0:T(8,128)(2,1)}, bf16[256,2048]{1,0:T(8,128)(2,1)}, u32[]{:S(2)}, u32[]{:S(2)}) collective-permute-start(bf16[256,2048]{1,0:T(8,128)(2,1)} %constant_dynamic-slice_fusion.4), channel_id=1, source_target_pairs={{0,1},{2,67},{1,0},{3,66},{64,65},{66,3},{65,64},{67,2},{4,5},{6,7... | collective-permute-start | bytes 3145736 | tf_op jit(solution)/shard_map/ppermute | solution.py:639
  41.3 42.6 %collective-permute-start.9 = (bf16[768,1024]{1,0:T(8,128)(2,1)}, bf16[768,1024]{1,0:T(8,128)(2,1)}, u32[]{:S(2)}, u32[]{:S(2)}) collective-permute-start(bf16[768,1024]{1,0:T(8,128)(2,1)} %constant_dynamic-slice_fusion), channel_id=1, source_target_pairs={{0,1},{2,67},{1,0},{3,66},{64,65},{66,3},{65,64},{67,2},{4,5},{6,7... | collective-permute-start | bytes 4718600 | tf_op jit(solution)/shard_map/ppermute | solution.py:639
  57.5 26.6 %collective-permute-start.2 = (bf16[256,2048]{1,0:T(8,128)(2,1)}, bf16[256,2048]{1,0:T(8,128)(2,1)S(1)}, u32[]{:S(2)}, u32[]{:S(2)}) collective-permute-start(bf16[256,2048]{1,0:T(8,128)(2,1)} %collective-permute-done.1.w1.k1), channel_id=1, source_target_pairs={{0,2},{2,0},{1,3},{3,1},{4,6},{6,4},{5,7},{7,5},{8,10},{10,8},{9,1... | collective-permute-start | bytes 3145736 | tf_op jit(solution)/shard_map/ppermute | solution.py:627
  60.9 18.9 %collective-permute-start.5 = (bf16[256,1024]{1,0:T(8,128)(2,1)}, bf16[256,1024]{1,0:T(8,128)(2,1)S(1)}, u32[]{:S(2)}, u32[]{:S(2)}) collective-permute-start(bf16[256,1024]{1,0:T(8,128)(2,1)} %constant_dynamic-slice_fusion.2), channel_id=1, source_target_pairs={{0,1},{2,67},{1,0},{3,66},{64,65},{66,3},{65,64},{67,2},{4,5},{6,7... | collective-permute-start | bytes 1572872 | tf_op jit(solution)/shard_map/ppermute | solution.py:639
  70.3 33.7 %collective-permute-start.8 = (bf16[256,1024]{1,0:T(8,128)(2,1)}, bf16[256,1024]{1,0:T(8,128)(2,1)S(1)}, u32[]{:S(2)}, u32[]{:S(2)}) collective-permute-start(bf16[256,1024]{1,0:T(8,128)(2,1)} %collective-permute-done.7.w1), channel_id=1, source_target_pairs={{0,2},{2,0},{1,3},{3,1},{4,6},{6,4},{5,7},{7,5},{8,10},{10,8},{9,1... | collective-permute-start | bytes 1572872 | tf_op jit(solution)/shard_map/ppermute | solution.py:627
  70.3 21.0 %collective-permute-start.4 = (bf16[256,1024]{1,0:T(8,128)(2,1)}, bf16[256,1024]{1,0:T(8,128)(2,1)S(1)}, u32[]{:S(2)}, u32[]{:S(2)}) collective-permute-start(bf16[256,1024]{1,0:T(8,128)(2,1)} %collective-permute-done.3.q1), channel_id=1, source_target_pairs={{0,2},{2,0},{1,3},{3,1},{4,6},{6,4},{5,7},{7,5},{8,10},{10,8},{9,1... | collective-permute-start | bytes 1572872 | tf_op jit(solution)/shard_map/ppermute | solution.py:627
  83.9 24.9 %collective-permute-start.10 = (bf16[768,1024]{1,0:T(8,128)(2,1)}, bf16[768,1024]{1,0:T(8,128)(2,1)S(1)}, u32[]{:S(2)}, u32[]{:S(2)}) collective-permute-start(bf16[768,1024]{1,0:T(8,128)(2,1)} %collective-permute-done.9.w1), channel_id=1, source_target_pairs={{0,2},{2,0},{1,3},{3,1},{4,6},{6,4},{5,7},{7,5},{8,10},{10,8},{9,1... | collective-permute-start | bytes 4718600 | tf_op jit(solution)/shard_map/ppermute | solution.py:627
  151.0 20.0 %collective-permute-start.17 = (bf16[192,4096]{1,0:T(8,128)(2,1)}, bf16[192,4096]{1,0:T(8,128)(2,1)}, u32[]{:S(2)}, u32[]{:S(2)}) collective-permute-start(bf16[192,4096]{1,0:T(8,128)(2,1)} %get-tuple-element.139.refs_10_), channel_id=1, source_target_pairs={{0,2},{2,0},{1,3},{3,1},{4,6},{6,4},{5,7},{7,5},{8,10},{10,8},{9,1... | collective-permute-start | bytes 4718600 | tf_op jit(solution)/shard_map/ppermute | solution.py:627
  151.5 19.4 %collective-permute-start.14 = (bf16[192,4096]{1,0:T(8,128)(2,1)}, bf16[192,4096]{1,0:T(8,128)(2,1)}, u32[]{:S(2)}, u32[]{:S(2)}) collective-permute-start(bf16[192,4096]{1,0:T(8,128)(2,1)} %get-tuple-element.132.refs_0_.refs_1_), channel_id=1, source_target_pairs={{0,2},{2,0},{1,3},{3,1},{4,6},{6,4},{5,7},{7,5},{8,10},{10,8},{9,1... | collective-permute-start | bytes 4718600 | tf_op jit(solution)/shard_map/ppermute | solution.py:627
  152.1 18.9 %collective-permute-start.15 = (bf16[192,1024]{1,0:T(8,128)(2,1)S(1)}, bf16[192,1024]{1,0:T(8,128)(2,1)}, u32[]{:S(2)}, u32[]{:S(2)}) collective-permute-start(bf16[192,1024]{1,0:T(8,128)(2,1)S(1)} %bitcast.252), channel_id=1, source_target_pairs={{0,2},{2,0},{1,3},{3,1},{4,6},{6,4},{5,7},{7,5},{8,10},{10,8},{9,1... | collective-permute-start | bytes 1179656 | tf_op jit(solution)/shard_map/ppermute | solution.py:627
  152.2 18.8 %collective-permute-start.16 = (bf16[192,1024]{1,0:T(8,128)(2,1)S(1)}, bf16[192,1024]{1,0:T(8,128)(2,1)}, u32[]{:S(2)}, u32[]{:S(2)}) collective-permute-start(bf16[192,1024]{1,0:T(8,128)(2,1)S(1)} %copy-done.7), channel_id=1, source_target_pairs={{0,2},{2,0},{1,3},{3,1},{4,6},{6,4},{5,7},{7,5},{8,10},{10,8},{9,1... | collective-permute-start | bytes 1179656 | tf_op jit(solution)/shard_map/ppermute | solution.py:627
  185.0 59.7 %collective-permute-start.19 = (bf16[2,2,512,512]{3,2,1,0:T(8,128)(2,1)}, bf16[2,2,512,512]{3,2,1,0:T(8,128)(2,1)}, u32[]{:S(2)}, u32[]{:S(2)}) collective-permute-start(bf16[2,2,512,512]{3,2,1,0:T(8,128)(2,1)} %get-tuple-element.140), channel_id=1, source_target_pairs={{0,16},{2,50},{16,0},{18,34},{32,48},{34,18},{48,32},{50,2},{1,17}... | collective-permute-start | bytes 6291464 | tf_op jit(solution)/shard_map/ppermute | solution.py:639
  187.5 40.8 %collective-permute-start.18 = (bf16[2,2,384,512]{3,2,1,0:T(8,128)(2,1)}, bf16[2,2,384,512]{3,2,1,0:T(8,128)(2,1)}, u32[]{:S(2)}, u32[]{:S(2)}) collective-permute-start(bf16[2,2,384,512]{3,2,1,0:T(8,128)(2,1)} %get-tuple-element.134), channel_id=1, source_target_pairs={{0,16},{2,50},{16,0},{18,34},{32,48},{34,18},{48,32},{50,2},{1,17}... | collective-permute-start | bytes 4718600 | tf_op jit(solution)/shard_map/ppermute | solution.py:639
  187.7 62.3 %collective-permute-start.20 = (bf16[2,2,128,2048]{3,2,1,0:T(8,128)(2,1)}, bf16[2,2,128,2048]{3,2,1,0:T(8,128)(2,1)}, u32[]{:S(2)}, u32[]{:S(2)}) collective-permute-start(bf16[2,2,128,2048]{3,2,1,0:T(8,128)(2,1)} %get-tuple-element.152), channel_id=1, source_target_pairs={{0,4},{2,14},{4,0},{6,10},{8,12},{10,6},{12,8},{14,2},{1,5},{3,15}... | collective-permute-start | bytes 6291464 | tf_op jit(solution)/shard_map/ppermute | solution.py:639
  191.5 62.2 %collective-permute-start.22 = (bf16[576,1024]{1,0:T(8,128)(2,1)S(1)}, bf16[576,1024]{1,0:T(8,128)(2,1)S(1)}, u32[]{:S(2)}, u32[]{:S(2)}) collective-permute-start(bf16[576,1024]{1,0:T(8,128)(2,1)S(1)} %copy-done.1), channel_id=1, source_target_pairs={{0,2},{2,0},{1,3},{3,1},{4,6},{6,4},{5,7},{7,5},{8,10},{10,8},{9,1... | collective-permute-start | bytes 3538952 | tf_op jit(solution)/shard_map/ppermute | solution.py:627
  191.5 64.3 %collective-permute-start.24 = (bf16[192,1024]{1,0:T(8,128)(2,1)S(1)}, bf16[192,1024]{1,0:T(8,128)(2,1)S(1)}, u32[]{:S(2)}, u32[]{:S(2)}) collective-permute-start(bf16[192,1024]{1,0:T(8,128)(2,1)S(1)} %copy-done.10), channel_id=1, source_target_pairs={{0,2},{2,0},{1,3},{3,1},{4,6},{6,4},{5,7},{7,5},{8,10},{10,8},{9,1... | collective-permute-start | bytes 1179656 | tf_op jit(solution)/shard_map/ppermute | solution.py:627
  229.7 23.8 %collective-permute-start.21 = (bf16[2,384,512]{2,1,0:T(8,128)(2,1)S(1)}, bf16[2,384,512]{2,1,0:T(8,128)(2,1)}, u32[]{:S(2)}, u32[]{:S(2)}) collective-permute-start(bf16[2,384,512]{2,1,0:T(8,128)(2,1)S(1)} %fusion.19), channel_id=1, source_target_pairs={{0,48},{2,18},{16,32},{18,2},{32,16},{34,50},{48,0},{50,34},{1,49}... | collective-permute-start | bytes 2359304 | tf_op jit(solution)/shard_map/ppermute | solution.py:639
  244.7 19.0 %collective-permute-start.27 = (bf16[576,1024]{1,0:T(8,128)(2,1)}, bf16[576,1024]{1,0:T(8,128)(2,1)}, u32[]{:S(2)}, u32[]{:S(2)}) collective-permute-start(bf16[576,1024]{1,0:T(8,128)(2,1)} %get-tuple-element.157.refs_22_), channel_id=1, source_target_pairs={{0,2},{2,0},{1,3},{3,1},{4,6},{6,4},{5,7},{7,5},{8,10},{10,8},{9,1... | collective-permute-start | bytes 3538952 | tf_op jit(solution)/shard_map/ppermute | solution.py:627
  253.7 33.8 %collective-permute-start.30 = (bf16[2,512,512]{2,1,0:T(8,128)(2,1)}, bf16[2,512,512]{2,1,0:T(8,128)(2,1)}, u32[]{:S(2)}, u32[]{:S(2)}) collective-permute-start(bf16[2,512,512]{2,1,0:T(8,128)(2,1)} %fusion.17), channel_id=1, source_target_pairs={{0,48},{2,18},{16,32},{18,2},{32,16},{34,50},{48,0},{50,34},{1,49}... | collective-permute-start | bytes 3145736 | tf_op jit(solution)/shard_map/ppermute | solution.py:639
  258.3 27.0 %collective-permute-start.29 = (bf16[2,2,96,512]{3,2,1,0:T(8,128)(2,1)}, bf16[2,2,96,512]{3,2,1,0:T(8,128)(2,1)S(1)}, u32[]{:S(2)}, u32[]{:S(2)}) collective-permute-start(bf16[2,2,96,512]{3,2,1,0:T(8,128)(2,1)} %pad_maximum_fusion.5), channel_id=1, source_target_pairs={{0,4},{2,14},{4,0},{6,10},{8,12},{10,6},{12,8},{14,2},{1,5},{3,15}... | collective-permute-start | bytes 1179656 | tf_op jit(solution)/shard_map/ppermute | solution.py:639
  263.6 28.2 %collective-permute-start.31 = (bf16[2,128,2048]{2,1,0:T(8,128)(2,1)S(1)}, bf16[2,128,2048]{2,1,0:T(8,128)(2,1)}, u32[]{:S(2)}, u32[]{:S(2)}) collective-permute-start(bf16[2,128,2048]{2,1,0:T(8,128)(2,1)S(1)} %copy-done.32), channel_id=1, source_target_pairs={{0,12},{2,6},{4,8},{6,2},{8,4},{10,14},{12,0},{14,10},{1,13},{3,7}... | collective-permute-start | bytes 3145736 | tf_op jit(solution)/shard_map/ppermute | solution.py:639
  282.7 22.2 %collective-permute-start.33 = (bf16[2,2,128,1024]{3,2,1,0:T(8,128)(2,1)}, bf16[2,2,128,1024]{3,2,1,0:T(8,128)(2,1)S(1)}, u32[]{:S(2)}, u32[]{:S(2)}) collective-permute-start(bf16[2,2,128,1024]{3,2,1,0:T(8,128)(2,1)} %get-tuple-element.165), channel_id=1, source_target_pairs={{0,4},{2,14},{4,0},{6,10},{8,12},{10,6},{12,8},{14,2},{1,5},{3,15}... | collective-permute-start | bytes 3145736 | tf_op jit(solution)/shard_map/ppermute | solution.py:639
  282.9 20.7 %collective-permute-start.28 = (bf16[2,2,128,1536]{3,2,1,0:T(8,128)(2,1)}, bf16[2,2,128,1536]{3,2,1,0:T(8,128)(2,1)S(1)}, u32[]{:S(2)}, u32[]{:S(2)}) collective-permute-start(bf16[2,2,128,1536]{3,2,1,0:T(8,128)(2,1)} %get-tuple-element.159), channel_id=1, source_target_pairs={{0,16},{2,50},{16,0},{18,34},{32,48},{34,18},{48,32},{50,2},{1,17}... | collective-permute-start | bytes 4718600 | tf_op jit(solution)/shard_map/ppermute | solution.py:639
  286.1 27.0 %collective-permute-start.38 = (bf16[2,96,512]{2,1,0:T(8,128)(2,1)}, bf16[2,96,512]{2,1,0:T(8,128)(2,1)}, u32[]{:S(2)}, u32[]{:S(2)}) collective-permute-start(bf16[2,96,512]{2,1,0:T(8,128)(2,1)} %fusion.33), channel_id=1, source_target_pairs={{0,12},{2,6},{4,8},{6,2},{8,4},{10,14},{12,0},{14,10},{1,13},{3,7}... | collective-permute-start | bytes 589832 | tf_op jit(solution)/shard_map/ppermute | solution.py:639
  289.6 16.4 %collective-permute-start.34 = (bf16[2,2,128,512]{3,2,1,0:T(8,128)(2,1)S(1)}, bf16[2,2,128,512]{3,2,1,0:T(8,128)(2,1)S(1)}, u32[]{:S(2)}, u32[]{:S(2)}) collective-permute-start(bf16[2,2,128,512]{3,2,1,0:T(8,128)(2,1)S(1)} %pad_maximum_fusion.3), channel_id=1, source_target_pairs={{0,4},{2,14},{4,0},{6,10},{8,12},{10,6},{12,8},{14,2},{1,5},{3,15}... | collective-permute-start | bytes 1572872 | tf_op jit(solution)/shard_map/ppermute | solution.py:639
  311.8 15.5 %collective-permute-start.40 = (bf16[2,128,1024]{2,1,0:T(8,128)(2,1)}, bf16[2,128,1024]{2,1,0:T(8,128)(2,1)S(1)}, u32[]{:S(2)}, u32[]{:S(2)}) collective-permute-start(bf16[2,128,1024]{2,1,0:T(8,128)(2,1)} %fusion.24), channel_id=1, source_target_pairs={{0,12},{2,6},{4,8},{6,2},{8,4},{10,14},{12,0},{14,10},{1,13},{3,7}... | collective-permute-start | bytes 1572872 | tf_op jit(solution)/shard_map/ppermute | solution.py:639
  355.7 119.1 %all-gather.11.cloned.1.call-start = ((), (), s32[]{:S(2)}) async-start(), calls=%async_computation.2 | async-start | bytes 11894784 | tf_op jit(solution)/shard_map/all_gather | solution.py:886
  (75 other events, 653.3 us)
Sparse Core Ops, SparseCore 0:
  20.0 56.9 all-gather.6
  355.8 56.5 all-gather.8
  415.2 59.5 all-gather.10
